TPU v7x, 512 devices: a whole 4x4x16 slice. The times are simulated.
512 devices in a mesh: section: 32 (over y_hi, z), dp: 16 (over y_lo, x, core).
Axes of the slice: x: 4, y: 4 (y_hi: 2, y_lo: 2; y = y_hi * 2 + y_lo), z: 16, core: 2. Of those that a mesh axis runs over, the one named last changes fastest.
Arguments:
- section_inputs: bfloat16 [2, 32, 512, 8192], P(None, 'section', 'dp'), may hold values from -6 to 6
- out_grads: bfloat16 [2, 32, 512, 8192], P(None, 'section', 'dp'), may hold values from -6 to 6
- adapters: bfloat16 [2, 32, 2, 64, 8192], P(None, 'section', None, None, 'dp'), as said below
Outputs:
- next_inputs: bfloat16 [2, 32, 512, 8192], P(None, 'section', 'dp')
- prev_grads: bfloat16 [2, 32, 512, 8192], P(None, 'section', 'dp')
- adapter_grads: float32 [2, 32, 2, 64, 8192], P(None, 'section', None, None, 'dp')
Inputs may be any that keep to these rules, and one draw needn't show every extreme that they name: adapters[1, p] equals adapters[0, 31 - p] for every p.
All inputs are finite; a program needn't handle non-finite values.
Results may differ from a plain program's by a relative error of at most 0.02.
Values may be sent and summed in bfloat16 or wider, within the bound.
No kernel may reach another device: no remote copies, remote signals or barrier semaphores. Data moves between devices by JAX's collectives and lax.ppermute only.
A program may use at most 64 MiB of HBM per device.

v0:
```python
import jax
import jax.numpy as jnp
from jax import lax
from jax.sharding import PartitionSpec as P


def passed_along(value, axis, steps):
    count = lax.axis_size(axis)
    first, last = (max(0, -steps), min(count, count - steps))
    return lax.ppermute(value, axis, [(source, source + steps) for source in range(first, last)])


def from_partner(array, axis, apart):
    return lax.ppermute(array, axis, [(i, i ^ 1 << apart) for i in range(lax.axis_size(axis))])


def section_pass(inputs, grads, down_map, up_map):
    xf = inputs.astype(jnp.float32)
    scale = lax.rsqrt(jnp.mean(xf * xf, axis=-1, keepdims=True) + 1e-05)
    normed = (xf * scale).astype(jnp.bfloat16)
    pre = jnp.dot(normed, down_map.T, preferred_element_type=jnp.float32)
    sig = jax.nn.sigmoid(pre)
    hidden = (pre * sig).astype(jnp.bfloat16)
    output = (xf + jnp.dot(hidden, up_map, preferred_element_type=jnp.float32)).astype(jnp.bfloat16)
    dhidden = jnp.dot(grads, up_map.T, preferred_element_type=jnp.float32)
    dpre = (dhidden * (sig * (1.0 + pre * (1.0 - sig)))).astype(jnp.bfloat16)
    dnorm = jnp.dot(dpre, down_map, preferred_element_type=jnp.float32)
    inner = jnp.mean(dnorm * xf, axis=-1, keepdims=True)
    dinput = (grads.astype(jnp.float32) + scale * (dnorm - xf * inner * scale * scale)).astype(
        jnp.bfloat16
    )
    part_a = jnp.dot(dpre.T, normed, preferred_element_type=jnp.float32).astype(jnp.bfloat16)
    part_b = jnp.dot(hidden.T, grads, preferred_element_type=jnp.float32).astype(jnp.bfloat16)
    return (output, dinput, jnp.stack([part_a, part_b]))


def shards(section_inputs, out_grads, adapters):
    weights = lax.all_gather(adapters, "dp", axis=4, tiled=True)
    down_out, down_din, down_parts = section_pass(
        section_inputs[0, 0], out_grads[0, 0], weights[0, 0, 0], weights[0, 0, 1]
    )
    up_out, up_din, up_parts = section_pass(
        section_inputs[1, 0], out_grads[1, 0], weights[1, 0, 0], weights[1, 0, 1]
    )
    from_lower = passed_along((down_out, up_din), "section", 1)
    from_upper = passed_along((up_out, down_din), "section", -1)
    next_inputs = jnp.stack([from_lower[0], from_upper[0]])[:, None]
    prev_grads = jnp.stack([from_upper[1], from_lower[1]])[:, None]
    partials = jnp.stack([down_parts, up_parts]).astype(jnp.float32)
    width = adapters.shape[4]
    totals = lax.psum(partials.astype(jnp.bfloat16), "dp").astype(jnp.float32)
    shares = lax.dynamic_slice_in_dim(totals, lax.axis_index("dp") * width, width, 3)
    levels = lax.axis_size("section").bit_length() - 1
    partner = shares
    for bit in range(levels):
        partner = from_partner(partner.astype(jnp.bfloat16), "section", bit).astype(partner.dtype)
    summed = jnp.stack([shares[0] + partner[1], shares[1] + partner[0]])
    return (next_inputs, prev_grads, summed[:, None])


def solution(mesh):
    in_specs = (
        P(None, "section", "dp", None),
        P(None, "section", "dp", None),
        P(None, "section", None, None, "dp"),
    )
    out_specs = (
        P(None, "section", "dp", None),
        P(None, "section", "dp", None),
        P(None, "section", None, None, "dp"),
    )
    return jax.shard_map(shards, mesh=mesh, in_specs=in_specs, out_specs=out_specs, check_vma=False)
```

profile of v0, /device:TPU:96, one launch (start us, length us, event | category | flops | bytes accessed | tf_op | source)
XLA Modules:
  0.0 325.6 jit_solution(1987833559476527847)
XLA Ops:
  7.2 0.0 copy-start
  7.2 0.0 copy-start.1
  7.2 0.0 all-gather.2.cloned.1.call-start
  7.2 0.7 all-gather.2.cloned.1.call-update
  7.9 0.0 all-reduce.2.cloned.1.call-start
  8.0 1.5 fusion.16
  9.5 49.0 %all-gather.2.cloned.1.call-done = bf16[2,1,2,64,8192]{4,3,2,1,0:T(8,128)(2,1)} async-done(((bf16[2,1,2,64,512]{4,3,2,1,0:T(8,128)(2,1)}), bf16[2,1,2,64,8192]{4,3,2,1,0:T(8,128)(2,1)}) %all-gather.2.cloned.1.call-update) | async-done | bytes 4194320 | tf_op jit(solution)/shard_map/all_gather | solution.py:38
  58.5 2.0 fusion.39
  60.5 1.5 fusion.3
  62.0 1.6 fusion.15
  63.7 0.0 copy-done
  63.7 0.5 fusion.2
  64.2 0.5 fusion.37
  64.6 0.5 fusion.1
  65.1 0.4 fusion.14
  65.5 0.5 fusion
  66.0 0.2 maximum_bitcast_fusion.1
  66.2 0.2 maximum_bitcast_fusion
  66.4 2.3 pad_maximum_fusion
  68.8 0.0 all-reduce.2.cloned.1.call-update
  68.8 2.3 fusion.5
  71.1 2.4 collective-permute-start.1
  73.5 2.3 fusion.4
  75.8 4.6 %collective-permute-start = (bf16[32,8192]{1,0:T(8,128)(2,1)}, bf16[32,8192]{1,0:T(8,128)(2,1)}, u32[]{:S(2)}, u32[]{:S(2)}) collective-permute-start(bf16[32,8192]{1,0:T(8,128)(2,1)} %fusion.4), channel_id=1, source_target_pairs={{0,16},{16,32},{32,48},{48,64},{64,80},{80,96},{96,112},{112,128},... | collective-permute-start | bytes 1572872 | tf_op jit(solution)/shard_map/ppermute | solution.py:10
  80.5 1.5 fusion.38
  82.0 131.9 %all-reduce.2.cloned.1.call-done = bf16[2,2,64,8192]{3,2,1,0:T(8,128)(2,1)} async-done(((bf16[2,2,64,8192]{3,2,1,0:T(8,128)(2,1)}), bf16[2,2,64,8192]{3,2,1,0:T(8,128)(2,1)}) %all-reduce.2.cloned.1.call-update) | async-done | bytes 4194320 | tf_op jit(solution)/shard_map/psum | solution.py:51
  213.9 1.0 dynamic-slice_convert_fusion
  214.9 2.4 collective-permute-start.4
  217.3 1.7 fusion.17
  219.0 5.1 %collective-permute-done.4 = bf16[2,2,64,512]{3,2,1,0:T(8,128)(2,1)S(1)} collective-permute-done((bf16[2,2,64,512]{3,2,1,0:T(8,128)(2,1)S(1)}, bf16[2,2,64,512]{3,2,1,0:T(8,128)(2,1)S(1)}, u32[]{:S(2)}, u32[]{:S(2)}) %collective-permute-start.4) | collective-permute-done | bytes 262176 | tf_op jit(solution)/shard_map/ppermute | solution.py:14
  224.2 2.3 collective-permute-start.5
  226.5 12.4 %collective-permute-done.5 = bf16[2,2,64,512]{3,2,1,0:T(8,128)(2,1)S(1)} collective-permute-done((bf16[2,2,64,512]{3,2,1,0:T(8,128)(2,1)S(1)}, bf16[2,2,64,512]{3,2,1,0:T(8,128)(2,1)S(1)}, u32[]{:S(2)}, u32[]{:S(2)}) %collective-permute-start.5) | collective-permute-done | bytes 262176 | tf_op jit(solution)/shard_map/ppermute | solution.py:14
  238.9 7.6 %collective-permute-start.6 = (bf16[2,2,64,512]{3,2,1,0:T(8,128)(2,1)S(1)}, bf16[2,2,64,512]{3,2,1,0:T(8,128)(2,1)S(1)}, u32[]{:S(2)}, u32[]{:S(2)}) collective-permute-start(bf16[2,2,64,512]{3,2,1,0:T(8,128)(2,1)S(1)} %collective-permute-done.5), channel_id=1, source_target_pairs={{0,64},{16,80},{32,96},{48,112},{64,0},{80,16},{96,32},{112,48},{1... | collective-permute-start | bytes 786440 | tf_op jit(solution)/shard_map/ppermute | solution.py:14
  246.5 0.7 fusion.23
  247.2 1.9 collective-permute-start.3
  249.1 3.9 %collective-permute-start.2 = (bf16[32,8192]{1,0:T(8,128)(2,1)S(1)}, bf16[32,8192]{1,0:T(8,128)(2,1)S(1)}, u32[]{:S(2)}, u32[]{:S(2)}) collective-permute-start(bf16[32,8192]{1,0:T(8,128)(2,1)S(1)} %get-tuple-element.12), channel_id=1, source_target_pairs={{16,0},{32,16},{48,32},{64,48},{80,64},{96,80},{112,96},{128,112},... | collective-permute-start | bytes 1572872 | tf_op jit(solution)/shard_map/ppermute | solution.py:10
  253.0 12.1 %collective-permute-done.6 = bf16[2,2,64,512]{3,2,1,0:T(8,128)(2,1)S(1)} collective-permute-done((bf16[2,2,64,512]{3,2,1,0:T(8,128)(2,1)S(1)}, bf16[2,2,64,512]{3,2,1,0:T(8,128)(2,1)S(1)}, u32[]{:S(2)}, u32[]{:S(2)}) %collective-permute-start.6) | collective-permute-done | bytes 262176 | tf_op jit(solution)/shard_map/ppermute | solution.py:14
  265.2 7.6 %collective-permute-start.7 = (bf16[2,2,64,512]{3,2,1,0:T(8,128)(2,1)S(1)}, bf16[2,2,64,512]{3,2,1,0:T(8,128)(2,1)S(1)}, u32[]{:S(2)}, u32[]{:S(2)}) collective-permute-start(bf16[2,2,64,512]{3,2,1,0:T(8,128)(2,1)S(1)} %collective-permute-done.6), channel_id=1, source_target_pairs={{0,128},{16,144},{32,160},{48,176},{64,192},{80,208},{96,224},{112... | collective-permute-start | bytes 786440 | tf_op jit(solution)/shard_map/ppermute | solution.py:14
  272.8 0.0 collective-permute-done.1
  272.8 0.0 collective-permute-done
  272.8 2.3 maximum_bitcast_fusion.2
  275.1 31.8 %collective-permute-done.7 = bf16[2,2,64,512]{3,2,1,0:T(8,128)(2,1)S(1)} collective-permute-done((bf16[2,2,64,512]{3,2,1,0:T(8,128)(2,1)S(1)}, bf16[2,2,64,512]{3,2,1,0:T(8,128)(2,1)S(1)}, u32[]{:S(2)}, u32[]{:S(2)}) %collective-permute-start.7) | collective-permute-done | bytes 262176 | tf_op jit(solution)/shard_map/ppermute | solution.py:14
  306.9 4.6 %collective-permute-start.8 = (bf16[2,2,64,512]{3,2,1,0:T(8,128)(2,1)S(1)}, bf16[2,2,64,512]{3,2,1,0:T(8,128)(2,1)S(1)}, u32[]{:S(2)}, u32[]{:S(2)}) collective-permute-start(bf16[2,2,64,512]{3,2,1,0:T(8,128)(2,1)S(1)} %collective-permute-done.7), channel_id=1, source_target_pairs={{0,256},{16,272},{32,288},{48,304},{64,320},{80,336},{96,352},{112... | collective-permute-start | bytes 786440 | tf_op jit(solution)/shard_map/ppermute | solution.py:14
  311.5 0.0 collective-permute-done.2
  311.5 1.1 maximum_bitcast_fusion.3
  312.6 5.2 %collective-permute-done.8 = bf16[2,2,64,512]{3,2,1,0:T(8,128)(2,1)S(1)} collective-permute-done((bf16[2,2,64,512]{3,2,1,0:T(8,128)(2,1)S(1)}, bf16[2,2,64,512]{3,2,1,0:T(8,128)(2,1)S(1)}, u32[]{:S(2)}, u32[]{:S(2)}) %collective-permute-start.8) | collective-permute-done | bytes 262176 | tf_op jit(solution)/shard_map/ppermute | solution.py:14
  317.9 0.1 slice_add_fusion.1
  318.0 0.8 maximum_bitcast_fusion.4
  (8 shorter events, 0.1 us)
Async XLA Ops:
  7.2 56.5 %copy-start = (bf16[2,1,32,8192]{3,2,1,0:T(8,128)(2,1)S(1)}, bf16[2,1,32,8192]{3,2,1,0:T(8,128)(2,1)}, u32[]{:S(2)}) copy-start(bf16[2,1,32,8192]{3,2,1,0:T(8,128)(2,1)} %param.3) | copy-start | bytes 3145732
  7.2 54.9 %copy-start.1 = (bf16[2,1,32,8192]{3,2,1,0:T(8,128)(2,1)S(1)}, bf16[2,1,32,8192]{3,2,1,0:T(8,128)(2,1)}, u32[]{:S(2)}) copy-start(bf16[2,1,32,8192]{3,2,1,0:T(8,128)(2,1)} %param.4) | copy-start | bytes 3145732
  7.2 51.3 %all-gather.2.cloned.1.call-start = ((), (), s32[]{:S(2)}) async-start(), calls=%async_computation | async-start | bytes 4456448 | tf_op jit(solution)/shard_map/all_gather | solution.py:38
  7.9 206.0 %all-reduce.2.cloned.1.call-start = ((), (), s32[]{:S(2)}) async-start(), calls=%async_computation.1 | async-start | bytes 8388608 | tf_op jit(solution)/shard_map/psum | solution.py:51
  58.5 5.7 %copy-start.2 = (bf16[2,1,2,64,8192]{4,3,2,1,0:T(8,128)(2,1)S(1)}, bf16[2,1,2,64,8192]{4,3,2,1,0:T(8,128)(2,1)}, u32[]{:S(2)}) copy-start(bf16[2,1,2,64,8192]{4,3,2,1,0:T(8,128)(2,1)} %all-gather.2.cloned.1.call-done) | copy-start | bytes 12582916
  71.1 201.7 %collective-permute-start.1 = (bf16[32,8192]{1,0:T(8,128)(2,1)}, bf16[32,8192]{1,0:T(8,128)(2,1)}, u32[]{:S(2)}, u32[]{:S(2)}) collective-permute-start(bf16[32,8192]{1,0:T(8,128)(2,1)} %fusion.5), channel_id=1, source_target_pairs={{16,0},{32,16},{48,32},{64,48},{80,64},{96,80},{112,96},{128,112},... | collective-permute-start | bytes 1572872 | tf_op jit(solution)/shard_map/ppermute | solution.py:10
  75.8 196.9 %collective-permute-start = (bf16[32,8192]{1,0:T(8,128)(2,1)}, bf16[32,8192]{1,0:T(8,128)(2,1)}, u32[]{:S(2)}, u32[]{:S(2)}) collective-permute-start(bf16[32,8192]{1,0:T(8,128)(2,1)} %fusion.4), channel_id=1, source_target_pairs={{0,16},{16,32},{32,48},{48,64},{64,80},{80,96},{96,112},{112,128},... | collective-permute-start | bytes 1572872 | tf_op jit(solution)/shard_map/ppermute | solution.py:10
  214.9 9.2 %collective-permute-start.4 = (bf16[2,2,64,512]{3,2,1,0:T(8,128)(2,1)S(1)}, bf16[2,2,64,512]{3,2,1,0:T(8,128)(2,1)S(1)}, u32[]{:S(2)}, u32[]{:S(2)}) collective-permute-start(bf16[2,2,64,512]{3,2,1,0:T(8,128)(2,1)S(1)} %get-tuple-element.11), channel_id=1, source_target_pairs={{0,16},{16,0},{32,48},{48,32},{64,80},{80,64},{96,112},{112,96},{1... | collective-permute-start | bytes 786440 | tf_op jit(solution)/shard_map/ppermute | solution.py:14
  224.2 14.7 %collective-permute-start.5 = (bf16[2,2,64,512]{3,2,1,0:T(8,128)(2,1)S(1)}, bf16[2,2,64,512]{3,2,1,0:T(8,128)(2,1)S(1)}, u32[]{:S(2)}, u32[]{:S(2)}) collective-permute-start(bf16[2,2,64,512]{3,2,1,0:T(8,128)(2,1)S(1)} %collective-permute-done.4), channel_id=1, source_target_pairs={{0,32},{16,48},{32,0},{48,16},{64,96},{80,112},{96,64},{112,80},{1... | collective-permute-start | bytes 786440 | tf_op jit(solution)/shard_map/ppermute | solution.py:14
  238.9 26.3 %collective-permute-start.6 = (bf16[2,2,64,512]{3,2,1,0:T(8,128)(2,1)S(1)}, bf16[2,2,64,512]{3,2,1,0:T(8,128)(2,1)S(1)}, u32[]{:S(2)}, u32[]{:S(2)}) collective-permute-start(bf16[2,2,64,512]{3,2,1,0:T(8,128)(2,1)S(1)} %collective-permute-done.5), channel_id=1, source_target_pairs={{0,64},{16,80},{32,96},{48,112},{64,0},{80,16},{96,32},{112,48},{1... | collective-permute-start | bytes 786440 | tf_op jit(solution)/shard_map/ppermute | solution.py:14
  247.2 64.3 %collective-permute-start.3 = (bf16[32,8192]{1,0:T(8,128)(2,1)S(1)}, bf16[32,8192]{1,0:T(8,128)(2,1)S(1)}, u32[]{:S(2)}, u32[]{:S(2)}) collective-permute-start(bf16[32,8192]{1,0:T(8,128)(2,1)S(1)} %get-tuple-element.13), channel_id=1, source_target_pairs={{0,16},{16,32},{32,48},{48,64},{64,80},{80,96},{96,112},{112,128},... | collective-permute-start | bytes 1572872 | tf_op jit(solution)/shard_map/ppermute | solution.py:10
  249.1 62.4 %collective-permute-start.2 = (bf16[32,8192]{1,0:T(8,128)(2,1)S(1)}, bf16[32,8192]{1,0:T(8,128)(2,1)S(1)}, u32[]{:S(2)}, u32[]{:S(2)}) collective-permute-start(bf16[32,8192]{1,0:T(8,128)(2,1)S(1)} %get-tuple-element.12), channel_id=1, source_target_pairs={{16,0},{32,16},{48,32},{64,48},{80,64},{96,80},{112,96},{128,112},... | collective-permute-start | bytes 1572872 | tf_op jit(solution)/shard_map/ppermute | solution.py:10
  265.2 41.7 %collective-permute-start.7 = (bf16[2,2,64,512]{3,2,1,0:T(8,128)(2,1)S(1)}, bf16[2,2,64,512]{3,2,1,0:T(8,128)(2,1)S(1)}, u32[]{:S(2)}, u32[]{:S(2)}) collective-permute-start(bf16[2,2,64,512]{3,2,1,0:T(8,128)(2,1)S(1)} %collective-permute-done.6), channel_id=1, source_target_pairs={{0,128},{16,144},{32,160},{48,176},{64,192},{80,208},{96,224},{112... | collective-permute-start | bytes 786440 | tf_op jit(solution)/shard_map/ppermute | solution.py:14
  306.9 10.9 %collective-permute-start.8 = (bf16[2,2,64,512]{3,2,1,0:T(8,128)(2,1)S(1)}, bf16[2,2,64,512]{3,2,1,0:T(8,128)(2,1)S(1)}, u32[]{:S(2)}, u32[]{:S(2)}) collective-permute-start(bf16[2,2,64,512]{3,2,1,0:T(8,128)(2,1)S(1)} %collective-permute-done.7), channel_id=1, source_target_pairs={{0,256},{16,272},{32,288},{48,304},{64,320},{80,336},{96,352},{112... | collective-permute-start | bytes 786440 | tf_op jit(solution)/shard_map/ppermute | solution.py:14
Sparse Core Ops, SparseCore 0:
  10.1 48.3 all-gather.1
  68.9 144.9 all-reduce.1
where the time goes:
time: 326 us
  waiting for transfers between devices  248 us (76%)
  starting transfers between devices  37.5 us (12%)
  matrix products  15.3 us (5%)
  between operations  14.3 us (4%)
  other arithmetic  10.2 us (3%)
    psum x1, waiting for transfers between devices, shards(): totals = lax.psum(partials.astype(jnp.bfloat16), 'dp').astype(jnp.float32)  132 us
    ppermute x5, waiting for transfers between devices, from_partner(): lax.ppermute(array, axis, [(i, i ^ 1 << apart) for i in range(lax.axis_si...  66.7 us
    all_gather x1, waiting for transfers between devices, shards(): weights = lax.all_gather(adapters, 'dp', axis=4, tiled=True)  49 us
    ppermute x5, starting transfers between devices, from_partner(): lax.ppermute(array, axis, [(i, i ^ 1 << apart) for i in range(lax.axis_si...  24.5 us
    ppermute x4, starting transfers between devices, passed_along(): lax.ppermute(value, axis, [(source, source + steps) for source in range(f...  12.9 us
  transfers between devices with their start and end apart: 11, of which 7 were waited for; matrix products, arithmetic and copies ran while one was open for 4% of the time, Pallas kernels for 0%

commit v1 on v0

--- a/solution.py
+++ b/solution.py
@@ -8,10 +8,6 @@
     count = lax.axis_size(axis)
     first, last = (max(0, -steps), min(count, count - steps))
     return lax.ppermute(value, axis, [(source, source + steps) for source in range(first, last)])
-
-
-def from_partner(array, axis, apart):
-    return lax.ppermute(array, axis, [(i, i ^ 1 << apart) for i in range(lax.axis_size(axis))])
 
 
 def section_pass(inputs, grads, down_map, up_map):
@@ -46,14 +42,12 @@
     from_upper = passed_along((up_out, down_din), "section", -1)
     next_inputs = jnp.stack([from_lower[0], from_upper[0]])[:, None]
     prev_grads = jnp.stack([from_upper[1], from_lower[1]])[:, None]
-    partials = jnp.stack([down_parts, up_parts]).astype(jnp.float32)
-    width = adapters.shape[4]
-    totals = lax.psum(partials.astype(jnp.bfloat16), "dp").astype(jnp.float32)
-    shares = lax.dynamic_slice_in_dim(totals, lax.axis_index("dp") * width, width, 3)
-    levels = lax.axis_size("section").bit_length() - 1
-    partner = shares
-    for bit in range(levels):
-        partner = from_partner(partner.astype(jnp.bfloat16), "section", bit).astype(partner.dtype)
+    partials = jnp.stack([down_parts, up_parts])
+    shares = lax.psum_scatter(partials, "dp", scatter_dimension=3, tiled=True)
+    count = lax.axis_size("section")
+    partner = lax.ppermute(shares, "section", [(i, count - 1 - i) for i in range(count)])
+    shares = shares.astype(jnp.float32)
+    partner = partner.astype(jnp.float32)
     summed = jnp.stack([shares[0] + partner[1], shares[1] + partner[0]])
     return (next_inputs, prev_grads, summed[:, None])
 

time: 326 us -> 183 us (0.56)
  the two profiles are of different devices: /device:TPU:96 before, /device:TPU:1 now
where the time goes in v1:
time: 183 us
  waiting for transfers between devices  133 us (73%)
  starting transfers between devices  15.2 us (8%)
  between operations  14.2 us (8%)
  matrix products  11.5 us (6%)
  other arithmetic  9.01 us (5%)
    reduce_scatter x1, waiting for transfers between devices, shards(): shares = lax.psum_scatter(partials, 'dp', scatter_dimension=3, tiled=True)  59 us
    all_gather x1, waiting for transfers between devices, shards(): weights = lax.all_gather(adapters, 'dp', axis=4, tiled=True)  51.3 us
    ppermute x1, waiting for transfers between devices, shards(): lax.ppermute(shares, 'section', [(i, count - 1 - i) for i in range(count)])  17.9 us
    ppermute x4, starting transfers between devices, passed_along(): lax.ppermute(value, axis, [(source, source + steps) for source in range(f...  10.6 us
    ppermute x1, starting transfers between devices, shards(): lax.ppermute(shares, 'section', [(i, count - 1 - i) for i in range(count)])  4.48 us
    ppermute x4, waiting for transfers between devices, passed_along(): lax.ppermute(value, axis, [(source, source + steps) for source in range(f...  3.82 us
    dot_general x2, matrix products, section_pass(): pre = jnp.dot(normed, down_map.T, preferred_element_type=jnp.float32)  3.66 us
  transfers between devices with their start and end apart: 7, of which 5 were waited for; matrix products, arithmetic and copies ran while one was open for 5% of the time, Pallas kernels for 0%

profile of v1, /device:TPU:1, one launch (start us, length us, event | category | flops | bytes accessed | tf_op | source)
XLA Modules:
  0.0 182.7 jit_solution(4097314955801286018)
XLA Ops:
  7.2 0.0 copy-start
  7.2 0.0 copy-start.1
  7.2 0.0 all-gather.2.cloned.1.call-start
  7.2 0.7 all-gather.2.cloned.1.call-update
  7.9 0.0 reduce-scatter.2.cloned.1.call-start
  8.0 1.5 fusion.16
  9.5 51.3 %all-gather.2.cloned.1.call-done = bf16[2,1,2,64,8192]{4,3,2,1,0:T(8,128)(2,1)} async-done(((bf16[2,1,2,64,512]{4,3,2,1,0:T(8,128)(2,1)}), bf16[2,1,2,64,8192]{4,3,2,1,0:T(8,128)(2,1)}) %all-gather.2.cloned.1.call-update) | async-done | bytes 4194320 | tf_op jit(solution)/shard_map/all_gather | solution.py:34
  60.8 0.0 copy-start.2
  60.8 2.0 %fusion.39 = f32[32,64]{1,0:T(8,128)S(1)} fusion(bf16[2,1,2,64,8192]{4,3,2,1,0:T(8,128)(2,1)} %all-gather.2.cloned.1.call-done, f32[32]{0:T(128)S(1)} %get-tuple-element.15, bf16[2,1,32,8192]{3,2,1,0:T(8,128)(2,1)} %param.3), kind=kOutput, calls=%fused_computation.60 | convolution fusion | flops 34340864 | bytes 1581184 | tf_op jit(solution)/shard_map/dot_general | solution.py:17
  62.8 1.5 fusion.3
  64.4 0.0 copy-done
  64.4 1.7 fusion.37
  66.0 0.0 copy-done.1
  66.1 0.5 fusion.1
  66.5 0.0 copy-done.2
  66.5 0.4 fusion.15
  67.0 0.5 fusion.2
  67.4 0.4 fusion.14
  67.8 0.5 fusion
  68.3 0.2 maximum_bitcast_fusion.1
  68.5 0.2 maximum_bitcast_fusion
  68.7 2.3 %pad_maximum_fusion = bf16[2,2,64,8192]{3,2,1,0:T(8,128)(2,1)} fusion(bf16[1,2,64,8192]{3,2,1,0:T(8,128)(2,1)S(1)} %maximum_bitcast_fusion.1, bf16[1,2,64,8192]{3,2,1,0:T(8,128)(2,1)S(1)} %maximum_bitcast_fusion), kind=kLoop, calls=%fused_computation.12 | loop fusion | flops 2097152 | bytes 8388608 | tf_op jit(solution)/shard_map/stack | solution.py:45
  71.1 0.0 reduce-scatter.2.cloned.1.call-update
  71.1 0.0 copy-start.3
  71.1 1.7 fusion.5
  72.8 1.3 collective-permute-start.1
  74.1 1.5 fusion.4
  75.6 4.0 %collective-permute-start = (bf16[32,8192]{1,0:T(8,128)(2,1)S(1)}, bf16[32,8192]{1,0:T(8,128)(2,1)S(1)}, u32[]{:S(2)}, u32[]{:S(2)}) collective-permute-start(bf16[32,8192]{1,0:T(8,128)(2,1)S(1)} %fusion.4), channel_id=1, source_target_pairs={{0,16},{16,32},{32,48},{48,64},{64,80},{80,96},{96,112},{112,128},... | collective-permute-start | bytes 1572872 | tf_op jit(solution)/shard_map/ppermute | solution.py:10
  79.7 0.0 copy-done.3
  79.7 0.3 fusion.38
  80.0 0.6 fusion.17
  80.5 0.7 fusion.23
  81.2 1.3 collective-permute-start.2
  82.5 4.0 %collective-permute-start.3 = (bf16[32,8192]{1,0:T(8,128)(2,1)S(1)}, bf16[32,8192]{1,0:T(8,128)(2,1)S(1)}, u32[]{:S(2)}, u32[]{:S(2)}) collective-permute-start(bf16[32,8192]{1,0:T(8,128)(2,1)S(1)} %get-tuple-element.11), channel_id=1, source_target_pairs={{0,16},{16,32},{32,48},{48,64},{64,80},{80,96},{96,112},{112,128},... | collective-permute-start | bytes 1572872 | tf_op jit(solution)/shard_map/ppermute | solution.py:10
  86.5 1.4 collective-permute-done.1
  88.0 2.4 %collective-permute-done = bf16[32,8192]{1,0:T(8,128)(2,1)S(1)} collective-permute-done((bf16[32,8192]{1,0:T(8,128)(2,1)S(1)}, bf16[32,8192]{1,0:T(8,128)(2,1)S(1)}, u32[]{:S(2)}, u32[]{:S(2)}) %collective-permute-start) | collective-permute-done | bytes 524320 | tf_op jit(solution)/shard_map/ppermute | solution.py:10
  90.4 1.1 maximum_bitcast_fusion.2
  91.4 59.0 %reduce-scatter.2.cloned.1.call-done = bf16[2,2,64,512]{3,2,1,0:T(8,128)(2,1)} async-done(((bf16[2,2,64,8192]{3,2,1,0:T(8,128)(2,1)}), bf16[2,2,64,512]{3,2,1,0:T(8,128)(2,1)}) %reduce-scatter.2.cloned.1.call-update) | async-done | bytes 262160 | tf_op jit(solution)/shard_map/reduce_scatter | solution.py:46
  150.4 4.5 %collective-permute-start.4 = (bf16[2,2,64,512]{3,2,1,0:T(8,128)(2,1)}, bf16[2,2,64,512]{3,2,1,0:T(8,128)(2,1)S(1)}, u32[]{:S(2)}, u32[]{:S(2)}) collective-permute-start(bf16[2,2,64,512]{3,2,1,0:T(8,128)(2,1)} %reduce-scatter.2.cloned.1.call-done), channel_id=1, source_target_pairs={{0,496},{16,480},{32,464},{48,448},{64,432},{80,416},{96,400},{112... | collective-permute-start | bytes 786440 | tf_op jit(solution)/shard_map/ppermute | solution.py:48
  154.9 0.0 collective-permute-done.2
  154.9 0.0 collective-permute-done.3
  155.0 1.1 maximum_bitcast_fusion.3
  156.0 1.0 convert_element_type.108
  157.0 17.9 %collective-permute-done.4 = bf16[2,2,64,512]{3,2,1,0:T(8,128)(2,1)S(1)} collective-permute-done((bf16[2,2,64,512]{3,2,1,0:T(8,128)(2,1)}, bf16[2,2,64,512]{3,2,1,0:T(8,128)(2,1)S(1)}, u32[]{:S(2)}, u32[]{:S(2)}) %collective-permute-start.4) | collective-permute-done | bytes 262176 | tf_op jit(solution)/shard_map/ppermute | solution.py:48
  174.9 0.1 slice_add_fusion.1
  175.0 0.8 maximum_bitcast_fusion.4
  (4 shorter events, 0.1 us)
Async XLA Ops:
  7.2 57.2 %copy-start = (bf16[2,1,32,8192]{3,2,1,0:T(8,128)(2,1)S(1)}, bf16[2,1,32,8192]{3,2,1,0:T(8,128)(2,1)}, u32[]{:S(2)}) copy-start(bf16[2,1,32,8192]{3,2,1,0:T(8,128)(2,1)} %param.3) | copy-start | bytes 3145732
  7.2 58.9 %copy-start.1 = (bf16[2,1,32,8192]{3,2,1,0:T(8,128)(2,1)S(1)}, bf16[2,1,32,8192]{3,2,1,0:T(8,128)(2,1)}, u32[]{:S(2)}) copy-start(bf16[2,1,32,8192]{3,2,1,0:T(8,128)(2,1)} %param.4) | copy-start | bytes 3145732
  7.2 53.6 %all-gather.2.cloned.1.call-start = ((), (), s32[]{:S(2)}) async-start(), calls=%async_computation.1 | async-start | bytes 4456448 | tf_op jit(solution)/shard_map/all_gather | solution.py:34
  7.9 142.5 %reduce-scatter.2.cloned.1.call-start = ((), (), s32[]{:S(2)}) async-start(), calls=%async_computation.2 | async-start | bytes 4456448 | tf_op jit(solution)/shard_map/reduce_scatter | solution.py:46
  60.8 5.7 %copy-start.2 = (bf16[2,1,2,64,8192]{4,3,2,1,0:T(8,128)(2,1)S(1)}, bf16[2,1,2,64,8192]{4,3,2,1,0:T(8,128)(2,1)}, u32[]{:S(2)}) copy-start(bf16[2,1,2,64,8192]{4,3,2,1,0:T(8,128)(2,1)} %all-gather.2.cloned.1.call-done) | copy-start | bytes 12582916
  71.1 8.6 %copy-start.3 = (bf16[2,1,2,64,8192]{4,3,2,1,0:T(8,128)(2,1)S(1)}, bf16[2,1,2,64,8192]{4,3,2,1,0:T(8,128)(2,1)}, u32[]{:S(2)}) copy-start(bf16[2,1,2,64,8192]{4,3,2,1,0:T(8,128)(2,1)} %all-gather.2.cloned.1.call-done) | copy-start | bytes 12582916
  72.8 15.1 %collective-permute-start.1 = (bf16[32,8192]{1,0:T(8,128)(2,1)S(1)}, bf16[32,8192]{1,0:T(8,128)(2,1)S(1)}, u32[]{:S(2)}, u32[]{:S(2)}) collective-permute-start(bf16[32,8192]{1,0:T(8,128)(2,1)S(1)} %fusion.5), channel_id=1, source_target_pairs={{16,0},{32,16},{48,32},{64,48},{80,64},{96,80},{112,96},{128,112},... | collective-permute-start | bytes 1572872 | tf_op jit(solution)/shard_map/ppermute | solution.py:10
  75.6 14.7 %collective-permute-start = (bf16[32,8192]{1,0:T(8,128)(2,1)S(1)}, bf16[32,8192]{1,0:T(8,128)(2,1)S(1)}, u32[]{:S(2)}, u32[]{:S(2)}) collective-permute-start(bf16[32,8192]{1,0:T(8,128)(2,1)S(1)} %fusion.4), channel_id=1, source_target_pairs={{0,16},{16,32},{32,48},{48,64},{64,80},{80,96},{96,112},{112,128},... | collective-permute-start | bytes 1572872 | tf_op jit(solution)/shard_map/ppermute | solution.py:10
  81.2 73.7 %collective-permute-start.2 = (bf16[32,8192]{1,0:T(8,128)(2,1)S(1)}, bf16[32,8192]{1,0:T(8,128)(2,1)S(1)}, u32[]{:S(2)}, u32[]{:S(2)}) collective-permute-start(bf16[32,8192]{1,0:T(8,128)(2,1)S(1)} %get-tuple-element.10), channel_id=1, source_target_pairs={{16,0},{32,16},{48,32},{64,48},{80,64},{96,80},{112,96},{128,112},... | collective-permute-start | bytes 1572872 | tf_op jit(solution)/shard_map/ppermute | solution.py:10
  82.5 72.4 %collective-permute-start.3 = (bf16[32,8192]{1,0:T(8,128)(2,1)S(1)}, bf16[32,8192]{1,0:T(8,128)(2,1)S(1)}, u32[]{:S(2)}, u32[]{:S(2)}) collective-permute-start(bf16[32,8192]{1,0:T(8,128)(2,1)S(1)} %get-tuple-element.11), channel_id=1, source_target_pairs={{0,16},{16,32},{32,48},{48,64},{64,80},{80,96},{96,112},{112,128},... | collective-permute-start | bytes 1572872 | tf_op jit(solution)/shard_map/ppermute | solution.py:10
  150.4 24.4 %collective-permute-start.4 = (bf16[2,2,64,512]{3,2,1,0:T(8,128)(2,1)}, bf16[2,2,64,512]{3,2,1,0:T(8,128)(2,1)S(1)}, u32[]{:S(2)}, u32[]{:S(2)}) collective-permute-start(bf16[2,2,64,512]{3,2,1,0:T(8,128)(2,1)} %reduce-scatter.2.cloned.1.call-done), channel_id=1, source_target_pairs={{0,496},{16,480},{32,464},{48,448},{64,432},{80,416},{96,400},{112... | collective-permute-start | bytes 786440 | tf_op jit(solution)/shard_map/ppermute | solution.py:48
Sparse Core Ops, SparseCore 0:
  10.1 50.6 all-gather.1
  71.2 79.1 reduce-scatter.1

commit v2 on v1

v2 whole, which is shorter than its diff:
```python
import jax
import jax.numpy as jnp
from jax import lax
from jax.experimental import pallas as pl
from jax.experimental.pallas import tpu as pltpu
from jax.sharding import PartitionSpec as P


def adapter_kernel(core_ref, x_ref, g_ref, taken_ref, w_ref, up_ref, down_ref, part_ref):
    core = core_ref[0]
    is_down = core == 0
    slices, _, rank, width = w_ref.shape
    tokens, model = 2 * x_ref.shape[1], x_ref.shape[2]
    across = (((1,), (1,)), ((), ()))
    over_tokens = (((0,), (0,)), ((), ()))
    f32 = jnp.float32

    def columns(i):
        cols = pl.ds(i * width, width)
        x = jnp.concatenate([x_ref[core, :, cols], taken_ref[0, :, cols]], axis=0)
        g = jnp.concatenate([g_ref[core, :, cols], taken_ref[1, :, cols]], axis=0)
        return cols, x, g

    u = jnp.zeros((tokens, rank), f32)
    v = jnp.zeros((tokens, rank), f32)
    squares = jnp.zeros((tokens, 128), f32)
    for i in range(slices):
        _, x, g = columns(i)
        u += lax.dot_general(x, w_ref[i, 0], across, preferred_element_type=f32)
        v += lax.dot_general(g, w_ref[i, 1], across, preferred_element_type=f32)
        xf = x.astype(f32)
        for j in range(width // 128):
            piece = xf[:, j * 128:(j + 1) * 128]
            squares += piece * piece
    scale = lax.rsqrt(jnp.sum(squares, axis=1, keepdims=True) / model + 1e-05)
    pre = scale * u
    sig = jax.nn.sigmoid(pre)
    hidden = (pre * sig).astype(jnp.bfloat16)
    dpre = v * (sig * (1.0 + pre * (1.0 - sig)))
    inner = jnp.sum(dpre * u, axis=1, keepdims=True) / model
    scaled = (scale * dpre).astype(jnp.bfloat16)
    back = inner * scale * scale * scale
    for i in range(slices):
        cols, x, g = columns(i)
        xf, gf = x.astype(f32), g.astype(f32)
        part_ref[i, 0] = lax.dot_general(scaled, x, over_tokens, preferred_element_type=f32).astype(part_ref.dtype)
        part_ref[i, 1] = lax.dot_general(hidden, g, over_tokens, preferred_element_type=f32).astype(part_ref.dtype)
        y = xf + jnp.dot(hidden, w_ref[i, 1], preferred_element_type=f32)
        dx = gf + jnp.dot(scaled, w_ref[i, 0], preferred_element_type=f32) - xf * back
        up_ref[:, cols] = jnp.where(is_down, y, dx).astype(up_ref.dtype)
        down_ref[:, cols] = jnp.where(is_down, dx, y).astype(down_ref.dtype)


def adapter(core, x, g, taken, w):
    tokens, model = 2 * x.shape[1], x.shape[2]
    whole = pl.BlockSpec(memory_space=pltpu.VMEM)
    relayed = jax.ShapeDtypeStruct((tokens, model), x.dtype)
    return pl.pallas_call(
        adapter_kernel,
        out_shape=(relayed, relayed, jax.ShapeDtypeStruct(w.shape, w.dtype)),
        in_specs=[pl.BlockSpec(memory_space=pltpu.SMEM)] + [whole] * 4,
        out_specs=(whole,) * 3,
        compiler_params=pltpu.CompilerParams(vmem_limit_bytes=8 << 20),
        cost_estimate=pl.CostEstimate(flops=6 * tokens * w.size, bytes_accessed=16 << 20, transcendentals=0),
    )(jnp.full((1,), core, jnp.int32), x, g, taken, w)


def shards(section_inputs, out_grads, adapters):
    n_dp = lax.axis_size("dp")
    count = lax.axis_size("section")
    half = count // 2
    section = lax.axis_index("section")
    core = lax.axis_index("dp") % 2
    is_down = core == 0
    tokens = section_inputs.shape[2]
    swap = [(i, i ^ 1) for i in range(n_dp)]
    weights = adapters[:, 0]
    inputs, grads = section_inputs[:, 0], out_grads[:, 0]

    to_all = jnp.broadcast_to(weights[None], (n_dp // 2,) + weights.shape).reshape((n_dp,) + weights.shape[1:])
    gathered = lax.all_to_all(to_all, "dp", 0, 0, tiled=True)
    given = jnp.stack([jnp.where(is_down, inputs[1], inputs[0]), jnp.where(is_down, grads[1], grads[0])])
    taken = lax.ppermute(given, "dp", swap)
    up, down, parts = adapter(core, inputs, grads, taken, gathered)

    terms = lax.all_to_all(parts, "dp", 0, 0, tiled=True)
    sums = jnp.sum(terms.reshape((n_dp // 2, 2) + terms.shape[1:]).astype(jnp.float32), axis=0)

    up = lax.ppermute(up, "section", [(i, i + 1) for i in range(count - 1) if i != half - 1] + [(half - 1, 0)])
    down = lax.ppermute(down, "section", [(i, i - 1) for i in range(1, count) if i != half] + [(half, count - 1)])
    other = lax.ppermute(jnp.stack([up[tokens:], down[tokens:]]), "dp", swap)
    up = jnp.stack([up[:tokens], other[0]])
    down = jnp.stack([down[:tokens], other[1]])
    crossing = lax.ppermute(jnp.where(section == 0, up, down), "section", [(0, half), (count - 1, half - 1)])
    none = jnp.zeros_like(up)
    up = jnp.where(section == half, crossing, jnp.where(section == 0, none, up))
    down = jnp.where(section == half - 1, crossing, jnp.where(section == count - 1, none, down))
    next_inputs = jnp.where(is_down, jnp.stack([up[0], down[1]]), jnp.stack([up[1], down[0]]))
    prev_grads = jnp.where(is_down, jnp.stack([down[0], up[1]]), jnp.stack([down[1], up[0]]))

    partner = lax.ppermute(sums.astype(jnp.bfloat16), "section", [(i, count - 1 - i) for i in range(count)])
    summed = sums + partner[::-1].astype(jnp.float32)
    return (next_inputs[:, None], prev_grads[:, None], summed[:, None])


def solution(mesh):
    in_specs = (
        P(None, "section", "dp", None),
        P(None, "section", "dp", None),
        P(None, "section", None, None, "dp"),
    )
    out_specs = (
        P(None, "section", "dp", None),
        P(None, "section", "dp", None),
        P(None, "section", None, None, "dp"),
    )
    return jax.shard_map(shards, mesh=mesh, in_specs=in_specs, out_specs=out_specs, check_vma=False)
```

time: 183 us -> 151 us (0.83)
  waiting for transfers between devices: 133 us -> 92.5 us
  starting transfers between devices: 15.2 us -> 37.6 us
  between operations: 14.2 us -> 0.84 us
  matrix products: 11.5 us -> 0 us
  local copies, waits for them, and re-layouts: 0.02 us -> 7.52 us
  Pallas kernels: 0 us -> 3.39 us
    reduce_scatter x1 -> x0, waiting for transfers between devices: 59 us -> none  [shards(): shares = lax.psum_scatter(partials, 'dp', scatter_dimension=3, tiled=True)]
    all_gather x1 -> x0, waiting for transfers between devices: 51.3 us -> none  [shards(): weights = lax.all_gather(adapters, 'dp', axis=4, tiled=True)]
    all_to_all x0 -> x2, waiting for transfers between devices: none -> 39.7 us  [the longest x1 20.6 us: shards(): gathered = lax.all_to_all(to_all, 'dp', 0, 0, tiled=True)]
    ppermute x5 -> x6, waiting for transfers between devices: 21.7 us -> 52.8 us  [the longest x1 27.5 us: shards(): lax.ppermute(up, 'section', [(i, i + 1) for i in range(count - 1) if i !=...]
    all_to_all x0 -> x2, starting transfers between devices: none -> 15 us  [the longest x1 10.5 us: shards(): gathered = lax.all_to_all(to_all, 'dp', 0, 0, tiled=True)]
    dot_general x12 -> x0, matrix products: 11.5 us -> none  [the longest x2 3.66 us: section_pass(): pre = jnp.dot(normed, down_map.T, preferred_element_type=jnp.float32)]
    ppermute x5 -> x6, starting transfers between devices: 15.1 us -> 22.6 us  [the longest x1 8.25 us: shards(): lax.ppermute(sums.astype(jnp.bfloat16), 'section', [(i, count - 1 - i) fo...]
    select_n x0 -> x4, other arithmetic: none -> 5.71 us  [the longest x1 1.64 us: shards(): jnp.where(is_down, jnp.stack([down[0], up[1]]), jnp.stack([down[1], up[0]]))]
  transfers between devices with their start and end apart: 7 -> 8, of which waited for: 5 -> 5; matrix products, arithmetic and copies ran while one was open for 5% -> 3% of each run, Pallas kernels for 0% -> 0%
where the time goes in v2:
time: 151 us; the launch traced here: 150 us
  waiting for transfers between devices  92.5 us (61%)
  starting transfers between devices  37.6 us (25%)
  other arithmetic  8.14 us (5%)
  local copies, waits for them, and re-layouts  7.52 us (5%)
  Pallas kernels  3.39 us (2%)
    ppermute x1, waiting for transfers between devices, shards(): lax.ppermute(up, 'section', [(i, i + 1) for i in range(count - 1) if i !=...  27.5 us
    ppermute x1, waiting for transfers between devices, shards(): lax.ppermute(sums.astype(jnp.bfloat16), 'section', [(i, count - 1 - i) fo...  23 us
    all_to_all x1, waiting for transfers between devices, shards(): gathered = lax.all_to_all(to_all, 'dp', 0, 0, tiled=True)  20.6 us
    all_to_all x1, waiting for transfers between devices, shards(): terms = lax.all_to_all(parts, 'dp', 0, 0, tiled=True)  19 us
    all_to_all x1, starting transfers between devices, shards(): gathered = lax.all_to_all(to_all, 'dp', 0, 0, tiled=True)  10.5 us
    ppermute x1, starting transfers between devices, shards(): lax.ppermute(sums.astype(jnp.bfloat16), 'section', [(i, count - 1 - i) fo...  8.25 us
    ppermute x1, starting transfers between devices, shards(): lax.ppermute(jnp.where(section == 0, up, down), 'section', [(0, half), (c...  5.99 us
    all_to_all x1, starting transfers between devices, shards(): terms = lax.all_to_all(parts, 'dp', 0, 0, tiled=True)  4.49 us
  transfers between devices with their start and end apart: 8, of which 5 were waited for; matrix products, arithmetic and copies ran while one was open for 3% of the time, Pallas kernels for 0%

profile of v2, /device:TPU:1, one launch (start us, length us, event | category | flops | bytes accessed | tf_op | source)
XLA Modules:
  0.0 150.0 jit_solution(16520859589327450453)
XLA Ops:
  0.6 2.5 %broadcast_in_dim.20 = bf16[8,2,2,64,512]{4,3,2,1,0:T(8,128)(2,1)} broadcast(bf16[2,2,64,512]{3,2,1,0:T(8,128)(2,1)} %bitcast.33), dimensions={1,2,3,4} | broadcast | bytes 2359296 | tf_op jit(solution)/shard_map/broadcast_in_dim | solution.py:80
  3.1 0.0 copy-start
  3.1 10.5 %all-to-all-start = ((bf16[16,2,64,512]{3,2,1,0:T(8,128)(2,1)}), bf16[16,2,64,512]{3,2,1,0:T(8,128)(2,1)S(1)}, u32[]{:S(2)}, u32[]{:S(2)}) async-start(bf16[16,2,64,512]{3,2,1,0:T(8,128)(2,1)} %bitcast.32), calls=%async_computation | async-start | bytes 4194304 | tf_op jit(solution)/shard_map/all_to_all | solution.py:81
  13.7 0.0 copy-done
  13.7 1.3 select_bitcast_fusion
  15.0 0.1 pad_maximum_fusion
  15.1 2.1 %collective-permute-start = (bf16[2,32,8192]{2,1,0:T(8,128)(2,1)S(1)}, bf16[2,32,8192]{2,1,0:T(8,128)(2,1)S(1)}, u32[]{:S(2)}, u32[]{:S(2)}) collective-permute-start(bf16[2,32,8192]{2,1,0:T(8,128)(2,1)S(1)} %pad_maximum_fusion), channel_id=1, source_target_pairs={{0,1},{1,0},{2,3},{3,2},{4,5},{5,4},{6,7},{7,6},{8,9},{9,8},{10,11... | collective-permute-start | bytes 3145736 | tf_op jit(solution)/shard_map/ppermute | solution.py:83
  17.2 2.4 %collective-permute-done.taken_ref = bf16[2,32,8192]{2,1,0:T(8,128)(2,1)S(1)} collective-permute-done((bf16[2,32,8192]{2,1,0:T(8,128)(2,1)S(1)}, bf16[2,32,8192]{2,1,0:T(8,128)(2,1)S(1)}, u32[]{:S(2)}, u32[]{:S(2)}) %collective-permute-start) | collective-permute-done | bytes 1048608 | tf_op jit(solution)/shard_map/ppermute | solution.py:83
  19.6 1.0 copy-done.2
  20.6 20.6 %all-to-all-done.w_ref = bf16[16,2,64,512]{3,2,1,0:T(8,128)(2,1)S(1)} async-done(((bf16[16,2,64,512]{3,2,1,0:T(8,128)(2,1)}), bf16[16,2,64,512]{3,2,1,0:T(8,128)(2,1)S(1)}, u32[]{:S(2)}, u32[]{:S(2)}) %all-to-all-start) | async-done | bytes 2097184 | tf_op jit(solution)/shard_map/all_to_all | solution.py:81
  41.2 1.2 copy-done.1
  42.5 1.2 copy-done.3
  43.7 3.4 %shard_map.58 = (bf16[64,8192]{1,0:T(8,128)(2,1)S(1)}, bf16[64,8192]{1,0:T(8,128)(2,1)S(1)}, bf16[16,2,64,512]{3,2,1,0:T(8,128)(2,1)}) custom-call(s32[1]{0:T(128)} %bitcast.core_ref, bf16[2,32,8192]{2,1,0:T(8,128)(2,1)S(1)} %bitcast.29, bf16[2,32,8192]{2,1,0:T(8,128)(2,1)S(1)} %bitcast.30, bf16[2,32,8192]{2,1,0:T(8,128)(2,1)S(1)} %copy-done.3, ...), custom_call_target="tpu_custom_call" | custom-call | flops 402653184 | bytes 16777216 | tf_op jit(solution)/shard_map/pallas_call | solution.py:58
  47.1 1.9 %collective-permute-start.1 = (bf16[64,8192]{1,0:T(8,128)(2,1)S(1)}, bf16[64,8192]{1,0:T(8,128)(2,1)S(1)}, u32[]{:S(2)}, u32[]{:S(2)}) collective-permute-start(bf16[64,8192]{1,0:T(8,128)(2,1)S(1)} %get-tuple-element.6), channel_id=1, source_target_pairs={{0,16},{16,32},{32,48},{48,64},{64,80},{80,96},{96,112},{112,128},... | collective-permute-start | bytes 3145736 | tf_op jit(solution)/shard_map/ppermute | solution.py:89
  49.0 1.3 collective-permute-start.2
  50.3 27.5 %collective-permute-done.1 = bf16[64,8192]{1,0:T(8,128)(2,1)S(1)} collective-permute-done((bf16[64,8192]{1,0:T(8,128)(2,1)S(1)}, bf16[64,8192]{1,0:T(8,128)(2,1)S(1)}, u32[]{:S(2)}, u32[]{:S(2)}) %collective-permute-start.1) | collective-permute-done | bytes 1048608 | tf_op jit(solution)/shard_map/ppermute | solution.py:89
  77.7 0.1 slice_bitcast_fusion.7
  77.8 0.0 collective-permute-done.2
  77.8 0.1 slice_bitcast_fusion.4
  77.9 0.0 copy-start.4
  77.9 1.1 pad_maximum_fusion.1
  79.0 3.0 %collective-permute-start.3 = (bf16[2,32,8192]{2,1,0:T(8,128)(2,1)}, bf16[2,32,8192]{2,1,0:T(8,128)(2,1)}, u32[]{:S(2)}, u32[]{:S(2)}) collective-permute-start(bf16[2,32,8192]{2,1,0:T(8,128)(2,1)} %pad_maximum_fusion.1), channel_id=1, source_target_pairs={{0,1},{1,0},{2,3},{3,2},{4,5},{5,4},{6,7},{7,6},{8,9},{9,8},{10,11... | collective-permute-start | bytes 3145736 | tf_op jit(solution)/shard_map/ppermute | solution.py:91
  82.1 4.5 %all-to-all-start.1 = ((bf16[16,2,64,512]{3,2,1,0:T(8,128)(2,1)}), bf16[16,2,64,512]{3,2,1,0:T(8,128)(2,1)S(1)}, u32[]{:S(2)}, u32[]{:S(2)}) async-start(bf16[16,2,64,512]{3,2,1,0:T(8,128)(2,1)} %get-tuple-element.8), calls=%async_computation.1 | async-start | bytes 4194304 | tf_op jit(solution)/shard_map/all_to_all | solution.py:86
  86.6 0.0 collective-permute-done.3
  86.6 1.3 fusion
  87.9 0.0 copy-start.6
  87.9 0.0 copy-start.8
  87.9 0.0 copy-done.4
  87.9 1.3 broadcast_select_fusion
  89.2 0.0 copy-done.6
  89.2 0.0 copy-done.8
  89.2 6.0 %collective-permute-start.4 = (bf16[2,32,8192]{2,1,0:T(8,128)(2,1)}, bf16[2,32,8192]{2,1,0:T(8,128)(2,1)}, u32[]{:S(2)}, u32[]{:S(2)}) collective-permute-start(bf16[2,32,8192]{2,1,0:T(8,128)(2,1)} %broadcast_select_fusion), channel_id=1, source_target_pairs={{0,256},{496,240},{1,257},{497,241},{2,258},{498,242},{3,259},{499... | collective-permute-start | bytes 3145736 | tf_op jit(solution)/shard_map/ppermute | solution.py:94
  95.2 19.0 %all-to-all-done.1 = bf16[16,2,64,512]{3,2,1,0:T(8,128)(2,1)S(1)} async-done(((bf16[16,2,64,512]{3,2,1,0:T(8,128)(2,1)}), bf16[16,2,64,512]{3,2,1,0:T(8,128)(2,1)S(1)}, u32[]{:S(2)}, u32[]{:S(2)}) %all-to-all-start.1) | async-done | bytes 2097184 | tf_op jit(solution)/shard_map/all_to_all | solution.py:86
  114.2 0.3 convert_reduce_fusion
  114.5 0.0 copy-start.5
  114.5 0.0 copy-start.7
  114.5 0.0 copy-start.9
  114.6 8.3 %collective-permute-start.5 = (bf16[2,2,64,512]{3,2,1,0:T(8,128)(2,1)S(1)}, bf16[2,2,64,512]{3,2,1,0:T(8,128)(2,1)S(1)}, u32[]{:S(2)}, u32[]{:S(2)}) collective-permute-start(bf16[2,2,64,512]{3,2,1,0:T(8,128)(2,1)S(1)} %convert_element_type.14), channel_id=1, source_target_pairs={{0,496},{16,480},{32,464},{48,448},{64,432},{80,416},{96,400},{112... | collective-permute-start | bytes 786440 | tf_op jit(solution)/shard_map/ppermute | solution.py:101
  122.9 23.0 %collective-permute-done.5 = bf16[2,2,64,512]{3,2,1,0:T(8,128)(2,1)S(1)} collective-permute-done((bf16[2,2,64,512]{3,2,1,0:T(8,128)(2,1)S(1)}, bf16[2,2,64,512]{3,2,1,0:T(8,128)(2,1)S(1)}, u32[]{:S(2)}, u32[]{:S(2)}) %collective-permute-start.5) | collective-permute-done | bytes 262176 | tf_op jit(solution)/shard_map/ppermute | solution.py:101
  145.8 0.9 add_bitcast_fusion
  146.7 0.0 collective-permute-done.4
  146.7 0.0 copy-done.5
  146.7 0.0 copy-done.7
  146.7 0.0 copy-done.9
  146.7 1.5 select_select_fusion.1
  148.2 0.1 slice_bitcast_fusion.1
  148.3 0.1 slice_bitcast_fusion
  148.4 1.6 %maximum_select_fusion.1 = (bf16[2,1,32,8192]{3,2,1,0:T(8,128)(2,1)}, bf16[2,1,32,8192]{3,2,1,0:T(8,128)(2,1)}) fusion(bf16[1,1,32,8192]{3,2,1,0:T(8,128)(2,1)S(1)} %get-tuple-element.11, bf16[1,1,32,8192]{3,2,1,0:T(8,128)(2,1)S(1)} %get-tuple-element.13, bf16[1,1,32,8192]{3,2,1,0:T(8,128)(2,1)S(1)} %get-tuple-element.12, ...), kind=kLoop, calls=%fused_computation.6 | loop fusion | flops 3145728 | bytes 4194305 | tf_op jit(solution)/shard_map/jit(_where)/select_n | solution.py:99
  (4 shorter events, 0.0 us)
Async XLA Ops:
  3.1 10.5 %copy-start = (bf16[2,1,32,8192]{3,2,1,0:T(8,128)(2,1)S(1)}, bf16[2,1,32,8192]{3,2,1,0:T(8,128)(2,1)}, u32[]{:S(2)}) copy-start(bf16[2,1,32,8192]{3,2,1,0:T(8,128)(2,1)} %param.3) | copy-start | bytes 3145732
  3.1 38.1 %all-to-all-start = ((bf16[16,2,64,512]{3,2,1,0:T(8,128)(2,1)}), bf16[16,2,64,512]{3,2,1,0:T(8,128)(2,1)S(1)}, u32[]{:S(2)}, u32[]{:S(2)}) async-start(bf16[16,2,64,512]{3,2,1,0:T(8,128)(2,1)} %bitcast.32), calls=%async_computation | async-start | bytes 4194304 | tf_op jit(solution)/shard_map/all_to_all | solution.py:81
  15.1 4.6 %collective-permute-start = (bf16[2,32,8192]{2,1,0:T(8,128)(2,1)S(1)}, bf16[2,32,8192]{2,1,0:T(8,128)(2,1)S(1)}, u32[]{:S(2)}, u32[]{:S(2)}) collective-permute-start(bf16[2,32,8192]{2,1,0:T(8,128)(2,1)S(1)} %pad_maximum_fusion), channel_id=1, source_target_pairs={{0,1},{1,0},{2,3},{3,2},{4,5},{5,4},{6,7},{7,6},{8,9},{9,8},{10,11... | collective-permute-start | bytes 3145736 | tf_op jit(solution)/shard_map/ppermute | solution.py:83
  19.6 1.0 copy-start.2
  41.2 1.2 copy-start.1
  42.5 1.2 copy-start.3
  47.1 30.7 %collective-permute-start.1 = (bf16[64,8192]{1,0:T(8,128)(2,1)S(1)}, bf16[64,8192]{1,0:T(8,128)(2,1)S(1)}, u32[]{:S(2)}, u32[]{:S(2)}) collective-permute-start(bf16[64,8192]{1,0:T(8,128)(2,1)S(1)} %get-tuple-element.6), channel_id=1, source_target_pairs={{0,16},{16,32},{32,48},{48,64},{64,80},{80,96},{96,112},{112,128},... | collective-permute-start | bytes 3145736 | tf_op jit(solution)/shard_map/ppermute | solution.py:89
  49.0 28.8 %collective-permute-start.2 = (bf16[64,8192]{1,0:T(8,128)(2,1)S(1)}, bf16[64,8192]{1,0:T(8,128)(2,1)S(1)}, u32[]{:S(2)}, u32[]{:S(2)}) collective-permute-start(bf16[64,8192]{1,0:T(8,128)(2,1)S(1)} %get-tuple-element.7), channel_id=1, source_target_pairs={{16,0},{32,16},{48,32},{64,48},{80,64},{96,80},{112,96},{128,112},... | collective-permute-start | bytes 3145736 | tf_op jit(solution)/shard_map/ppermute | solution.py:90
  77.9 10.0 %copy-start.4 = (bf16[1,32,8192]{2,1,0:T(8,128)(2,1)}, bf16[1,32,8192]{2,1,0:T(8,128)(2,1)S(1)}, u32[]{:S(2)}) copy-start(bf16[1,32,8192]{2,1,0:T(8,128)(2,1)S(1)} %get-tuple-element.21) | copy-start | bytes 1572868
  79.0 7.5 %collective-permute-start.3 = (bf16[2,32,8192]{2,1,0:T(8,128)(2,1)}, bf16[2,32,8192]{2,1,0:T(8,128)(2,1)}, u32[]{:S(2)}, u32[]{:S(2)}) collective-permute-start(bf16[2,32,8192]{2,1,0:T(8,128)(2,1)} %pad_maximum_fusion.1), channel_id=1, source_target_pairs={{0,1},{1,0},{2,3},{3,2},{4,5},{5,4},{6,7},{7,6},{8,9},{9,8},{10,11... | collective-permute-start | bytes 3145736 | tf_op jit(solution)/shard_map/ppermute | solution.py:91
  82.1 32.1 %all-to-all-start.1 = ((bf16[16,2,64,512]{3,2,1,0:T(8,128)(2,1)}), bf16[16,2,64,512]{3,2,1,0:T(8,128)(2,1)S(1)}, u32[]{:S(2)}, u32[]{:S(2)}) async-start(bf16[16,2,64,512]{3,2,1,0:T(8,128)(2,1)} %get-tuple-element.8), calls=%async_computation.1 | async-start | bytes 4194304 | tf_op jit(solution)/shard_map/all_to_all | solution.py:86
  87.9 1.3 copy-start.6
  87.9 1.3 copy-start.8
  89.2 57.5 %collective-permute-start.4 = (bf16[2,32,8192]{2,1,0:T(8,128)(2,1)}, bf16[2,32,8192]{2,1,0:T(8,128)(2,1)}, u32[]{:S(2)}, u32[]{:S(2)}) collective-permute-start(bf16[2,32,8192]{2,1,0:T(8,128)(2,1)} %broadcast_select_fusion), channel_id=1, source_target_pairs={{0,256},{496,240},{1,257},{497,241},{2,258},{498,242},{3,259},{499... | collective-permute-start | bytes 3145736 | tf_op jit(solution)/shard_map/ppermute | solution.py:94
  114.5 32.2 %copy-start.5 = (bf16[1,32,8192]{2,1,0:T(8,128)(2,1)S(1)}, bf16[1,32,8192]{2,1,0:T(8,128)(2,1)}, u32[]{:S(2)}) copy-start(bf16[1,32,8192]{2,1,0:T(8,128)(2,1)} %copy-done.4) | copy-start | bytes 1572868
  114.5 32.2 %copy-start.7 = (bf16[1,32,8192]{2,1,0:T(8,128)(2,1)S(1)}, bf16[1,32,8192]{2,1,0:T(8,128)(2,1)}, u32[]{:S(2)}) copy-start(bf16[1,32,8192]{2,1,0:T(8,128)(2,1)} %copy-done.6) | copy-start | bytes 1572868
  114.5 32.2 %copy-start.9 = (bf16[1,32,8192]{2,1,0:T(8,128)(2,1)S(1)}, bf16[1,32,8192]{2,1,0:T(8,128)(2,1)}, u32[]{:S(2)}) copy-start(bf16[1,32,8192]{2,1,0:T(8,128)(2,1)} %copy-done.8) | copy-start | bytes 1572868
  114.6 31.3 %collective-permute-start.5 = (bf16[2,2,64,512]{3,2,1,0:T(8,128)(2,1)S(1)}, bf16[2,2,64,512]{3,2,1,0:T(8,128)(2,1)S(1)}, u32[]{:S(2)}, u32[]{:S(2)}) collective-permute-start(bf16[2,2,64,512]{3,2,1,0:T(8,128)(2,1)S(1)} %convert_element_type.14), channel_id=1, source_target_pairs={{0,496},{16,480},{32,464},{48,448},{64,432},{80,416},{96,400},{112... | collective-permute-start | bytes 786440 | tf_op jit(solution)/shard_map/ppermute | solution.py:101

commit v3 on v2

v3 whole, which is shorter than its diff:
```python
import jax
import jax.numpy as jnp
from jax import lax
from jax.experimental import pallas as pl
from jax.experimental.pallas import tpu as pltpu
from jax.sharding import PartitionSpec as P

WHOLE = pl.BlockSpec(memory_space=pltpu.VMEM)
ANYWHERE = pl.BlockSpec(memory_space=pl.ANY)
SCALARS = pl.BlockSpec(memory_space=pltpu.SMEM)
ACROSS = (((1,), (1,)), ((), ()))
OVER_TOKENS = (((0,), (0,)), ((), ()))
PARAMS = pltpu.CompilerParams(vmem_limit_bytes=12 << 20)
F32 = jnp.float32


def spread_kernel(w_ref, out_ref, sems):
    copies = [
        pltpu.make_async_copy(w_ref, out_ref.at[pl.ds(2 * i, 2)], sems.at[i]) for i in range(out_ref.shape[0] // 2)
    ]
    for copy in copies:
        copy.start()
    for copy in copies:
        copy.wait()


def spread(w, n_dp):
    return pl.pallas_call(
        spread_kernel,
        out_shape=pltpu.HBM((n_dp,) + w.shape[1:], w.dtype),
        in_specs=[WHOLE],
        out_specs=ANYWHERE,
        scratch_shapes=[pltpu.SemaphoreType.DMA((n_dp // 2,))],
        compiler_params=PARAMS,
        cost_estimate=pl.CostEstimate(flops=0, bytes_accessed=n_dp * w.size, transcendentals=0),
    )(w)


def adapter_kernel(
    core_ref, x_ref, g_ref, taken_ref, w_ref, up_ref, down_ref, send_ref, part_ref, xs, gs, ps, ms, loads, part_stores, stores
):
    core = core_ref[0]
    is_down = core == 0
    slices, _, rank, width = w_ref.shape
    tokens, model = x_ref.shape[1:]
    chunks = loads.shape[0]
    own, others = pl.ds(0, tokens), pl.ds(tokens, tokens)

    fetches = []
    for j in range(chunks):
        cols = pl.ds(j * (model // chunks), model // chunks)
        fetches.append([
            pltpu.make_async_copy(x_ref.at[core, :, cols], xs.at[own, cols], loads.at[j, 0]),
            pltpu.make_async_copy(taken_ref.at[0, :, cols], xs.at[others, cols], loads.at[j, 1]),
            pltpu.make_async_copy(g_ref.at[core, :, cols], gs.at[own, cols], loads.at[j, 2]),
            pltpu.make_async_copy(taken_ref.at[1, :, cols], gs.at[others, cols], loads.at[j, 3]),
        ])
        for copy in fetches[-1]:
            copy.start()

    u = jnp.zeros((2 * tokens, rank), F32)
    v = jnp.zeros((2 * tokens, rank), F32)
    squares = jnp.zeros((2 * tokens, 128), F32)
    for i in range(slices):
        if i % (slices // chunks) == 0:
            for copy in fetches[i // (slices // chunks)]:
                copy.wait()
        cols = pl.ds(i * width, width)
        x = xs[:, cols]
        u += lax.dot_general(x, w_ref[i, 0], ACROSS, preferred_element_type=F32)
        v += lax.dot_general(gs[:, cols], w_ref[i, 1], ACROSS, preferred_element_type=F32)
        xf = x.astype(F32)
        for j in range(width // 128):
            piece = xf[:, j * 128:(j + 1) * 128]
            squares += piece * piece
    scale = lax.rsqrt(jnp.sum(squares, axis=1, keepdims=True) / model + 1e-05)
    pre = scale * u
    sig = jax.nn.sigmoid(pre)
    hidden = (pre * sig).astype(jnp.bfloat16)
    dpre = v * (sig * (1.0 + pre * (1.0 - sig)))
    inner = jnp.sum(dpre * u, axis=1, keepdims=True) / model
    scaled = (scale * dpre).astype(jnp.bfloat16)
    back = inner * scale * scale * scale

    stored = []
    per = slices // chunks
    for i in range(slices):
        cols = pl.ds(i * width, width)
        ps[i, 0] = lax.dot_general(scaled, xs[:, cols], OVER_TOKENS, preferred_element_type=F32).astype(ps.dtype)
        ps[i, 1] = lax.dot_general(hidden, gs[:, cols], OVER_TOKENS, preferred_element_type=F32).astype(ps.dtype)
        if i % per == per - 1:
            some = pl.ds(i + 1 - per, per)
            stored.append(pltpu.make_async_copy(ps.at[some], part_ref.at[some], part_stores.at[i // per]))
            stored[-1].start()
    for i in range(slices):
        cols = pl.ds(i * width, width)
        xf, gf = xs[:, cols].astype(F32), gs[:, cols].astype(F32)
        y = (xf + jnp.dot(hidden, w_ref[i, 1], preferred_element_type=F32)).astype(ms.dtype)
        dx = (gf + jnp.dot(scaled, w_ref[i, 0], preferred_element_type=F32) - xf * back).astype(ms.dtype)
        ms[0, :, cols] = jnp.where(is_down, y, dx)
        ms[1, :, cols] = jnp.where(is_down, dx, y)
        if i % per == per - 1:
            j = i // per
            cols = pl.ds(j * (model // chunks), model // chunks)
            for copy in (
                pltpu.make_async_copy(ms.at[0, own, cols], up_ref.at[:, cols], stores.at[j, 0]),
                pltpu.make_async_copy(ms.at[1, own, cols], down_ref.at[:, cols], stores.at[j, 1]),
                pltpu.make_async_copy(ms.at[0, others, cols], send_ref.at[0, :, cols], stores.at[j, 2]),
                pltpu.make_async_copy(ms.at[1, others, cols], send_ref.at[1, :, cols], stores.at[j, 3]),
            ):
                copy.start()
                stored.append(copy)
    for copy in stored:
        copy.wait()


def adapter(core, x, g, taken, w):
    tokens, model = x.shape[1:]
    one = pltpu.HBM((tokens, model), x.dtype)
    both = pltpu.VMEM((2 * tokens, model), x.dtype)
    return pl.pallas_call(
        adapter_kernel,
        out_shape=(one, one, pltpu.HBM((2, tokens, model), x.dtype), pltpu.HBM(w.shape, w.dtype)),
        in_specs=[SCALARS] + [ANYWHERE] * 3 + [WHOLE],
        out_specs=(ANYWHERE,) * 4,
        scratch_shapes=[
            both,
            both,
            pltpu.VMEM(w.shape, w.dtype),
            pltpu.VMEM((2, 2 * tokens, model), x.dtype),
            pltpu.SemaphoreType.DMA((4, 4)),
            pltpu.SemaphoreType.DMA((4,)),
            pltpu.SemaphoreType.DMA((4, 4)),
        ],
        compiler_params=PARAMS,
        cost_estimate=pl.CostEstimate(flops=12 * tokens * w.size, bytes_accessed=12 << 20, transcendentals=0),
    )(core, *(pltpu.with_memory_space_constraint(a, pltpu.HBM) for a in (x, g, taken)), w)


def add_kernel(sums_ref, partner_ref, out_ref):
    out_ref[0] = sums_ref[0] + partner_ref[1].astype(F32)
    out_ref[1] = sums_ref[1] + partner_ref[0].astype(F32)


def add_mirrored(sums, partner):
    return pl.pallas_call(
        add_kernel,
        out_shape=jax.ShapeDtypeStruct(sums.shape, F32),
        in_specs=[WHOLE] * 2,
        out_specs=WHOLE,
        compiler_params=PARAMS,
        cost_estimate=pl.CostEstimate(flops=0, bytes_accessed=2 << 20, transcendentals=0),
    )(sums, partner)


def moved(value, pairs, n_dp, flip=()):
    turn = n_dp // 2
    routes = [(a * n_dp + d, b * n_dp + d) for a, b in pairs for d in range(n_dp)]
    routes += [(a * n_dp + d, b * n_dp + (d ^ turn)) for a, b in flip for d in range(n_dp)]
    return lax.ppermute(value, ("section", "dp"), routes)


def shards(section_inputs, out_grads, adapters):
    n_dp = lax.axis_size("dp")
    count = lax.axis_size("section")
    half = count // 2
    section = lax.axis_index("section")
    core = lax.axis_index("dp") % 2
    is_down = core == 0
    swap = [(i, i ^ 1) for i in range(n_dp)]
    which = jnp.full((1,), core, jnp.int32)
    inputs, grads = section_inputs[:, 0], out_grads[:, 0]

    gathered = lax.all_to_all(spread(adapters[:, 0], n_dp), "dp", 0, 0, tiled=True)
    given = jnp.stack([jnp.where(is_down, inputs[1], inputs[0]), jnp.where(is_down, grads[1], grads[0])])
    taken = lax.ppermute(given, "dp", swap)
    up_own, down_own, send, parts = adapter(which, inputs, grads, taken, gathered)

    terms = lax.all_to_all(parts, "dp", 0, 0, tiled=True)
    sums = jnp.sum(terms.reshape((n_dp // 2, 2) + terms.shape[1:]).astype(F32), axis=0)

    got = lax.ppermute(send, "dp", swap)
    up_own, down_own, up_got, down_got = lax.optimization_barrier((up_own, down_own, got[0], got[1]))
    ups = [(i, i + 1) for i in range(count - 1) if i != half - 1]
    downs = [(i, i - 1) for i in range(1, count) if i != half]
    up_own = moved(up_own, ups, n_dp, [(half - 1, half)])
    down_own = moved(down_own, downs, n_dp, [(half, half - 1)])
    up_got = moved(up_got, ups + [(half - 1, 0)], n_dp)
    down_got = moved(down_got, downs + [(half, count - 1)], n_dp)
    sums, up_own, down_own, up_got, down_got = lax.optimization_barrier((sums, up_own, down_own, up_got, down_got))

    partner = lax.ppermute(sums.astype(jnp.bfloat16), "section", [(i, count - 1 - i) for i in range(count)])
    crossed_own = moved(
        jnp.where(section == half, up_own, down_own), [], n_dp, [(half, half), (half - 1, half - 1)]
    )
    crossed_got = moved(jnp.where(section == 0, up_got, down_got), [(0, half), (count - 1, half - 1)], n_dp)
    none = jnp.zeros_like(up_got)
    up_own = jnp.where(section == half, crossed_own, up_own)
    down_own = jnp.where(section == half - 1, crossed_own, down_own)
    up_got = jnp.where(section == half, crossed_got, jnp.where(section == 0, none, up_got))
    down_got = jnp.where(section == half - 1, crossed_got, jnp.where(section == count - 1, none, down_got))
    next_inputs = jnp.stack([jnp.where(is_down, up_own, up_got), jnp.where(is_down, down_got, down_own)])
    prev_grads = jnp.stack([jnp.where(is_down, down_own, down_got), jnp.where(is_down, up_got, up_own)])

    summed = add_mirrored(sums, partner)
    return (next_inputs[:, None], prev_grads[:, None], summed[:, None])


def solution(mesh):
    in_specs = (
        P(None, "section", "dp", None),
        P(None, "section", "dp", None),
        P(None, "section", None, None, "dp"),
    )
    out_specs = (
        P(None, "section", "dp", None),
        P(None, "section", "dp", None),
        P(None, "section", None, None, "dp"),
    )
    return jax.shard_map(shards, mesh=mesh, in_specs=in_specs, out_specs=out_specs, check_vma=False)
```

time: 151 us -> 128 us (0.85)
  waiting for transfers between devices: 92.5 us -> 69.8 us
  local copies, waits for them, and re-layouts: 7.52 us -> 3.19 us
  Pallas kernels: 3.39 us -> 7.01 us
    ppermute x4 -> x7, waiting for transfers between devices: 27.5 us -> 5.46 us  [the longest x6 5.46 us: moved(): return lax.ppermute(value, ('section', 'dp'), routes)]
    ppermute x4 -> x7, starting transfers between devices: 12.2 us -> 16.7 us  [the longest x6 14.1 us: moved(): return lax.ppermute(value, ('section', 'dp'), routes)]
    ppermute x1, starting transfers between devices: 8.25 us -> 4.42 us  [shards(): lax.ppermute(sums.astype(jnp.bfloat16), 'section', [(i, count - 1 - i) fo...]
    pallas_call x1 -> x3, Pallas kernels: 3.39 us -> 7.01 us  [the longest x1 4.76 us: adapter(): pl.pallas_call(adapter_kernel, out_shape=(one, one, pltpu.HBM((2, tokens,...]
    broadcast_in_dim x1 -> x0, local copies, waits for them, and re-layouts: 2.52 us -> none  [shards(): jnp.broadcast_to(weights[None], (n_dp // 2,) + weights.shape)]
    unnamed x20 -> x6, local copies, waits for them, and re-layouts: 3.45 us -> 0.95 us
    squeeze x0 -> x1, local copies, waits for them, and re-layouts: none -> 2.23 us  [shards(): got[1]]
    unnamed x0 -> x2, other arithmetic: none -> 2.12 us
  transfers between devices with their start and end apart: 8 -> 11, of which waited for: 5 -> 5; matrix products, arithmetic and copies ran while one was open for 3% -> 5% of each run, Pallas kernels for 0% -> 1%
where the time goes in v3:
time: 128 us; the launch traced here: 127 us
  waiting for transfers between devices  69.8 us (55%)
  starting transfers between devices  38.4 us (30%)
  other arithmetic  8.24 us (6%)
  Pallas kernels  7.01 us (5%)
  local copies, waits for them, and re-layouts  3.19 us (2%)
    ppermute x1, waiting for transfers between devices, shards(): lax.ppermute(sums.astype(jnp.bfloat16), 'section', [(i, count - 1 - i) fo...  22.8 us
    all_to_all x1, waiting for transfers between devices, shards(): lax.all_to_all(spread(adapters[:, 0], n_dp), 'dp', 0, 0, tiled=True)  21.6 us
    all_to_all x1, waiting for transfers between devices, shards(): terms = lax.all_to_all(parts, 'dp', 0, 0, tiled=True)  17.5 us
    ppermute x6, starting transfers between devices, moved(): return lax.ppermute(value, ('section', 'dp'), routes)  14.1 us
    all_to_all x1, starting transfers between devices, shards(): lax.all_to_all(spread(adapters[:, 0], n_dp), 'dp', 0, 0, tiled=True)  10.5 us
    ppermute x6, waiting for transfers between devices, moved(): return lax.ppermute(value, ('section', 'dp'), routes)  5.46 us
    pallas_call x1, Pallas kernels, adapter(): pl.pallas_call(adapter_kernel, out_shape=(one, one, pltpu.HBM((2, tokens,...  4.76 us
    all_to_all x1, starting transfers between devices, shards(): terms = lax.all_to_all(parts, 'dp', 0, 0, tiled=True)  4.59 us
  transfers between devices with their start and end apart: 11, of which 5 were waited for; matrix products, arithmetic and copies ran while one was open for 5% of the time, Pallas kernels for 1%

profile of v3, /device:TPU:1, one launch (start us, length us, event | category | flops | bytes accessed | tf_op | source)
XLA Modules:
  0.0 127.4 jit_solution(10212548335938231271)
XLA Ops:
  0.6 0.0 copy-start
  0.6 0.9 copy-done
  1.6 1.4 %shard_map.58 = bf16[16,2,64,512]{3,2,1,0:T(8,128)(2,1)} custom-call(bf16[2,2,64,512]{3,2,1,0:T(8,128)(2,1)S(1)} %bitcast.33), custom_call_target="tpu_custom_call" | custom-call | bytes 2097152 | tf_op jit(solution)/shard_map/pallas_call | solution.py:28
  3.0 0.0 copy-start.1
  3.0 10.5 %all-to-all-start = ((bf16[16,2,64,512]{3,2,1,0:T(8,128)(2,1)}), bf16[16,2,64,512]{3,2,1,0:T(8,128)(2,1)S(1)}, u32[]{:S(2)}, u32[]{:S(2)}) async-start(bf16[16,2,64,512]{3,2,1,0:T(8,128)(2,1)} %shard_map.58), calls=%async_computation | async-start | bytes 4194304 | tf_op jit(solution)/shard_map/all_to_all | solution.py:174
  13.5 0.0 copy-done.1
  13.5 1.3 %select_bitcast_fusion.4 = (bf16[1,32,8192]{2,1,0:T(8,128)(2,1)S(1)}, bf16[1,32,8192]{2,1,0:T(8,128)(2,1)S(1)}) fusion(bf16[2,1,32,8192]{3,2,1,0:T(8,128)(2,1)} %param.4, pred[]{:T(512)S(6)} %eq.21, bf16[2,1,32,8192]{3,2,1,0:T(8,128)(2,1)S(1)} %copy-done.1), kind=kLoop, calls=%fused_computation.12 | loop fusion | flops 524288 | bytes 3145729 | tf_op jit(solution)/shard_map/jit(_where)/select_n | solution.py:175
  14.9 0.1 pad_maximum_fusion
  15.0 2.1 %collective-permute-start = (bf16[2,32,8192]{2,1,0:T(8,128)(2,1)S(1)}, bf16[2,32,8192]{2,1,0:T(8,128)(2,1)S(1)}, u32[]{:S(2)}, u32[]{:S(2)}) collective-permute-start(bf16[2,32,8192]{2,1,0:T(8,128)(2,1)S(1)} %pad_maximum_fusion), channel_id=1, source_target_pairs={{0,1},{1,0},{2,3},{3,2},{4,5},{5,4},{6,7},{7,6},{8,9},{9,8},{10,11... | collective-permute-start | bytes 3145736 | tf_op jit(solution)/shard_map/ppermute | solution.py:176
  17.1 2.4 %collective-permute-done.taken_ref = bf16[2,32,8192]{2,1,0:T(8,128)(2,1)S(1)} collective-permute-done((bf16[2,32,8192]{2,1,0:T(8,128)(2,1)S(1)}, bf16[2,32,8192]{2,1,0:T(8,128)(2,1)S(1)}, u32[]{:S(2)}, u32[]{:S(2)}) %collective-permute-start) | collective-permute-done | bytes 1048608 | tf_op jit(solution)/shard_map/ppermute | solution.py:176
  19.5 0.0 copy-start.2
  19.5 21.6 %all-to-all-done.w_ref = bf16[16,2,64,512]{3,2,1,0:T(8,128)(2,1)S(1)} async-done(((bf16[16,2,64,512]{3,2,1,0:T(8,128)(2,1)}), bf16[16,2,64,512]{3,2,1,0:T(8,128)(2,1)S(1)}, u32[]{:S(2)}, u32[]{:S(2)}) %all-to-all-start) | async-done | bytes 2097184 | tf_op jit(solution)/shard_map/all_to_all | solution.py:174
  41.1 0.0 copy-done.2
  41.1 4.8 %shard_map.59 = (bf16[32,8192]{1,0:T(8,128)(2,1)}, bf16[32,8192]{1,0:T(8,128)(2,1)}, bf16[2,32,8192]{2,1,0:T(8,128)(2,1)}, bf16[16,2,64,512]{3,2,1,0:T(8,128)(2,1)}) custom-call(s32[1]{0:T(128)} %bitcast.core_ref, bf16[2,32,8192]{2,1,0:T(8,128)(2,1)} %bitcast.35, bf16[2,32,8192]{2,1,0:T(8,128)(2,1)} %bitcast.36, bf16[2,32,8192]{2,1,0:T(8,128)(2,1)} %copy-done.2, ...), custom_call_target="tpu_custom_call" | custom-call | flops 402653184 | bytes 12582912 | tf_op jit(solution)/shard_map/pallas_call | solution.py:121
  45.9 2.6 %collective-permute-start.1 = (bf16[2,32,8192]{2,1,0:T(8,128)(2,1)}, bf16[2,32,8192]{2,1,0:T(8,128)(2,1)}, u32[]{:S(2)}, u32[]{:S(2)}) collective-permute-start(bf16[2,32,8192]{2,1,0:T(8,128)(2,1)} %get-tuple-element.19), channel_id=1, source_target_pairs={{0,1},{1,0},{2,3},{3,2},{4,5},{5,4},{6,7},{7,6},{8,9},{9,8},{10,11... | collective-permute-start | bytes 3145736 | tf_op jit(solution)/shard_map/ppermute | solution.py:182
  48.5 4.6 %all-to-all-start.1 = ((bf16[16,2,64,512]{3,2,1,0:T(8,128)(2,1)}), bf16[16,2,64,512]{3,2,1,0:T(8,128)(2,1)S(1)}, u32[]{:S(2)}, u32[]{:S(2)}) async-start(bf16[16,2,64,512]{3,2,1,0:T(8,128)(2,1)} %get-tuple-element.16), calls=%async_computation.1 | async-start | bytes 4194304 | tf_op jit(solution)/shard_map/all_to_all | solution.py:179
  53.1 0.0 collective-permute-done.1
  53.1 2.2 %slice_bitcast_fusion = (bf16[32,8192]{1,0:T(8,128)(2,1)}, bf16[32,8192]{1,0:T(8,128)(2,1)}) fusion(bf16[2,32,8192]{2,1,0:T(8,128)(2,1)} %collective-permute-done.1), kind=kLoop, calls=%fused_computation.4 | loop fusion | bytes 2097152 | tf_op jit(solution)/shard_map/squeeze | solution.py:183
  55.3 1.3 %collective-permute-start.2 = (bf16[32,8192]{1,0:T(8,128)(2,1)}, bf16[32,8192]{1,0:T(8,128)(2,1)S(1)}, u32[]{:S(2)}, u32[]{:S(2)}) collective-permute-start(bf16[32,8192]{1,0:T(8,128)(2,1)} %get-tuple-element.20), channel_id=1, source_target_pairs={{0,16},{1,17},{2,18},{3,19},{4,20},{5,21},{6,22},{7,23},{8,24},{9,... | collective-permute-start | bytes 1572872 | tf_op jit(solution)/shard_map/ppermute | solution.py:160
  56.6 1.3 %collective-permute-start.3 = (bf16[32,8192]{1,0:T(8,128)(2,1)}, bf16[32,8192]{1,0:T(8,128)(2,1)}, u32[]{:S(2)}, u32[]{:S(2)}) collective-permute-start(bf16[32,8192]{1,0:T(8,128)(2,1)} %get-tuple-element.21), channel_id=1, source_target_pairs={{16,0},{17,1},{18,2},{19,3},{20,4},{21,5},{22,6},{23,7},{24,8},{25... | collective-permute-start | bytes 1572872 | tf_op jit(solution)/shard_map/ppermute | solution.py:160
  57.9 4.0 %collective-permute-start.4 = (bf16[32,8192]{1,0:T(8,128)(2,1)}, bf16[32,8192]{1,0:T(8,128)(2,1)}, u32[]{:S(2)}, u32[]{:S(2)}) collective-permute-start(bf16[32,8192]{1,0:T(8,128)(2,1)} %get-tuple-element.22), channel_id=1, source_target_pairs={{0,16},{1,17},{2,18},{3,19},{4,20},{5,21},{6,22},{7,23},{8,24},{9,... | collective-permute-start | bytes 1572872 | tf_op jit(solution)/shard_map/ppermute | solution.py:160
  62.0 1.3 %collective-permute-start.5 = (bf16[32,8192]{1,0:T(8,128)(2,1)}, bf16[32,8192]{1,0:T(8,128)(2,1)}, u32[]{:S(2)}, u32[]{:S(2)}) collective-permute-start(bf16[32,8192]{1,0:T(8,128)(2,1)} %get-tuple-element.23), channel_id=1, source_target_pairs={{16,0},{17,1},{18,2},{19,3},{20,4},{21,5},{22,6},{23,7},{24,8},{25... | collective-permute-start | bytes 1572872 | tf_op jit(solution)/shard_map/ppermute | solution.py:160
  63.3 17.5 %all-to-all-done.1 = bf16[16,2,64,512]{3,2,1,0:T(8,128)(2,1)S(1)} async-done(((bf16[16,2,64,512]{3,2,1,0:T(8,128)(2,1)}), bf16[16,2,64,512]{3,2,1,0:T(8,128)(2,1)S(1)}, u32[]{:S(2)}, u32[]{:S(2)}) %all-to-all-start.1) | async-done | bytes 2097184 | tf_op jit(solution)/shard_map/all_to_all | solution.py:179
  80.8 0.3 convert_reduce_fusion.sums_ref
  81.1 0.0 collective-permute-done.2
  81.1 0.0 collective-permute-done.3
  81.1 5.4 %collective-permute-done.4 = bf16[32,8192]{1,0:T(8,128)(2,1)} collective-permute-done((bf16[32,8192]{1,0:T(8,128)(2,1)}, bf16[32,8192]{1,0:T(8,128)(2,1)}, u32[]{:S(2)}, u32[]{:S(2)}) %collective-permute-start.4) | collective-permute-done | bytes 524320 | tf_op jit(solution)/shard_map/ppermute | solution.py:160
  86.5 0.0 collective-permute-done.5
  86.5 1.1 broadcast_select_fusion.1
  87.6 5.5 %collective-permute-start.7 = (bf16[32,8192]{1,0:T(8,128)(2,1)S(1)}, bf16[32,8192]{1,0:T(8,128)(2,1)S(1)}, u32[]{:S(2)}, u32[]{:S(2)}) collective-permute-start(bf16[32,8192]{1,0:T(8,128)(2,1)S(1)} %broadcast_select_fusion.1), channel_id=1, source_target_pairs={{0,256},{1,257},{2,258},{3,259},{4,260},{5,261},{6,262},{7,263},{8... | collective-permute-start | bytes 1572872 | tf_op jit(solution)/shard_map/ppermute | solution.py:160
  93.1 1.9 %broadcast_select_fusion.3 = bf16[32,8192]{1,0:T(8,128)(2,1)} fusion(bf16[32,8192]{1,0:T(8,128)(2,1)S(1)} %collective-permute-done.2, bf16[32,8192]{1,0:T(8,128)(2,1)} %collective-permute-done.3, pred[]{:T(512)S(6)} %eq.22), kind=kLoop, calls=%fused_computation.17 | loop fusion | flops 262144 | bytes 1572865 | tf_op jit(solution)/shard_map/jit(_where)/select_n | solution.py:194
  95.0 0.7 collective-permute-start.6
  95.8 4.4 %collective-permute-start.8 = (bf16[2,2,64,512]{3,2,1,0:T(8,128)(2,1)S(1)}, bf16[2,2,64,512]{3,2,1,0:T(8,128)(2,1)S(1)}, u32[]{:S(2)}, u32[]{:S(2)}) collective-permute-start(bf16[2,2,64,512]{3,2,1,0:T(8,128)(2,1)S(1)} %convert_element_type.11), channel_id=1, source_target_pairs={{0,496},{16,480},{32,464},{48,448},{64,432},{80,416},{96,400},{112... | collective-permute-start | bytes 786440 | tf_op jit(solution)/shard_map/ppermute | solution.py:192
  100.2 22.8 %collective-permute-done.8.partner_ref = bf16[2,2,64,512]{3,2,1,0:T(8,128)(2,1)S(1)} collective-permute-done((bf16[2,2,64,512]{3,2,1,0:T(8,128)(2,1)S(1)}, bf16[2,2,64,512]{3,2,1,0:T(8,128)(2,1)S(1)}, u32[]{:S(2)}, u32[]{:S(2)}) %collective-permute-start.8) | collective-permute-done | bytes 262176 | tf_op jit(solution)/shard_map/ppermute | solution.py:192
  123.0 0.8 shard_map.60
  123.9 0.0 collective-permute-done.7
  123.9 0.0 collective-permute-done.6
  123.9 1.4 %select_bitcast_fusion.1 = (bf16[1,32,8192]{2,1,0:T(8,128)(2,1)S(1)}, bf16[1,32,8192]{2,1,0:T(8,128)(2,1)S(1)}, bf16[1,32,8192]{2,1,0:T(8,128)(2,1)S(1)}, bf16[1,32,8192]{2,1,0:T(8,128)(2,1)S(1)}) fusion(pred[]{:T(512)S(6)} %eq.21, bf16[32,8192]{1,0:T(8,128)(2,1)S(1)} %collective-permute-done.6, bf16[32,8192]{1,0:T(8,128)(2,1)} %collective-permute-done.3, ...), kind=kLoop, calls=%fused_computation.7 | loop fusion | flops 2621440 | bytes 5242885 | tf_op jit(solution)/shard_map/stack | solution.py:203
  125.3 1.1 maximum_bitcast_fusion.1
  126.3 1.1 maximum_bitcast_fusion
  (1 shorter events, 0.0 us)
Async XLA Ops:
  0.6 1.0 copy-start
  3.0 10.5 %copy-start.1 = (bf16[2,1,32,8192]{3,2,1,0:T(8,128)(2,1)S(1)}, bf16[2,1,32,8192]{3,2,1,0:T(8,128)(2,1)}, u32[]{:S(2)}) copy-start(bf16[2,1,32,8192]{3,2,1,0:T(8,128)(2,1)} %param.3) | copy-start | bytes 3145732
  3.0 38.1 %all-to-all-start = ((bf16[16,2,64,512]{3,2,1,0:T(8,128)(2,1)}), bf16[16,2,64,512]{3,2,1,0:T(8,128)(2,1)S(1)}, u32[]{:S(2)}, u32[]{:S(2)}) async-start(bf16[16,2,64,512]{3,2,1,0:T(8,128)(2,1)} %shard_map.58), calls=%async_computation | async-start | bytes 4194304 | tf_op jit(solution)/shard_map/all_to_all | solution.py:174
  15.0 4.6 %collective-permute-start = (bf16[2,32,8192]{2,1,0:T(8,128)(2,1)S(1)}, bf16[2,32,8192]{2,1,0:T(8,128)(2,1)S(1)}, u32[]{:S(2)}, u32[]{:S(2)}) collective-permute-start(bf16[2,32,8192]{2,1,0:T(8,128)(2,1)S(1)} %pad_maximum_fusion), channel_id=1, source_target_pairs={{0,1},{1,0},{2,3},{3,2},{4,5},{5,4},{6,7},{7,6},{8,9},{9,8},{10,11... | collective-permute-start | bytes 3145736 | tf_op jit(solution)/shard_map/ppermute | solution.py:176
  19.5 21.6 %copy-start.2 = (bf16[2,32,8192]{2,1,0:T(8,128)(2,1)}, bf16[2,32,8192]{2,1,0:T(8,128)(2,1)S(1)}, u32[]{:S(2)}) copy-start(bf16[2,32,8192]{2,1,0:T(8,128)(2,1)S(1)} %collective-permute-done.taken_ref) | copy-start | bytes 3145732
  45.9 7.2 %collective-permute-start.1 = (bf16[2,32,8192]{2,1,0:T(8,128)(2,1)}, bf16[2,32,8192]{2,1,0:T(8,128)(2,1)}, u32[]{:S(2)}, u32[]{:S(2)}) collective-permute-start(bf16[2,32,8192]{2,1,0:T(8,128)(2,1)} %get-tuple-element.19), channel_id=1, source_target_pairs={{0,1},{1,0},{2,3},{3,2},{4,5},{5,4},{6,7},{7,6},{8,9},{9,8},{10,11... | collective-permute-start | bytes 3145736 | tf_op jit(solution)/shard_map/ppermute | solution.py:182
  48.5 32.3 %all-to-all-start.1 = ((bf16[16,2,64,512]{3,2,1,0:T(8,128)(2,1)}), bf16[16,2,64,512]{3,2,1,0:T(8,128)(2,1)S(1)}, u32[]{:S(2)}, u32[]{:S(2)}) async-start(bf16[16,2,64,512]{3,2,1,0:T(8,128)(2,1)} %get-tuple-element.16), calls=%async_computation.1 | async-start | bytes 4194304 | tf_op jit(solution)/shard_map/all_to_all | solution.py:179
  55.3 25.7 %collective-permute-start.2 = (bf16[32,8192]{1,0:T(8,128)(2,1)}, bf16[32,8192]{1,0:T(8,128)(2,1)S(1)}, u32[]{:S(2)}, u32[]{:S(2)}) collective-permute-start(bf16[32,8192]{1,0:T(8,128)(2,1)} %get-tuple-element.20), channel_id=1, source_target_pairs={{0,16},{1,17},{2,18},{3,19},{4,20},{5,21},{6,22},{7,23},{8,24},{9,... | collective-permute-start | bytes 1572872 | tf_op jit(solution)/shard_map/ppermute | solution.py:160
  56.6 24.4 %collective-permute-start.3 = (bf16[32,8192]{1,0:T(8,128)(2,1)}, bf16[32,8192]{1,0:T(8,128)(2,1)}, u32[]{:S(2)}, u32[]{:S(2)}) collective-permute-start(bf16[32,8192]{1,0:T(8,128)(2,1)} %get-tuple-element.21), channel_id=1, source_target_pairs={{16,0},{17,1},{18,2},{19,3},{20,4},{21,5},{22,6},{23,7},{24,8},{25... | collective-permute-start | bytes 1572872 | tf_op jit(solution)/shard_map/ppermute | solution.py:160
  57.9 28.6 %collective-permute-start.4 = (bf16[32,8192]{1,0:T(8,128)(2,1)}, bf16[32,8192]{1,0:T(8,128)(2,1)}, u32[]{:S(2)}, u32[]{:S(2)}) collective-permute-start(bf16[32,8192]{1,0:T(8,128)(2,1)} %get-tuple-element.22), channel_id=1, source_target_pairs={{0,16},{1,17},{2,18},{3,19},{4,20},{5,21},{6,22},{7,23},{8,24},{9,... | collective-permute-start | bytes 1572872 | tf_op jit(solution)/shard_map/ppermute | solution.py:160
  62.0 24.6 %collective-permute-start.5 = (bf16[32,8192]{1,0:T(8,128)(2,1)}, bf16[32,8192]{1,0:T(8,128)(2,1)}, u32[]{:S(2)}, u32[]{:S(2)}) collective-permute-start(bf16[32,8192]{1,0:T(8,128)(2,1)} %get-tuple-element.23), channel_id=1, source_target_pairs={{16,0},{17,1},{18,2},{19,3},{20,4},{21,5},{22,6},{23,7},{24,8},{25... | collective-permute-start | bytes 1572872 | tf_op jit(solution)/shard_map/ppermute | solution.py:160
  87.6 36.2 %collective-permute-start.7 = (bf16[32,8192]{1,0:T(8,128)(2,1)S(1)}, bf16[32,8192]{1,0:T(8,128)(2,1)S(1)}, u32[]{:S(2)}, u32[]{:S(2)}) collective-permute-start(bf16[32,8192]{1,0:T(8,128)(2,1)S(1)} %broadcast_select_fusion.1), channel_id=1, source_target_pairs={{0,256},{1,257},{2,258},{3,259},{4,260},{5,261},{6,262},{7,263},{8... | collective-permute-start | bytes 1572872 | tf_op jit(solution)/shard_map/ppermute | solution.py:160
  95.0 28.8 %collective-permute-start.6 = (bf16[32,8192]{1,0:T(8,128)(2,1)}, bf16[32,8192]{1,0:T(8,128)(2,1)S(1)}, u32[]{:S(2)}, u32[]{:S(2)}) collective-permute-start(bf16[32,8192]{1,0:T(8,128)(2,1)} %broadcast_select_fusion.3), channel_id=1, source_target_pairs={{256,264},{257,265},{258,266},{259,267},{260,268},{261,269},{262,2... | collective-permute-start | bytes 1572872 | tf_op jit(solution)/shard_map/ppermute | solution.py:160
  95.8 27.3 %collective-permute-start.8 = (bf16[2,2,64,512]{3,2,1,0:T(8,128)(2,1)S(1)}, bf16[2,2,64,512]{3,2,1,0:T(8,128)(2,1)S(1)}, u32[]{:S(2)}, u32[]{:S(2)}) collective-permute-start(bf16[2,2,64,512]{3,2,1,0:T(8,128)(2,1)S(1)} %convert_element_type.11), channel_id=1, source_target_pairs={{0,496},{16,480},{32,464},{48,448},{64,432},{80,416},{96,400},{112... | collective-permute-start | bytes 786440 | tf_op jit(solution)/shard_map/ppermute | solution.py:192

commit v4 on v3

v4 whole, which is shorter than its diff:
```python
import functools

import jax
import jax.numpy as jnp
from jax import lax
from jax.experimental import pallas as pl
from jax.experimental.pallas import tpu as pltpu
from jax.sharding import PartitionSpec as P

WHOLE = pl.BlockSpec(memory_space=pltpu.VMEM)
ANYWHERE = pl.BlockSpec(memory_space=pl.ANY)
SCALARS = pl.BlockSpec(memory_space=pltpu.SMEM)
ACROSS = (((1,), (1,)), ((), ()))
OVER_TOKENS = (((0,), (0,)), ((), ()))
PARAMS = pltpu.CompilerParams(vmem_limit_bytes=12 << 20)
F32 = jnp.float32


def spread_kernel(w_ref, out_ref, sems):
    copies = [
        pltpu.make_async_copy(w_ref, out_ref.at[pl.ds(2 * i, 2)], sems.at[i]) for i in range(out_ref.shape[0] // 2)
    ]
    for copy in copies:
        copy.start()
    for copy in copies:
        copy.wait()


def spread(w, n_dp):
    return pl.pallas_call(
        spread_kernel,
        out_shape=pltpu.HBM((n_dp,) + w.shape[1:], w.dtype),
        in_specs=[WHOLE],
        out_specs=ANYWHERE,
        scratch_shapes=[pltpu.SemaphoreType.DMA((n_dp // 2,))],
        compiler_params=PARAMS,
        cost_estimate=pl.CostEstimate(flops=0, bytes_accessed=n_dp * w.size, transcendentals=0),
    )(w)


def fetch(core, x_ref, g_ref, taken_ref, xs, gs, sems):
    tokens, model = x_ref.shape[1:]
    chunks = sems.shape[0]
    own, others = pl.ds(0, tokens), pl.ds(tokens, tokens)
    copies = []
    for j in range(chunks):
        cols = pl.ds(j * (model // chunks), model // chunks)
        copies.append([
            pltpu.make_async_copy(x_ref.at[core, :, cols], xs.at[own, cols], sems.at[j, 0]),
            pltpu.make_async_copy(taken_ref.at[0, :, cols], xs.at[others, cols], sems.at[j, 1]),
            pltpu.make_async_copy(g_ref.at[core, :, cols], gs.at[own, cols], sems.at[j, 2]),
            pltpu.make_async_copy(taken_ref.at[1, :, cols], gs.at[others, cols], sems.at[j, 3]),
        ])
        for copy in copies[-1]:
            copy.start()
    return copies


def partials_kernel(
    core_ref, x_ref, g_ref, taken_ref, w_ref, part_ref, hidden_ref, scaled_ref, back_ref, xs, gs, ps, loads, stores
):
    slices, _, rank, width = w_ref.shape
    tokens, model = xs.shape
    chunks = loads.shape[0]
    per = slices // chunks
    fetches = fetch(core_ref[0], x_ref, g_ref, taken_ref, xs, gs, loads)

    u = jnp.zeros((tokens, rank), F32)
    v = jnp.zeros((tokens, rank), F32)
    squares = jnp.zeros((tokens, 128), F32)
    for i in range(slices):
        if i % per == 0:
            for copy in fetches[i // per]:
                copy.wait()
        cols = pl.ds(i * width, width)
        x = xs[:, cols]
        u += lax.dot_general(x, w_ref[i, 0], ACROSS, preferred_element_type=F32)
        v += lax.dot_general(gs[:, cols], w_ref[i, 1], ACROSS, preferred_element_type=F32)
        xf = x.astype(F32)
        for j in range(width // 128):
            piece = xf[:, j * 128:(j + 1) * 128]
            squares += piece * piece
    scale = lax.rsqrt(jnp.sum(squares, axis=1, keepdims=True) / model + 1e-05)
    pre = scale * u
    sig = jax.nn.sigmoid(pre)
    hidden = (pre * sig).astype(jnp.bfloat16)
    dpre = v * (sig * (1.0 + pre * (1.0 - sig)))
    inner = jnp.sum(dpre * u, axis=1, keepdims=True) / model
    scaled = (scale * dpre).astype(jnp.bfloat16)
    hidden_ref[...] = hidden
    scaled_ref[...] = scaled
    back_ref[...] = jnp.broadcast_to(inner * scale * scale * scale, back_ref.shape)

    stored = []
    for i in range(slices):
        cols = pl.ds(i * width, width)
        ps[i, 0] = lax.dot_general(scaled, xs[:, cols], OVER_TOKENS, preferred_element_type=F32).astype(ps.dtype)
        ps[i, 1] = lax.dot_general(hidden, gs[:, cols], OVER_TOKENS, preferred_element_type=F32).astype(ps.dtype)
        if i % per == per - 1:
            some = pl.ds(i + 1 - per, per)
            stored.append(pltpu.make_async_copy(ps.at[some], part_ref.at[some], stores.at[i // per]))
            stored[-1].start()
    for copy in stored:
        copy.wait()


def partials(core, x, g, taken, w):
    tokens, model, rank = 2 * x.shape[1], x.shape[2], w.shape[2]
    both = pltpu.VMEM((tokens, model), x.dtype)
    inside = jax.ShapeDtypeStruct((tokens, rank), x.dtype)
    return pl.pallas_call(
        partials_kernel,
        out_shape=(pltpu.HBM(w.shape, w.dtype), inside, inside, jax.ShapeDtypeStruct((tokens, 128), F32)),
        in_specs=[SCALARS] + [ANYWHERE] * 3 + [WHOLE],
        out_specs=(ANYWHERE,) + (WHOLE,) * 3,
        scratch_shapes=[
            both,
            both,
            pltpu.VMEM(w.shape, w.dtype),
            pltpu.SemaphoreType.DMA((4, 4)),
            pltpu.SemaphoreType.DMA((4,)),
        ],
        compiler_params=PARAMS,
        cost_estimate=pl.CostEstimate(flops=4 * tokens * w.size, bytes_accessed=8 << 20, transcendentals=0),
    )(core, x, g, taken, w)


def outputs_kernel(
    core_ref, x_ref, g_ref, taken_ref, w_ref, hidden_ref, scaled_ref, back_ref, up_ref, down_ref, send_ref, xs, gs, ms,
    loads, stores
):
    core = core_ref[0]
    is_down = core == 0
    slices, _, rank, width = w_ref.shape
    tokens, model = x_ref.shape[1:]
    chunks = loads.shape[0]
    per = slices // chunks
    own, others = pl.ds(0, tokens), pl.ds(tokens, tokens)
    fetches = fetch(core, x_ref, g_ref, taken_ref, xs, gs, loads)
    hidden, scaled, back = hidden_ref[...], scaled_ref[...], back_ref[:, :1]
    stored = []
    for i in range(slices):
        if i % per == 0:
            for copy in fetches[i // per]:
                copy.wait()
        cols = pl.ds(i * width, width)
        xf, gf = xs[:, cols].astype(F32), gs[:, cols].astype(F32)
        y = (xf + jnp.dot(hidden, w_ref[i, 1], preferred_element_type=F32)).astype(ms.dtype)
        dx = (gf + jnp.dot(scaled, w_ref[i, 0], preferred_element_type=F32) - xf * back).astype(ms.dtype)
        ms[0, :, cols] = jnp.where(is_down, y, dx)
        ms[1, :, cols] = jnp.where(is_down, dx, y)
        if i % per == per - 1:
            j = i // per
            cols = pl.ds(j * (model // chunks), model // chunks)
            for copy in (
                pltpu.make_async_copy(ms.at[0, own, cols], up_ref.at[:, cols], stores.at[j, 0]),
                pltpu.make_async_copy(ms.at[1, own, cols], down_ref.at[:, cols], stores.at[j, 1]),
                pltpu.make_async_copy(ms.at[0, others, cols], send_ref.at[0, :, cols], stores.at[j, 2]),
                pltpu.make_async_copy(ms.at[1, others, cols], send_ref.at[1, :, cols], stores.at[j, 3]),
            ):
                copy.start()
                stored.append(copy)
    for copy in stored:
        copy.wait()


def outputs(core, x, g, taken, w, hidden, scaled, back):
    tokens, model = x.shape[1:]
    one = pltpu.HBM((tokens, model), x.dtype)
    both = pltpu.VMEM((2 * tokens, model), x.dtype)
    return pl.pallas_call(
        outputs_kernel,
        out_shape=(one, one, pltpu.HBM((2, tokens, model), x.dtype)),
        in_specs=[SCALARS] + [ANYWHERE] * 3 + [WHOLE] * 4,
        out_specs=(ANYWHERE,) * 3,
        scratch_shapes=[
            both,
            both,
            pltpu.VMEM((2, 2 * tokens, model), x.dtype),
            pltpu.SemaphoreType.DMA((4, 4)),
            pltpu.SemaphoreType.DMA((4, 4)),
        ],
        compiler_params=PARAMS,
        cost_estimate=pl.CostEstimate(flops=4 * tokens * w.size, bytes_accessed=8 << 20, transcendentals=0),
    )(core, x, g, taken, w, hidden, scaled, back)


def split_kernel(both_ref, first_ref, second_ref, sems):
    copies = [
        pltpu.make_async_copy(both_ref.at[0], first_ref, sems.at[0]),
        pltpu.make_async_copy(both_ref.at[1], second_ref, sems.at[1]),
    ]
    for copy in copies:
        copy.start()
    for copy in copies:
        copy.wait()


def split(both):
    one = pltpu.HBM(both.shape[1:], both.dtype)
    return pl.pallas_call(
        split_kernel,
        out_shape=(one, one),
        in_specs=[ANYWHERE],
        out_specs=(ANYWHERE,) * 2,
        scratch_shapes=[pltpu.SemaphoreType.DMA((2,))],
        compiler_params=PARAMS,
        cost_estimate=pl.CostEstimate(flops=0, bytes_accessed=4 * both.size, transcendentals=0),
    )(both)


def crossing_kernel(count, at_ref, up_own, down_own, up_got, down_got, own_out, got_out, sems):
    section = at_ref[0]
    half = count // 2

    def copy(src, dst, i):
        moving = pltpu.make_async_copy(src, dst, sems.at[i])
        moving.start()
        moving.wait()

    @pl.when(section == half)
    def _():
        copy(up_own, own_out, 0)

    @pl.when(section == half - 1)
    def _():
        copy(down_own, own_out, 0)

    @pl.when(section == 0)
    def _():
        copy(up_got, got_out, 1)

    @pl.when(section == count - 1)
    def _():
        copy(down_got, got_out, 1)


def crossing(count, section, *moved_parts):
    one = pltpu.HBM(moved_parts[0].shape, moved_parts[0].dtype)
    return pl.pallas_call(
        functools.partial(crossing_kernel, count),
        out_shape=(one, one),
        in_specs=[SCALARS] + [ANYWHERE] * 4,
        out_specs=(ANYWHERE,) * 2,
        scratch_shapes=[pltpu.SemaphoreType.DMA((2,))],
        compiler_params=PARAMS,
        cost_estimate=pl.CostEstimate(flops=0, bytes_accessed=4 * moved_parts[0].size, transcendentals=0),
    )(section, *moved_parts)


def finish_kernel(
    count, core_ref, at_ref, up_own, down_own, up_got, down_got, crossed_own, crossed_got, next_ref, prev_ref, sems
):
    core, section = core_ref[0], at_ref[0]
    half = count // 2

    def put(i, src, on_down, on_up):
        @pl.when(core == 0)
        def _():
            pltpu.make_async_copy(src, on_down, sems.at[i]).start()

        @pl.when(core != 0)
        def _():
            pltpu.make_async_copy(src, on_up, sems.at[i]).start()

    places = (
        (next_ref.at[0], prev_ref.at[1]),
        (prev_ref.at[0], next_ref.at[1]),
        (prev_ref.at[1], next_ref.at[0]),
        (next_ref.at[1], prev_ref.at[0]),
    )

    @pl.when(section == half)
    def _():
        put(0, crossed_own, *places[0])
        put(2, crossed_got, *places[2])

    @pl.when(section != half)
    def _():
        put(0, up_own, *places[0])

        @pl.when(section == 0)
        def _():
            put(2, up_own, *places[2])

        @pl.when(section != 0)
        def _():
            put(2, up_got, *places[2])

    @pl.when(section == half - 1)
    def _():
        put(1, crossed_own, *places[1])
        put(3, crossed_got, *places[3])

    @pl.when(section != half - 1)
    def _():
        put(1, down_own, *places[1])

        @pl.when(section == count - 1)
        def _():
            put(3, down_own, *places[3])

        @pl.when(section != count - 1)
        def _():
            put(3, down_got, *places[3])

    for i in range(4):
        pltpu.make_async_copy(up_own, next_ref.at[0], sems.at[i]).wait()


def finish(count, core, section, *moved_parts):
    tokens, model = moved_parts[0].shape
    both = pltpu.HBM((2, tokens, model), moved_parts[0].dtype)
    return pl.pallas_call(
        functools.partial(finish_kernel, count),
        out_shape=(both, both),
        in_specs=[SCALARS] * 2 + [ANYWHERE] * 6,
        out_specs=(ANYWHERE,) * 2,
        scratch_shapes=[pltpu.SemaphoreType.DMA((4,))],
        compiler_params=PARAMS,
        cost_estimate=pl.CostEstimate(flops=0, bytes_accessed=16 * tokens * model, transcendentals=0),
    )(core, section, *moved_parts)


def add_kernel(sums_ref, partner_ref, out_ref):
    out_ref[0] = sums_ref[0] + partner_ref[1].astype(F32)
    out_ref[1] = sums_ref[1] + partner_ref[0].astype(F32)


def add_mirrored(sums, partner):
    return pl.pallas_call(
        add_kernel,
        out_shape=jax.ShapeDtypeStruct(sums.shape, F32),
        in_specs=[WHOLE] * 2,
        out_specs=WHOLE,
        compiler_params=PARAMS,
        cost_estimate=pl.CostEstimate(flops=40_000_000_000, bytes_accessed=2 << 20, transcendentals=0),
    )(sums, partner)


def moved(value, pairs, n_dp, flip=()):
    turn = n_dp // 2
    routes = [(a * n_dp + d, b * n_dp + d) for a, b in pairs for d in range(n_dp)]
    routes += [(a * n_dp + d, b * n_dp + (d ^ turn)) for a, b in flip for d in range(n_dp)]
    return lax.ppermute(value, ("section", "dp"), routes)


def shards(section_inputs, out_grads, adapters):
    n_dp = lax.axis_size("dp")
    count = lax.axis_size("section")
    half = count // 2
    core = jnp.full((1,), lax.axis_index("dp") % 2, jnp.int32)
    section = jnp.full((1,), lax.axis_index("section"), jnp.int32)
    is_down = core[0] == 0
    swap = [(i, i ^ 1) for i in range(n_dp)]
    inputs, grads = section_inputs[:, 0], out_grads[:, 0]

    gathered = lax.all_to_all(spread(adapters[:, 0], n_dp), "dp", 0, 0, tiled=True)
    given = jnp.stack([jnp.where(is_down, inputs[1], inputs[0]), jnp.where(is_down, grads[1], grads[0])])
    taken = lax.ppermute(given, "dp", swap)
    x, g, taken = (pltpu.with_memory_space_constraint(a, pltpu.HBM) for a in (inputs, grads, taken))
    parts, hidden, scaled, back = partials(core, x, g, taken, gathered)

    terms = lax.all_to_all(parts, "dp", 0, 0, tiled=True)
    sums = jnp.sum(terms.reshape((n_dp // 2, 2) + terms.shape[1:]).astype(F32), axis=0)

    up_own, down_own, send = outputs(core, x, g, taken, gathered, hidden, scaled, back)
    got = lax.ppermute(send, "dp", swap)
    up_own, down_own, got = lax.optimization_barrier((up_own, down_own, got))
    up_got, down_got = split(got)
    ups = [(i, i + 1) for i in range(count - 1) if i != half - 1]
    downs = [(i, i - 1) for i in range(1, count) if i != half]
    up_own = moved(up_own, ups, n_dp, [(half - 1, half)])
    down_own = moved(down_own, downs, n_dp, [(half, half - 1)])
    up_got = moved(up_got, ups + [(half - 1, 0)], n_dp)
    down_got = moved(down_got, downs + [(half, count - 1)], n_dp)
    narrow = sums.astype(jnp.bfloat16)
    partner = lax.ppermute(narrow, "section", [(i, count - 1 - i) for i in range(count)])
    narrow, up_own, down_own, up_got, down_got = lax.optimization_barrier((narrow, up_own, down_own, up_got, down_got))

    cross_own, cross_got = crossing(count, section, up_own, down_own, up_got, down_got)
    crossed_own = moved(cross_own, [], n_dp, [(half, half), (half - 1, half - 1)])
    crossed_got = moved(cross_got, [(0, half), (count - 1, half - 1)], n_dp)
    summed = add_mirrored(sums, partner)
    next_inputs, prev_grads = finish(
        count, core, section, up_own, down_own, up_got, down_got, crossed_own, crossed_got
    )
    return (next_inputs[:, None], prev_grads[:, None], summed[:, None])


def solution(mesh):
    in_specs = (
        P(None, "section", "dp", None),
        P(None, "section", "dp", None),
        P(None, "section", None, None, "dp"),
    )
    out_specs = (
        P(None, "section", "dp", None),
        P(None, "section", "dp", None),
        P(None, "section", None, None, "dp"),
    )
    return jax.shard_map(shards, mesh=mesh, in_specs=in_specs, out_specs=out_specs, check_vma=False)
```

time: 128 us -> 129 us (level)
  the two profiles are of different devices: /device:TPU:1 before, /device:TPU:22 now
where the time goes in v4:
time: 129 us; the launch traced here: 128 us
  waiting for transfers between devices  61.5 us (48%)
  starting transfers between devices  49 us (38%)
  Pallas kernels  12.6 us (10%)
  other arithmetic  3.38 us (3%)
    ppermute x6, waiting for transfers between devices, moved(): return lax.ppermute(value, ('section', 'dp'), routes)  36.6 us
    ppermute x6, starting transfers between devices, moved(): return lax.ppermute(value, ('section', 'dp'), routes)  22.9 us
    all_to_all x1, waiting for transfers between devices, shards(): lax.all_to_all(spread(adapters[:, 0], n_dp), 'dp', 0, 0, tiled=True)  19.7 us
    ppermute x1, starting transfers between devices, shards(): lax.ppermute(narrow, 'section', [(i, count - 1 - i) for i in range(count)])  9.42 us
    all_to_all x1, starting transfers between devices, shards(): terms = lax.all_to_all(parts, 'dp', 0, 0, tiled=True)  6.94 us
    all_to_all x1, starting transfers between devices, shards(): lax.all_to_all(spread(adapters[:, 0], n_dp), 'dp', 0, 0, tiled=True)  5.65 us
    pallas_call x1, Pallas kernels, partials(): pl.pallas_call(partials_kernel, out_shape=(pltpu.HBM(w.shape, w.dtype), i...  3.77 us
    pallas_call x1, Pallas kernels, outputs(): pl.pallas_call(outputs_kernel, out_shape=(one, one, pltpu.HBM((2, tokens,...  3.4 us
  transfers between devices with their start and end apart: 11, of which 6 were waited for; matrix products, arithmetic and copies ran while one was open for 3% of the time, Pallas kernels for 5%

profile of v4, /device:TPU:22, one launch (start us, length us, event | category | flops | bytes accessed | tf_op | source)
XLA Modules:
  0.0 128.2 jit_solution(17905098586960378992)
XLA Ops:
  0.6 0.0 copy-start
  0.6 0.9 copy-done
  1.6 1.4 %shard_map.58 = bf16[16,2,64,512]{3,2,1,0:T(8,128)(2,1)} custom-call(bf16[2,2,64,512]{3,2,1,0:T(8,128)(2,1)S(1)} %bitcast.20), custom_call_target="tpu_custom_call" | custom-call | bytes 2097152 | tf_op jit(solution)/shard_map/pallas_call | solution.py:30
  3.0 0.0 copy-start.1
  3.0 5.7 %all-to-all-start = ((bf16[16,2,64,512]{3,2,1,0:T(8,128)(2,1)}), bf16[16,2,64,512]{3,2,1,0:T(8,128)(2,1)S(1)}, u32[]{:S(2)}, u32[]{:S(2)}) async-start(bf16[16,2,64,512]{3,2,1,0:T(8,128)(2,1)} %shard_map.58), calls=%async_computation | async-start | bytes 4194304 | tf_op jit(solution)/shard_map/all_to_all | solution.py:358
  8.7 0.0 copy-done.1
  8.7 1.3 %select_bitcast_fusion = (bf16[1,32,8192]{2,1,0:T(8,128)(2,1)S(1)}, bf16[1,32,8192]{2,1,0:T(8,128)(2,1)S(1)}) fusion(bf16[2,1,32,8192]{3,2,1,0:T(8,128)(2,1)} %param.4, pred[]{:T(512)S(6)} %eq.5, bf16[2,1,32,8192]{3,2,1,0:T(8,128)(2,1)S(1)} %copy-done.1), kind=kLoop, calls=%fused_computation.2 | loop fusion | flops 524288 | bytes 3145729 | tf_op jit(solution)/shard_map/jit(_where)/select_n | solution.py:359
  10.0 0.1 pad_maximum_fusion
  10.1 2.1 %collective-permute-start = (bf16[2,32,8192]{2,1,0:T(8,128)(2,1)S(1)}, bf16[2,32,8192]{2,1,0:T(8,128)(2,1)S(1)}, u32[]{:S(2)}, u32[]{:S(2)}) collective-permute-start(bf16[2,32,8192]{2,1,0:T(8,128)(2,1)S(1)} %pad_maximum_fusion), channel_id=1, source_target_pairs={{0,1},{1,0},{2,3},{3,2},{4,5},{5,4},{6,7},{7,6},{8,9},{9,8},{10,11... | collective-permute-start | bytes 3145736 | tf_op jit(solution)/shard_map/ppermute | solution.py:360
  12.2 2.5 %collective-permute-done.taken_ref = bf16[2,32,8192]{2,1,0:T(8,128)(2,1)S(1)} collective-permute-done((bf16[2,32,8192]{2,1,0:T(8,128)(2,1)S(1)}, bf16[2,32,8192]{2,1,0:T(8,128)(2,1)S(1)}, u32[]{:S(2)}, u32[]{:S(2)}) %collective-permute-start) | collective-permute-done | bytes 1048608 | tf_op jit(solution)/shard_map/ppermute | solution.py:360
  14.6 0.0 copy-start.2
  14.6 19.7 %all-to-all-done.w_ref = bf16[16,2,64,512]{3,2,1,0:T(8,128)(2,1)S(1)} async-done(((bf16[16,2,64,512]{3,2,1,0:T(8,128)(2,1)}), bf16[16,2,64,512]{3,2,1,0:T(8,128)(2,1)S(1)}, u32[]{:S(2)}, u32[]{:S(2)}) %all-to-all-start) | async-done | bytes 2097184 | tf_op jit(solution)/shard_map/all_to_all | solution.py:358
  34.4 0.0 copy-done.2
  34.4 3.8 %shard_map.59 = (bf16[16,2,64,512]{3,2,1,0:T(8,128)(2,1)}, bf16[64,64]{1,0:T(8,128)(2,1)S(1)}, bf16[64,64]{1,0:T(8,128)(2,1)S(1)}, f32[64,128]{1,0:T(8,128)S(1)}) custom-call(s32[1]{0:T(128)} %bitcast.core_ref, bf16[2,32,8192]{2,1,0:T(8,128)(2,1)} %bitcast.21, bf16[2,32,8192]{2,1,0:T(8,128)(2,1)} %bitcast.23, bf16[2,32,8192]{2,1,0:T(8,128)(2,1)} %copy-done.2, ...), custom_call_target="tpu_custom_call" | custom-call | flops 268435456 | bytes 8388608 | tf_op jit(solution)/shard_map/pallas_call | solution.py:111
  38.2 6.9 %all-to-all-start.1 = ((bf16[16,2,64,512]{3,2,1,0:T(8,128)(2,1)}), bf16[16,2,64,512]{3,2,1,0:T(8,128)(2,1)}, u32[]{:S(2)}, u32[]{:S(2)}) async-start(bf16[16,2,64,512]{3,2,1,0:T(8,128)(2,1)} %get-tuple-element.23), calls=%async_computation.1 | async-start | bytes 4194304 | tf_op jit(solution)/shard_map/all_to_all | solution.py:364
  45.1 3.4 %shard_map.60 = (bf16[32,8192]{1,0:T(8,128)(2,1)}, bf16[32,8192]{1,0:T(8,128)(2,1)}, bf16[2,32,8192]{2,1,0:T(8,128)(2,1)}) custom-call(s32[1]{0:T(128)} %bitcast.core_ref, bf16[2,32,8192]{2,1,0:T(8,128)(2,1)} %bitcast.22, bf16[2,32,8192]{2,1,0:T(8,128)(2,1)} %bitcast.24, bf16[2,32,8192]{2,1,0:T(8,128)(2,1)} %copy-done.2, ...), custom_call_target="tpu_custom_call" | custom-call | flops 134217728 | bytes 8388608 | tf_op jit(solution)/shard_map/pallas_call | solution.py:171
  48.5 2.1 %collective-permute-start.1 = (bf16[2,32,8192]{2,1,0:T(8,128)(2,1)}, bf16[2,32,8192]{2,1,0:T(8,128)(2,1)S(1)}, u32[]{:S(2)}, u32[]{:S(2)}) collective-permute-start(bf16[2,32,8192]{2,1,0:T(8,128)(2,1)} %get-tuple-element.29), channel_id=1, source_target_pairs={{0,1},{1,0},{2,3},{3,2},{4,5},{5,4},{6,7},{7,6},{8,9},{9,8},{10,11... | collective-permute-start | bytes 3145736 | tf_op jit(solution)/shard_map/ppermute | solution.py:368
  50.6 2.7 %collective-permute-done.1.both_ref = bf16[2,32,8192]{2,1,0:T(8,128)(2,1)S(1)} collective-permute-done((bf16[2,32,8192]{2,1,0:T(8,128)(2,1)}, bf16[2,32,8192]{2,1,0:T(8,128)(2,1)S(1)}, u32[]{:S(2)}, u32[]{:S(2)}) %collective-permute-start.1) | collective-permute-done | bytes 1048608 | tf_op jit(solution)/shard_map/ppermute | solution.py:368
  53.3 3.8 %collective-permute-start.2 = (bf16[32,8192]{1,0:T(8,128)(2,1)}, bf16[32,8192]{1,0:T(8,128)(2,1)S(1)}, u32[]{:S(2)}, u32[]{:S(2)}) collective-permute-start(bf16[32,8192]{1,0:T(8,128)(2,1)} %get-tuple-element.30), channel_id=1, source_target_pairs={{0,16},{1,17},{2,18},{3,19},{4,20},{5,21},{6,22},{7,23},{8,24},{9,... | collective-permute-start | bytes 1572872 | tf_op jit(solution)/shard_map/ppermute | solution.py:345
  57.1 9.6 %collective-permute-start.3 = (bf16[32,8192]{1,0:T(8,128)(2,1)}, bf16[32,8192]{1,0:T(8,128)(2,1)S(1)}, u32[]{:S(2)}, u32[]{:S(2)}) collective-permute-start(bf16[32,8192]{1,0:T(8,128)(2,1)} %get-tuple-element.31), channel_id=1, source_target_pairs={{16,0},{17,1},{18,2},{19,3},{20,4},{21,5},{22,6},{23,7},{24,8},{25... | collective-permute-start | bytes 1572872 | tf_op jit(solution)/shard_map/ppermute | solution.py:345
  66.7 1.0 shard_map.61
  67.6 1.3 %collective-permute-start.4 = (bf16[32,8192]{1,0:T(8,128)(2,1)}, bf16[32,8192]{1,0:T(8,128)(2,1)S(1)}, u32[]{:S(2)}, u32[]{:S(2)}) collective-permute-start(bf16[32,8192]{1,0:T(8,128)(2,1)} %get-tuple-element.33), channel_id=1, source_target_pairs={{0,16},{1,17},{2,18},{3,19},{4,20},{5,21},{6,22},{7,23},{8,24},{9,... | collective-permute-start | bytes 1572872 | tf_op jit(solution)/shard_map/ppermute | solution.py:345
  69.0 3.8 %collective-permute-start.5 = (bf16[32,8192]{1,0:T(8,128)(2,1)}, bf16[32,8192]{1,0:T(8,128)(2,1)S(1)}, u32[]{:S(2)}, u32[]{:S(2)}) collective-permute-start(bf16[32,8192]{1,0:T(8,128)(2,1)} %get-tuple-element.34), channel_id=1, source_target_pairs={{16,0},{17,1},{18,2},{19,3},{20,4},{21,5},{22,6},{23,7},{24,8},{25... | collective-permute-start | bytes 1572872 | tf_op jit(solution)/shard_map/ppermute | solution.py:345
  72.8 0.0 all-to-all-done.1
  72.8 1.9 %convert_reduce_fusion.sums_ref = f32[2,2,64,512]{3,2,1,0:T(8,128)S(1)} fusion(bf16[8,2,2,64,512]{4,3,2,1,0:T(8,128)(2,1)} %bitcast.14), kind=kLoop, calls=%fused_computation | loop fusion | flops 1966080 | bytes 2621440 | tf_op jit(solution)/shard_map/reduce_sum | solution.py:365
  74.8 9.4 %collective-permute-start.8 = (bf16[2,2,64,512]{3,2,1,0:T(8,128)(2,1)S(1)}, bf16[2,2,64,512]{3,2,1,0:T(8,128)(2,1)S(1)}, u32[]{:S(2)}, u32[]{:S(2)}) collective-permute-start(bf16[2,2,64,512]{3,2,1,0:T(8,128)(2,1)S(1)} %convert_element_type.11), channel_id=1, source_target_pairs={{0,496},{16,480},{32,464},{48,448},{64,432},{80,416},{96,400},{112... | collective-permute-start | bytes 786440 | tf_op jit(solution)/shard_map/ppermute | solution.py:378
  84.2 0.0 collective-permute-done.2.up_own
  84.3 0.0 collective-permute-done.3.down_own
  84.3 0.0 collective-permute-done.4.up_got
  84.3 23.0 %collective-permute-done.5.down_got = bf16[32,8192]{1,0:T(8,128)(2,1)S(1)} collective-permute-done((bf16[32,8192]{1,0:T(8,128)(2,1)}, bf16[32,8192]{1,0:T(8,128)(2,1)S(1)}, u32[]{:S(2)}, u32[]{:S(2)}) %collective-permute-start.5) | collective-permute-done | bytes 524320 | tf_op jit(solution)/shard_map/ppermute | solution.py:345
  107.3 0.8 shard_map.62
  108.1 3.1 %collective-permute-start.6 = (bf16[32,8192]{1,0:T(8,128)(2,1)}, bf16[32,8192]{1,0:T(8,128)(2,1)S(1)}, u32[]{:S(2)}, u32[]{:S(2)}) collective-permute-start(bf16[32,8192]{1,0:T(8,128)(2,1)} %get-tuple-element.39), channel_id=1, source_target_pairs={{256,264},{257,265},{258,266},{259,267},{260,268},{261,269},{262,2... | collective-permute-start | bytes 1572872 | tf_op jit(solution)/shard_map/ppermute | solution.py:345
  111.2 1.3 %collective-permute-start.7 = (bf16[32,8192]{1,0:T(8,128)(2,1)}, bf16[32,8192]{1,0:T(8,128)(2,1)S(1)}, u32[]{:S(2)}, u32[]{:S(2)}) collective-permute-start(bf16[32,8192]{1,0:T(8,128)(2,1)} %get-tuple-element.40), channel_id=1, source_target_pairs={{0,256},{1,257},{2,258},{3,259},{4,260},{5,261},{6,262},{7,263},{8... | collective-permute-start | bytes 1572872 | tf_op jit(solution)/shard_map/ppermute | solution.py:345
  112.5 0.0 collective-permute-done.8.partner_ref
  112.5 0.8 shard_map.64
  113.4 9.2 %collective-permute-done.6.crossed_own = bf16[32,8192]{1,0:T(8,128)(2,1)S(1)} collective-permute-done((bf16[32,8192]{1,0:T(8,128)(2,1)}, bf16[32,8192]{1,0:T(8,128)(2,1)S(1)}, u32[]{:S(2)}, u32[]{:S(2)}) %collective-permute-start.6) | collective-permute-done | bytes 524320 | tf_op jit(solution)/shard_map/ppermute | solution.py:345
  122.6 4.3 %collective-permute-done.7.crossed_got = bf16[32,8192]{1,0:T(8,128)(2,1)S(1)} collective-permute-done((bf16[32,8192]{1,0:T(8,128)(2,1)}, bf16[32,8192]{1,0:T(8,128)(2,1)S(1)}, u32[]{:S(2)}, u32[]{:S(2)}) %collective-permute-start.7) | collective-permute-done | bytes 524320 | tf_op jit(solution)/shard_map/ppermute | solution.py:345
  126.9 1.3 %shard_map.63 = (bf16[2,32,8192]{2,1,0:T(8,128)(2,1)}, bf16[2,32,8192]{2,1,0:T(8,128)(2,1)}) custom-call(s32[1]{0:T(128)} %bitcast.core_ref, s32[1]{0:T(128)} %bitcast.1.at_ref, bf16[32,8192]{1,0:T(8,128)(2,1)S(1)} %collective-permute-done.2.up_own, bf16[32,8192]{1,0:T(8,128)(2,1)S(1)} %collective-permute-done.3.down_own, ...), custom_call_target="tpu_custom_call" | custom-call | bytes 4194304 | tf_op jit(solution)/shard_map/pallas_call | solution.py:314
  (1 shorter events, 0.0 us)
Async XLA Ops:
  0.6 1.0 copy-start
  3.0 5.7 %copy-start.1 = (bf16[2,1,32,8192]{3,2,1,0:T(8,128)(2,1)S(1)}, bf16[2,1,32,8192]{3,2,1,0:T(8,128)(2,1)}, u32[]{:S(2)}) copy-start(bf16[2,1,32,8192]{3,2,1,0:T(8,128)(2,1)} %param.3) | copy-start | bytes 3145732
  3.0 31.4 %all-to-all-start = ((bf16[16,2,64,512]{3,2,1,0:T(8,128)(2,1)}), bf16[16,2,64,512]{3,2,1,0:T(8,128)(2,1)S(1)}, u32[]{:S(2)}, u32[]{:S(2)}) async-start(bf16[16,2,64,512]{3,2,1,0:T(8,128)(2,1)} %shard_map.58), calls=%async_computation | async-start | bytes 4194304 | tf_op jit(solution)/shard_map/all_to_all | solution.py:358
  10.1 4.6 %collective-permute-start = (bf16[2,32,8192]{2,1,0:T(8,128)(2,1)S(1)}, bf16[2,32,8192]{2,1,0:T(8,128)(2,1)S(1)}, u32[]{:S(2)}, u32[]{:S(2)}) collective-permute-start(bf16[2,32,8192]{2,1,0:T(8,128)(2,1)S(1)} %pad_maximum_fusion), channel_id=1, source_target_pairs={{0,1},{1,0},{2,3},{3,2},{4,5},{5,4},{6,7},{7,6},{8,9},{9,8},{10,11... | collective-permute-start | bytes 3145736 | tf_op jit(solution)/shard_map/ppermute | solution.py:360
  14.6 19.7 %copy-start.2 = (bf16[2,32,8192]{2,1,0:T(8,128)(2,1)}, bf16[2,32,8192]{2,1,0:T(8,128)(2,1)S(1)}, u32[]{:S(2)}) copy-start(bf16[2,32,8192]{2,1,0:T(8,128)(2,1)S(1)} %collective-permute-done.taken_ref) | copy-start | bytes 3145732
  38.2 34.7 %all-to-all-start.1 = ((bf16[16,2,64,512]{3,2,1,0:T(8,128)(2,1)}), bf16[16,2,64,512]{3,2,1,0:T(8,128)(2,1)}, u32[]{:S(2)}, u32[]{:S(2)}) async-start(bf16[16,2,64,512]{3,2,1,0:T(8,128)(2,1)} %get-tuple-element.23), calls=%async_computation.1 | async-start | bytes 4194304 | tf_op jit(solution)/shard_map/all_to_all | solution.py:364
  48.5 4.8 %collective-permute-start.1 = (bf16[2,32,8192]{2,1,0:T(8,128)(2,1)}, bf16[2,32,8192]{2,1,0:T(8,128)(2,1)S(1)}, u32[]{:S(2)}, u32[]{:S(2)}) collective-permute-start(bf16[2,32,8192]{2,1,0:T(8,128)(2,1)} %get-tuple-element.29), channel_id=1, source_target_pairs={{0,1},{1,0},{2,3},{3,2},{4,5},{5,4},{6,7},{7,6},{8,9},{9,8},{10,11... | collective-permute-start | bytes 3145736 | tf_op jit(solution)/shard_map/ppermute | solution.py:368
  53.3 31.0 %collective-permute-start.2 = (bf16[32,8192]{1,0:T(8,128)(2,1)}, bf16[32,8192]{1,0:T(8,128)(2,1)S(1)}, u32[]{:S(2)}, u32[]{:S(2)}) collective-permute-start(bf16[32,8192]{1,0:T(8,128)(2,1)} %get-tuple-element.30), channel_id=1, source_target_pairs={{0,16},{1,17},{2,18},{3,19},{4,20},{5,21},{6,22},{7,23},{8,24},{9,... | collective-permute-start | bytes 1572872 | tf_op jit(solution)/shard_map/ppermute | solution.py:345
  57.1 27.2 %collective-permute-start.3 = (bf16[32,8192]{1,0:T(8,128)(2,1)}, bf16[32,8192]{1,0:T(8,128)(2,1)S(1)}, u32[]{:S(2)}, u32[]{:S(2)}) collective-permute-start(bf16[32,8192]{1,0:T(8,128)(2,1)} %get-tuple-element.31), channel_id=1, source_target_pairs={{16,0},{17,1},{18,2},{19,3},{20,4},{21,5},{22,6},{23,7},{24,8},{25... | collective-permute-start | bytes 1572872 | tf_op jit(solution)/shard_map/ppermute | solution.py:345
  67.6 16.6 %collective-permute-start.4 = (bf16[32,8192]{1,0:T(8,128)(2,1)}, bf16[32,8192]{1,0:T(8,128)(2,1)S(1)}, u32[]{:S(2)}, u32[]{:S(2)}) collective-permute-start(bf16[32,8192]{1,0:T(8,128)(2,1)} %get-tuple-element.33), channel_id=1, source_target_pairs={{0,16},{1,17},{2,18},{3,19},{4,20},{5,21},{6,22},{7,23},{8,24},{9,... | collective-permute-start | bytes 1572872 | tf_op jit(solution)/shard_map/ppermute | solution.py:345
  69.0 38.3 %collective-permute-start.5 = (bf16[32,8192]{1,0:T(8,128)(2,1)}, bf16[32,8192]{1,0:T(8,128)(2,1)S(1)}, u32[]{:S(2)}, u32[]{:S(2)}) collective-permute-start(bf16[32,8192]{1,0:T(8,128)(2,1)} %get-tuple-element.34), channel_id=1, source_target_pairs={{16,0},{17,1},{18,2},{19,3},{20,4},{21,5},{22,6},{23,7},{24,8},{25... | collective-permute-start | bytes 1572872 | tf_op jit(solution)/shard_map/ppermute | solution.py:345
  74.8 37.7 %collective-permute-start.8 = (bf16[2,2,64,512]{3,2,1,0:T(8,128)(2,1)S(1)}, bf16[2,2,64,512]{3,2,1,0:T(8,128)(2,1)S(1)}, u32[]{:S(2)}, u32[]{:S(2)}) collective-permute-start(bf16[2,2,64,512]{3,2,1,0:T(8,128)(2,1)S(1)} %convert_element_type.11), channel_id=1, source_target_pairs={{0,496},{16,480},{32,464},{48,448},{64,432},{80,416},{96,400},{112... | collective-permute-start | bytes 786440 | tf_op jit(solution)/shard_map/ppermute | solution.py:378
  108.1 14.5 %collective-permute-start.6 = (bf16[32,8192]{1,0:T(8,128)(2,1)}, bf16[32,8192]{1,0:T(8,128)(2,1)S(1)}, u32[]{:S(2)}, u32[]{:S(2)}) collective-permute-start(bf16[32,8192]{1,0:T(8,128)(2,1)} %get-tuple-element.39), channel_id=1, source_target_pairs={{256,264},{257,265},{258,266},{259,267},{260,268},{261,269},{262,2... | collective-permute-start | bytes 1572872 | tf_op jit(solution)/shard_map/ppermute | solution.py:345
  111.2 15.7 %collective-permute-start.7 = (bf16[32,8192]{1,0:T(8,128)(2,1)}, bf16[32,8192]{1,0:T(8,128)(2,1)S(1)}, u32[]{:S(2)}, u32[]{:S(2)}) collective-permute-start(bf16[32,8192]{1,0:T(8,128)(2,1)} %get-tuple-element.40), channel_id=1, source_target_pairs={{0,256},{1,257},{2,258},{3,259},{4,260},{5,261},{6,262},{7,263},{8... | collective-permute-start | bytes 1572872 | tf_op jit(solution)/shard_map/ppermute | solution.py:345

commit v5 on v4

--- a/solution.py
+++ b/solution.py
@@ -126,8 +126,8 @@
 
 
 def outputs_kernel(
-    core_ref, x_ref, g_ref, taken_ref, w_ref, hidden_ref, scaled_ref, back_ref, up_ref, down_ref, send_ref, xs, gs, ms,
-    loads, stores
+    count, core_ref, at_ref, x_ref, g_ref, taken_ref, w_ref, hidden_ref, scaled_ref, back_ref, keep_ref, edge_ref,
+    send_ref, xs, gs, ms, loads, stores, edge_sem
 ):
     core = core_ref[0]
     is_down = core == 0
@@ -153,25 +153,31 @@
             j = i // per
             cols = pl.ds(j * (model // chunks), model // chunks)
             for copy in (
-                pltpu.make_async_copy(ms.at[0, own, cols], up_ref.at[:, cols], stores.at[j, 0]),
-                pltpu.make_async_copy(ms.at[1, own, cols], down_ref.at[:, cols], stores.at[j, 1]),
+                pltpu.make_async_copy(ms.at[0, own, cols], keep_ref.at[0, :, cols], stores.at[j, 0]),
+                pltpu.make_async_copy(ms.at[1, own, cols], keep_ref.at[1, :, cols], stores.at[j, 1]),
                 pltpu.make_async_copy(ms.at[0, others, cols], send_ref.at[0, :, cols], stores.at[j, 2]),
                 pltpu.make_async_copy(ms.at[1, others, cols], send_ref.at[1, :, cols], stores.at[j, 3]),
             ):
                 copy.start()
                 stored.append(copy)
+    for way, position in ((0, count // 2 - 1), (1, count // 2)):
+        @pl.when(at_ref[0] == position)
+        def _():
+            copy = pltpu.make_async_copy(ms.at[way, own], edge_ref, edge_sem)
+            copy.start()
+            copy.wait()
     for copy in stored:
         copy.wait()
 
 
-def outputs(core, x, g, taken, w, hidden, scaled, back):
+def outputs(count, core, section, x, g, taken, w, hidden, scaled, back):
     tokens, model = x.shape[1:]
-    one = pltpu.HBM((tokens, model), x.dtype)
+    pair = pltpu.HBM((2, tokens, model), x.dtype)
     both = pltpu.VMEM((2 * tokens, model), x.dtype)
     return pl.pallas_call(
-        outputs_kernel,
-        out_shape=(one, one, pltpu.HBM((2, tokens, model), x.dtype)),
-        in_specs=[SCALARS] + [ANYWHERE] * 3 + [WHOLE] * 4,
+        functools.partial(outputs_kernel, count),
+        out_shape=(pair, pltpu.HBM((tokens, model), x.dtype), pair),
+        in_specs=[SCALARS] * 2 + [ANYWHERE] * 3 + [WHOLE] * 4,
         out_specs=(ANYWHERE,) * 3,
         scratch_shapes=[
             both,
@@ -179,77 +185,47 @@
             pltpu.VMEM((2, 2 * tokens, model), x.dtype),
             pltpu.SemaphoreType.DMA((4, 4)),
             pltpu.SemaphoreType.DMA((4, 4)),
+            pltpu.SemaphoreType.DMA,
         ],
         compiler_params=PARAMS,
         cost_estimate=pl.CostEstimate(flops=4 * tokens * w.size, bytes_accessed=8 << 20, transcendentals=0),
-    )(core, x, g, taken, w, hidden, scaled, back)
-
-
-def split_kernel(both_ref, first_ref, second_ref, sems):
+    )(core, section, x, g, taken, w, hidden, scaled, back)
+
+
+def pack_kernel(count, at_ref, keep_ref, got_ref, up_ref, down_ref, edge_ref, sems):
     copies = [
-        pltpu.make_async_copy(both_ref.at[0], first_ref, sems.at[0]),
-        pltpu.make_async_copy(both_ref.at[1], second_ref, sems.at[1]),
+        pltpu.make_async_copy(keep_ref.at[0], up_ref.at[0], sems.at[0]),
+        pltpu.make_async_copy(got_ref.at[0], up_ref.at[1], sems.at[1]),
+        pltpu.make_async_copy(keep_ref.at[1], down_ref.at[0], sems.at[2]),
+        pltpu.make_async_copy(got_ref.at[1], down_ref.at[1], sems.at[3]),
     ]
     for copy in copies:
         copy.start()
+    for way, position in ((0, count // 2 - 1), (1, count // 2)):
+        @pl.when(at_ref[0] == position)
+        def _():
+            copy = pltpu.make_async_copy(got_ref.at[way], edge_ref, sems.at[4])
+            copy.start()
+            copy.wait()
     for copy in copies:
         copy.wait()
 
 
-def split(both):
-    one = pltpu.HBM(both.shape[1:], both.dtype)
-    return pl.pallas_call(
-        split_kernel,
-        out_shape=(one, one),
-        in_specs=[ANYWHERE],
-        out_specs=(ANYWHERE,) * 2,
-        scratch_shapes=[pltpu.SemaphoreType.DMA((2,))],
-        compiler_params=PARAMS,
-        cost_estimate=pl.CostEstimate(flops=0, bytes_accessed=4 * both.size, transcendentals=0),
-    )(both)
-
-
-def crossing_kernel(count, at_ref, up_own, down_own, up_got, down_got, own_out, got_out, sems):
-    section = at_ref[0]
-    half = count // 2
-
-    def copy(src, dst, i):
-        moving = pltpu.make_async_copy(src, dst, sems.at[i])
-        moving.start()
-        moving.wait()
-
-    @pl.when(section == half)
-    def _():
-        copy(up_own, own_out, 0)
-
-    @pl.when(section == half - 1)
-    def _():
-        copy(down_own, own_out, 0)
-
-    @pl.when(section == 0)
-    def _():
-        copy(up_got, got_out, 1)
-
-    @pl.when(section == count - 1)
-    def _():
-        copy(down_got, got_out, 1)
-
-
-def crossing(count, section, *moved_parts):
-    one = pltpu.HBM(moved_parts[0].shape, moved_parts[0].dtype)
-    return pl.pallas_call(
-        functools.partial(crossing_kernel, count),
-        out_shape=(one, one),
-        in_specs=[SCALARS] + [ANYWHERE] * 4,
-        out_specs=(ANYWHERE,) * 2,
-        scratch_shapes=[pltpu.SemaphoreType.DMA((2,))],
-        compiler_params=PARAMS,
-        cost_estimate=pl.CostEstimate(flops=0, bytes_accessed=4 * moved_parts[0].size, transcendentals=0),
-    )(section, *moved_parts)
+def pack(count, section, keep, got):
+    pair = pltpu.HBM(keep.shape, keep.dtype)
+    return pl.pallas_call(
+        functools.partial(pack_kernel, count),
+        out_shape=(pair, pair, pltpu.HBM(keep.shape[1:], keep.dtype)),
+        in_specs=[SCALARS] + [ANYWHERE] * 2,
+        out_specs=(ANYWHERE,) * 3,
+        scratch_shapes=[pltpu.SemaphoreType.DMA((5,))],
+        compiler_params=PARAMS,
+        cost_estimate=pl.CostEstimate(flops=0, bytes_accessed=8 * keep.size, transcendentals=0),
+    )(section, keep, got)
 
 
 def finish_kernel(
-    count, core_ref, at_ref, up_own, down_own, up_got, down_got, crossed_own, crossed_got, next_ref, prev_ref, sems
+    count, core_ref, at_ref, up_ref, down_ref, crossed_own, crossed_got, next_ref, prev_ref, sems
 ):
     core, section = core_ref[0], at_ref[0]
     half = count // 2
@@ -269,57 +245,32 @@
         (prev_ref.at[1], next_ref.at[0]),
         (next_ref.at[1], prev_ref.at[0]),
     )
-
-    @pl.when(section == half)
-    def _():
-        put(0, crossed_own, *places[0])
-        put(2, crossed_got, *places[2])
-
-    @pl.when(section != half)
-    def _():
-        put(0, up_own, *places[0])
-
-        @pl.when(section == 0)
-        def _():
-            put(2, up_own, *places[2])
-
-        @pl.when(section != 0)
-        def _():
-            put(2, up_got, *places[2])
-
-    @pl.when(section == half - 1)
-    def _():
-        put(1, crossed_own, *places[1])
-        put(3, crossed_got, *places[3])
-
-    @pl.when(section != half - 1)
-    def _():
-        put(1, down_own, *places[1])
-
-        @pl.when(section == count - 1)
-        def _():
-            put(3, down_own, *places[3])
-
-        @pl.when(section != count - 1)
-        def _():
-            put(3, down_got, *places[3])
+    for way, position, arrived in ((0, half, up_ref), (1, half - 1, down_ref)):
+        @pl.when(section == position)
+        def _():
+            put(way, crossed_own, *places[way])
+            put(way + 2, crossed_got, *places[way + 2])
+
+        @pl.when(section != position)
+        def _():
+            put(way, arrived.at[0], *places[way])
+            put(way + 2, arrived.at[1], *places[way + 2])
 
     for i in range(4):
-        pltpu.make_async_copy(up_own, next_ref.at[0], sems.at[i]).wait()
-
-
-def finish(count, core, section, *moved_parts):
-    tokens, model = moved_parts[0].shape
-    both = pltpu.HBM((2, tokens, model), moved_parts[0].dtype)
+        pltpu.make_async_copy(crossed_own, next_ref.at[0], sems.at[i]).wait()
+
+
+def finish(count, core, section, up, down, crossed_own, crossed_got):
+    pair = pltpu.HBM(up.shape, up.dtype)
     return pl.pallas_call(
         functools.partial(finish_kernel, count),
-        out_shape=(both, both),
-        in_specs=[SCALARS] * 2 + [ANYWHERE] * 6,
+        out_shape=(pair, pair),
+        in_specs=[SCALARS] * 2 + [ANYWHERE] * 4,
         out_specs=(ANYWHERE,) * 2,
         scratch_shapes=[pltpu.SemaphoreType.DMA((4,))],
         compiler_params=PARAMS,
-        cost_estimate=pl.CostEstimate(flops=0, bytes_accessed=16 * tokens * model, transcendentals=0),
-    )(core, section, *moved_parts)
+        cost_estimate=pl.CostEstimate(flops=0, bytes_accessed=8 * up.size, transcendentals=0),
+    )(core, section, up, down, crossed_own, crossed_got)
 
 
 def add_kernel(sums_ref, partner_ref, out_ref):
@@ -334,7 +285,7 @@
         in_specs=[WHOLE] * 2,
         out_specs=WHOLE,
         compiler_params=PARAMS,
-        cost_estimate=pl.CostEstimate(flops=40_000_000_000, bytes_accessed=2 << 20, transcendentals=0),
+        cost_estimate=pl.CostEstimate(flops=4_000_000_000, bytes_accessed=2 << 20, transcendentals=0),
     )(sums, partner)
 
 
@@ -364,27 +315,21 @@
     terms = lax.all_to_all(parts, "dp", 0, 0, tiled=True)
     sums = jnp.sum(terms.reshape((n_dp // 2, 2) + terms.shape[1:]).astype(F32), axis=0)
 
-    up_own, down_own, send = outputs(core, x, g, taken, gathered, hidden, scaled, back)
+    keep, edge_own, send = outputs(count, core, section, x, g, taken, gathered, hidden, scaled, back)
     got = lax.ppermute(send, "dp", swap)
-    up_own, down_own, got = lax.optimization_barrier((up_own, down_own, got))
-    up_got, down_got = split(got)
-    ups = [(i, i + 1) for i in range(count - 1) if i != half - 1]
-    downs = [(i, i - 1) for i in range(1, count) if i != half]
-    up_own = moved(up_own, ups, n_dp, [(half - 1, half)])
-    down_own = moved(down_own, downs, n_dp, [(half, half - 1)])
-    up_got = moved(up_got, ups + [(half - 1, 0)], n_dp)
-    down_got = moved(down_got, downs + [(half, count - 1)], n_dp)
+    up, down, edge_got = pack(count, section, keep, got)
+    near_own = moved(edge_own, [], n_dp, [(half - 1, half), (half, half - 1)])
+    near_got = moved(edge_got, [(half - 1, 0), (half, count - 1)], n_dp)
+    up = moved(up, [(i, i + 1) for i in range(count - 1) if i != half - 1], n_dp)
+    down = moved(down, [(i, i - 1) for i in range(1, count) if i != half], n_dp)
+
     narrow = sums.astype(jnp.bfloat16)
     partner = lax.ppermute(narrow, "section", [(i, count - 1 - i) for i in range(count)])
-    narrow, up_own, down_own, up_got, down_got = lax.optimization_barrier((narrow, up_own, down_own, up_got, down_got))
-
-    cross_own, cross_got = crossing(count, section, up_own, down_own, up_got, down_got)
-    crossed_own = moved(cross_own, [], n_dp, [(half, half), (half - 1, half - 1)])
-    crossed_got = moved(cross_got, [(0, half), (count - 1, half - 1)], n_dp)
+    narrow, near_own, near_got = lax.optimization_barrier((narrow, near_own, near_got))
+    crossed_own = moved(near_own, [], n_dp, [(half, half), (half - 1, half - 1)])
+    crossed_got = moved(near_got, [(0, half), (count - 1, half - 1)], n_dp)
     summed = add_mirrored(sums, partner)
-    next_inputs, prev_grads = finish(
-        count, core, section, up_own, down_own, up_got, down_got, crossed_own, crossed_got
-    )
+    next_inputs, prev_grads = finish(count, core, section, up, down, crossed_own, crossed_got)
     return (next_inputs[:, None], prev_grads[:, None], summed[:, None])
 
 

time: 129 us -> 118 us (0.915)
  the two profiles are of different devices: /device:TPU:22 before, /device:TPU:226 now
where the time goes in v5:
time: 118 us
  waiting for transfers between devices  67.6 us (57%)
  starting transfers between devices  31.4 us (27%)
  Pallas kernels  12.1 us (10%)
  other arithmetic  3.39 us (3%)
  local copies, waits for them, and re-layouts  2.18 us (2%)
    ppermute x1, waiting for transfers between devices, shards(): lax.ppermute(narrow, 'section', [(i, count - 1 - i) for i in range(count)])  30.4 us
    all_to_all x1, waiting for transfers between devices, shards(): lax.all_to_all(spread(adapters[:, 0], n_dp), 'dp', 0, 0, tiled=True)  22.6 us
    all_to_all x1, waiting for transfers between devices, shards(): terms = lax.all_to_all(parts, 'dp', 0, 0, tiled=True)  9.96 us
    ppermute x6, starting transfers between devices, moved(): return lax.ppermute(value, ('section', 'dp'), routes)  9.75 us
    ppermute x1, starting transfers between devices, shards(): lax.ppermute(narrow, 'section', [(i, count - 1 - i) for i in range(count)])  7.37 us
    all_to_all x1, starting transfers between devices, shards(): lax.all_to_all(spread(adapters[:, 0], n_dp), 'dp', 0, 0, tiled=True)  6 us
    all_to_all x1, starting transfers between devices, shards(): terms = lax.all_to_all(parts, 'dp', 0, 0, tiled=True)  4.34 us
    pallas_call x1, Pallas kernels, partials(): pl.pallas_call(partials_kernel, out_shape=(pltpu.HBM(w.shape, w.dtype), i...  3.76 us
  transfers between devices with their start and end apart: 11, of which 5 were waited for; matrix products, arithmetic and copies ran while one was open for 3% of the time, Pallas kernels for 5%

profile of v5, /device:TPU:226, one launch (start us, length us, event | category | flops | bytes accessed | tf_op | source)
XLA Modules:
  0.0 117.5 jit_solution(1529092128861457743)
XLA Ops:
  0.6 0.0 copy-start.1
  0.6 0.9 copy-done.1
  1.6 1.4 %shard_map.58 = bf16[16,2,64,512]{3,2,1,0:T(8,128)(2,1)} custom-call(bf16[2,2,64,512]{3,2,1,0:T(8,128)(2,1)S(1)} %bitcast.20), custom_call_target="tpu_custom_call" | custom-call | bytes 2097152 | tf_op jit(solution)/shard_map/pallas_call | solution.py:30
  3.0 0.0 copy-start.2
  3.0 6.0 %all-to-all-start = ((bf16[16,2,64,512]{3,2,1,0:T(8,128)(2,1)}), bf16[16,2,64,512]{3,2,1,0:T(8,128)(2,1)S(1)}, u32[]{:S(2)}, u32[]{:S(2)}) async-start(bf16[16,2,64,512]{3,2,1,0:T(8,128)(2,1)} %shard_map.58), calls=%async_computation | async-start | bytes 4194304 | tf_op jit(solution)/shard_map/all_to_all | solution.py:309
  9.0 0.0 copy-done.2
  9.0 1.3 %select_bitcast_fusion = (bf16[1,32,8192]{2,1,0:T(8,128)(2,1)S(1)}, bf16[1,32,8192]{2,1,0:T(8,128)(2,1)S(1)}) fusion(bf16[2,1,32,8192]{3,2,1,0:T(8,128)(2,1)} %param.4, pred[]{:T(512)S(6)} %eq.5, bf16[2,1,32,8192]{3,2,1,0:T(8,128)(2,1)S(1)} %copy-done.2), kind=kLoop, calls=%fused_computation.2 | loop fusion | flops 524288 | bytes 3145729 | tf_op jit(solution)/shard_map/jit(_where)/select_n | solution.py:310
  10.3 0.1 pad_maximum_fusion
  10.4 2.1 %collective-permute-start = (bf16[2,32,8192]{2,1,0:T(8,128)(2,1)S(1)}, bf16[2,32,8192]{2,1,0:T(8,128)(2,1)S(1)}, u32[]{:S(2)}, u32[]{:S(2)}) collective-permute-start(bf16[2,32,8192]{2,1,0:T(8,128)(2,1)S(1)} %pad_maximum_fusion), channel_id=1, source_target_pairs={{0,1},{1,0},{2,3},{3,2},{4,5},{5,4},{6,7},{7,6},{8,9},{9,8},{10,11... | collective-permute-start | bytes 3145736 | tf_op jit(solution)/shard_map/ppermute | solution.py:311
  12.5 2.5 %collective-permute-done.taken_ref = bf16[2,32,8192]{2,1,0:T(8,128)(2,1)S(1)} collective-permute-done((bf16[2,32,8192]{2,1,0:T(8,128)(2,1)S(1)}, bf16[2,32,8192]{2,1,0:T(8,128)(2,1)S(1)}, u32[]{:S(2)}, u32[]{:S(2)}) %collective-permute-start) | collective-permute-done | bytes 1048608 | tf_op jit(solution)/shard_map/ppermute | solution.py:311
  15.0 0.0 copy-start.3
  15.0 22.6 %all-to-all-done.w_ref = bf16[16,2,64,512]{3,2,1,0:T(8,128)(2,1)S(1)} async-done(((bf16[16,2,64,512]{3,2,1,0:T(8,128)(2,1)}), bf16[16,2,64,512]{3,2,1,0:T(8,128)(2,1)S(1)}, u32[]{:S(2)}, u32[]{:S(2)}) %all-to-all-start) | async-done | bytes 2097184 | tf_op jit(solution)/shard_map/all_to_all | solution.py:309
  37.6 0.0 copy-done.3
  37.6 3.8 %shard_map.59 = (bf16[16,2,64,512]{3,2,1,0:T(8,128)(2,1)}, bf16[64,64]{1,0:T(8,128)(2,1)S(1)}, bf16[64,64]{1,0:T(8,128)(2,1)S(1)}, f32[64,128]{1,0:T(8,128)S(1)}) custom-call(s32[1]{0:T(128)} %bitcast.core_ref, bf16[2,32,8192]{2,1,0:T(8,128)(2,1)} %bitcast.21, bf16[2,32,8192]{2,1,0:T(8,128)(2,1)} %bitcast.23, bf16[2,32,8192]{2,1,0:T(8,128)(2,1)} %copy-done.3, ...), custom_call_target="tpu_custom_call" | custom-call | flops 268435456 | bytes 8388608 | tf_op jit(solution)/shard_map/pallas_call | solution.py:111
  41.4 4.3 %all-to-all-start.1 = ((bf16[16,2,64,512]{3,2,1,0:T(8,128)(2,1)}), bf16[16,2,64,512]{3,2,1,0:T(8,128)(2,1)}, u32[]{:S(2)}, u32[]{:S(2)}) async-start(bf16[16,2,64,512]{3,2,1,0:T(8,128)(2,1)} %get-tuple-element.24), calls=%async_computation.1 | async-start | bytes 4194304 | tf_op jit(solution)/shard_map/all_to_all | solution.py:315
  45.8 3.4 %shard_map.60 = (bf16[2,32,8192]{2,1,0:T(8,128)(2,1)}, bf16[32,8192]{1,0:T(8,128)(2,1)}, bf16[2,32,8192]{2,1,0:T(8,128)(2,1)}) custom-call(s32[1]{0:T(128)} %bitcast.core_ref, s32[1]{0:T(128)} %bitcast.1.at_ref, bf16[2,32,8192]{2,1,0:T(8,128)(2,1)} %bitcast.22, bf16[2,32,8192]{2,1,0:T(8,128)(2,1)} %bitcast.24, bf16[2,32,8192]{2,1,0:T(8,128)(2,1)} %copy-done.3, ...), custom_call_target="tpu_custom_call" | custom-call | flops 134217728 | bytes 8388608 | tf_op jit(solution)/shard_map/pallas_call | solution.py:177
  49.2 1.9 %collective-permute-start.1 = (bf16[2,32,8192]{2,1,0:T(8,128)(2,1)}, bf16[2,32,8192]{2,1,0:T(8,128)(2,1)S(1)}, u32[]{:S(2)}, u32[]{:S(2)}) collective-permute-start(bf16[2,32,8192]{2,1,0:T(8,128)(2,1)} %get-tuple-element.21), channel_id=1, source_target_pairs={{0,1},{1,0},{2,3},{3,2},{4,5},{5,4},{6,7},{7,6},{8,9},{9,8},{10,11... | collective-permute-start | bytes 3145736 | tf_op jit(solution)/shard_map/ppermute | solution.py:319
  51.1 0.7 collective-permute-start.4
  51.8 2.1 %collective-permute-done.1.got_ref = bf16[2,32,8192]{2,1,0:T(8,128)(2,1)S(1)} collective-permute-done((bf16[2,32,8192]{2,1,0:T(8,128)(2,1)}, bf16[2,32,8192]{2,1,0:T(8,128)(2,1)S(1)}, u32[]{:S(2)}, u32[]{:S(2)}) %collective-permute-start.1) | collective-permute-done | bytes 1048608 | tf_op jit(solution)/shard_map/ppermute | solution.py:319
  53.9 0.0 copy-start
  53.9 1.2 %copy-done = bf16[2,32,8192]{2,1,0:T(8,128)(2,1)S(1)} copy-done((bf16[2,32,8192]{2,1,0:T(8,128)(2,1)S(1)}, bf16[2,32,8192]{2,1,0:T(8,128)(2,1)}, u32[]{:S(2)}) %copy-start) | copy-done | bytes 1048600
  55.2 1.4 %shard_map.61 = (bf16[2,32,8192]{2,1,0:T(8,128)(2,1)}, bf16[2,32,8192]{2,1,0:T(8,128)(2,1)}, bf16[32,8192]{1,0:T(8,128)(2,1)}) custom-call(s32[1]{0:T(128)} %bitcast.1.at_ref, bf16[2,32,8192]{2,1,0:T(8,128)(2,1)S(1)} %copy-done, bf16[2,32,8192]{2,1,0:T(8,128)(2,1)S(1)} %collective-permute-done.1.got_ref), custom_call_target="tpu_custom_call" | custom-call | bytes 4194304 | tf_op jit(solution)/shard_map/pallas_call | solution.py:216
  56.5 0.7 collective-permute-start.5
  57.2 5.1 %collective-permute-start.2 = (bf16[2,32,8192]{2,1,0:T(8,128)(2,1)}, bf16[2,32,8192]{2,1,0:T(8,128)(2,1)S(1)}, u32[]{:S(2)}, u32[]{:S(2)}) collective-permute-start(bf16[2,32,8192]{2,1,0:T(8,128)(2,1)} %get-tuple-element.22), channel_id=1, source_target_pairs={{0,16},{1,17},{2,18},{3,19},{4,20},{5,21},{6,22},{7,23},{8,24},{9,... | collective-permute-start | bytes 3145736 | tf_op jit(solution)/shard_map/ppermute | solution.py:296
  62.3 1.9 %collective-permute-start.3 = (bf16[2,32,8192]{2,1,0:T(8,128)(2,1)}, bf16[2,32,8192]{2,1,0:T(8,128)(2,1)S(1)}, u32[]{:S(2)}, u32[]{:S(2)}) collective-permute-start(bf16[2,32,8192]{2,1,0:T(8,128)(2,1)} %get-tuple-element.23), channel_id=1, source_target_pairs={{16,0},{17,1},{18,2},{19,3},{20,4},{21,5},{22,6},{23,7},{24,8},{25... | collective-permute-start | bytes 3145736 | tf_op jit(solution)/shard_map/ppermute | solution.py:296
  64.2 10.0 %all-to-all-done.1 = bf16[16,2,64,512]{3,2,1,0:T(8,128)(2,1)} async-done(((bf16[16,2,64,512]{3,2,1,0:T(8,128)(2,1)}), bf16[16,2,64,512]{3,2,1,0:T(8,128)(2,1)}, u32[]{:S(2)}, u32[]{:S(2)}) %all-to-all-start.1) | async-done | bytes 2097184 | tf_op jit(solution)/shard_map/all_to_all | solution.py:315
  74.2 2.0 %convert_reduce_fusion.sums_ref = f32[2,2,64,512]{3,2,1,0:T(8,128)S(1)} fusion(bf16[8,2,2,64,512]{4,3,2,1,0:T(8,128)(2,1)} %bitcast.14), kind=kLoop, calls=%fused_computation | loop fusion | flops 1966080 | bytes 2621440 | tf_op jit(solution)/shard_map/reduce_sum | solution.py:316
  76.2 7.4 %collective-permute-start.8 = (bf16[2,2,64,512]{3,2,1,0:T(8,128)(2,1)S(1)}, bf16[2,2,64,512]{3,2,1,0:T(8,128)(2,1)S(1)}, u32[]{:S(2)}, u32[]{:S(2)}) collective-permute-start(bf16[2,2,64,512]{3,2,1,0:T(8,128)(2,1)S(1)} %convert_element_type.11), channel_id=1, source_target_pairs={{0,496},{16,480},{32,464},{48,448},{64,432},{80,416},{96,400},{112... | collective-permute-start | bytes 786440 | tf_op jit(solution)/shard_map/ppermute | solution.py:327
  83.5 0.0 collective-permute-done.4
  83.6 0.0 collective-permute-done.5
  83.6 0.7 collective-permute-start.6
  84.3 0.7 collective-permute-start.7
  85.0 30.4 %collective-permute-done.8.partner_ref = bf16[2,2,64,512]{3,2,1,0:T(8,128)(2,1)S(1)} collective-permute-done((bf16[2,2,64,512]{3,2,1,0:T(8,128)(2,1)S(1)}, bf16[2,2,64,512]{3,2,1,0:T(8,128)(2,1)S(1)}, u32[]{:S(2)}, u32[]{:S(2)}) %collective-permute-start.8) | collective-permute-done | bytes 262176 | tf_op jit(solution)/shard_map/ppermute | solution.py:327
  115.3 0.8 shard_map.63
  116.2 0.0 collective-permute-done.2.up_ref
  116.2 0.0 collective-permute-done.3.down_ref
  116.2 0.0 collective-permute-done.6.crossed_own
  116.2 0.0 collective-permute-done.7.crossed_got
  116.2 1.4 %shard_map.62 = (bf16[2,32,8192]{2,1,0:T(8,128)(2,1)}, bf16[2,32,8192]{2,1,0:T(8,128)(2,1)}) custom-call(s32[1]{0:T(128)} %bitcast.core_ref, s32[1]{0:T(128)} %bitcast.1.at_ref, bf16[2,32,8192]{2,1,0:T(8,128)(2,1)S(1)} %collective-permute-done.2.up_ref, bf16[2,32,8192]{2,1,0:T(8,128)(2,1)S(1)} %collective-permute-done.3.down_ref, ...), custom_call_target="tpu_custom_call" | custom-call | bytes 4194304 | tf_op jit(solution)/shard_map/pallas_call | solution.py:265
  (1 shorter events, 0.0 us)
Async XLA Ops:
  0.6 1.0 copy-start.1
  3.0 6.0 %copy-start.2 = (bf16[2,1,32,8192]{3,2,1,0:T(8,128)(2,1)S(1)}, bf16[2,1,32,8192]{3,2,1,0:T(8,128)(2,1)}, u32[]{:S(2)}) copy-start(bf16[2,1,32,8192]{3,2,1,0:T(8,128)(2,1)} %param.3) | copy-start | bytes 3145732
  3.0 34.6 %all-to-all-start = ((bf16[16,2,64,512]{3,2,1,0:T(8,128)(2,1)}), bf16[16,2,64,512]{3,2,1,0:T(8,128)(2,1)S(1)}, u32[]{:S(2)}, u32[]{:S(2)}) async-start(bf16[16,2,64,512]{3,2,1,0:T(8,128)(2,1)} %shard_map.58), calls=%async_computation | async-start | bytes 4194304 | tf_op jit(solution)/shard_map/all_to_all | solution.py:309
  10.4 4.6 %collective-permute-start = (bf16[2,32,8192]{2,1,0:T(8,128)(2,1)S(1)}, bf16[2,32,8192]{2,1,0:T(8,128)(2,1)S(1)}, u32[]{:S(2)}, u32[]{:S(2)}) collective-permute-start(bf16[2,32,8192]{2,1,0:T(8,128)(2,1)S(1)} %pad_maximum_fusion), channel_id=1, source_target_pairs={{0,1},{1,0},{2,3},{3,2},{4,5},{5,4},{6,7},{7,6},{8,9},{9,8},{10,11... | collective-permute-start | bytes 3145736 | tf_op jit(solution)/shard_map/ppermute | solution.py:311
  15.0 22.7 %copy-start.3 = (bf16[2,32,8192]{2,1,0:T(8,128)(2,1)}, bf16[2,32,8192]{2,1,0:T(8,128)(2,1)S(1)}, u32[]{:S(2)}) copy-start(bf16[2,32,8192]{2,1,0:T(8,128)(2,1)S(1)} %collective-permute-done.taken_ref) | copy-start | bytes 3145732
  41.4 32.8 %all-to-all-start.1 = ((bf16[16,2,64,512]{3,2,1,0:T(8,128)(2,1)}), bf16[16,2,64,512]{3,2,1,0:T(8,128)(2,1)}, u32[]{:S(2)}, u32[]{:S(2)}) async-start(bf16[16,2,64,512]{3,2,1,0:T(8,128)(2,1)} %get-tuple-element.24), calls=%async_computation.1 | async-start | bytes 4194304 | tf_op jit(solution)/shard_map/all_to_all | solution.py:315
  49.2 4.8 %collective-permute-start.1 = (bf16[2,32,8192]{2,1,0:T(8,128)(2,1)}, bf16[2,32,8192]{2,1,0:T(8,128)(2,1)S(1)}, u32[]{:S(2)}, u32[]{:S(2)}) collective-permute-start(bf16[2,32,8192]{2,1,0:T(8,128)(2,1)} %get-tuple-element.21), channel_id=1, source_target_pairs={{0,1},{1,0},{2,3},{3,2},{4,5},{5,4},{6,7},{7,6},{8,9},{9,8},{10,11... | collective-permute-start | bytes 3145736 | tf_op jit(solution)/shard_map/ppermute | solution.py:319
  51.1 32.4 %collective-permute-start.4 = (bf16[32,8192]{1,0:T(8,128)(2,1)}, bf16[32,8192]{1,0:T(8,128)(2,1)S(1)}, u32[]{:S(2)}, u32[]{:S(2)}) collective-permute-start(bf16[32,8192]{1,0:T(8,128)(2,1)} %get-tuple-element.25), channel_id=1, source_target_pairs={{240,264},{241,265},{242,266},{243,267},{244,268},{245,269},{246,2... | collective-permute-start | bytes 1572872 | tf_op jit(solution)/shard_map/ppermute | solution.py:296
  53.9 1.2 %copy-start = (bf16[2,32,8192]{2,1,0:T(8,128)(2,1)S(1)}, bf16[2,32,8192]{2,1,0:T(8,128)(2,1)}, u32[]{:S(2)}) copy-start(bf16[2,32,8192]{2,1,0:T(8,128)(2,1)} %get-tuple-element.20.keep_ref) | copy-start | bytes 3145732
  56.5 27.0 %collective-permute-start.5 = (bf16[32,8192]{1,0:T(8,128)(2,1)}, bf16[32,8192]{1,0:T(8,128)(2,1)S(1)}, u32[]{:S(2)}, u32[]{:S(2)}) collective-permute-start(bf16[32,8192]{1,0:T(8,128)(2,1)} %get-tuple-element.26), channel_id=1, source_target_pairs={{240,0},{241,1},{242,2},{243,3},{244,4},{245,5},{246,6},{247,7},{2... | collective-permute-start | bytes 1572872 | tf_op jit(solution)/shard_map/ppermute | solution.py:296
  57.2 58.9 %collective-permute-start.2 = (bf16[2,32,8192]{2,1,0:T(8,128)(2,1)}, bf16[2,32,8192]{2,1,0:T(8,128)(2,1)S(1)}, u32[]{:S(2)}, u32[]{:S(2)}) collective-permute-start(bf16[2,32,8192]{2,1,0:T(8,128)(2,1)} %get-tuple-element.22), channel_id=1, source_target_pairs={{0,16},{1,17},{2,18},{3,19},{4,20},{5,21},{6,22},{7,23},{8,24},{9,... | collective-permute-start | bytes 3145736 | tf_op jit(solution)/shard_map/ppermute | solution.py:296
  62.3 53.9 %collective-permute-start.3 = (bf16[2,32,8192]{2,1,0:T(8,128)(2,1)}, bf16[2,32,8192]{2,1,0:T(8,128)(2,1)S(1)}, u32[]{:S(2)}, u32[]{:S(2)}) collective-permute-start(bf16[2,32,8192]{2,1,0:T(8,128)(2,1)} %get-tuple-element.23), channel_id=1, source_target_pairs={{16,0},{17,1},{18,2},{19,3},{20,4},{21,5},{22,6},{23,7},{24,8},{25... | collective-permute-start | bytes 3145736 | tf_op jit(solution)/shard_map/ppermute | solution.py:296
  76.2 39.2 %collective-permute-start.8 = (bf16[2,2,64,512]{3,2,1,0:T(8,128)(2,1)S(1)}, bf16[2,2,64,512]{3,2,1,0:T(8,128)(2,1)S(1)}, u32[]{:S(2)}, u32[]{:S(2)}) collective-permute-start(bf16[2,2,64,512]{3,2,1,0:T(8,128)(2,1)S(1)} %convert_element_type.11), channel_id=1, source_target_pairs={{0,496},{16,480},{32,464},{48,448},{64,432},{80,416},{96,400},{112... | collective-permute-start | bytes 786440 | tf_op jit(solution)/shard_map/ppermute | solution.py:327
  83.6 32.6 %collective-permute-start.6 = (bf16[32,8192]{1,0:T(8,128)(2,1)S(1)}, bf16[32,8192]{1,0:T(8,128)(2,1)S(1)}, u32[]{:S(2)}, u32[]{:S(2)}) collective-permute-start(bf16[32,8192]{1,0:T(8,128)(2,1)S(1)} %collective-permute-done.4), channel_id=1, source_target_pairs={{256,264},{257,265},{258,266},{259,267},{260,268},{261,269},{262,2... | collective-permute-start | bytes 1572872 | tf_op jit(solution)/shard_map/ppermute | solution.py:296
  84.3 31.9 %collective-permute-start.7 = (bf16[32,8192]{1,0:T(8,128)(2,1)S(1)}, bf16[32,8192]{1,0:T(8,128)(2,1)S(1)}, u32[]{:S(2)}, u32[]{:S(2)}) collective-permute-start(bf16[32,8192]{1,0:T(8,128)(2,1)S(1)} %collective-permute-done.5), channel_id=1, source_target_pairs={{0,256},{1,257},{2,258},{3,259},{4,260},{5,261},{6,262},{7,263},{8... | collective-permute-start | bytes 1572872 | tf_op jit(solution)/shard_map/ppermute | solution.py:296

commit v6 on v5

v6 whole, which is shorter than its diff:
```python
import functools

import jax
import jax.numpy as jnp
from jax import lax
from jax.experimental import pallas as pl
from jax.experimental.pallas import tpu as pltpu
from jax.sharding import PartitionSpec as P

WHOLE = pl.BlockSpec(memory_space=pltpu.VMEM)
ANYWHERE = pl.BlockSpec(memory_space=pl.ANY)
SCALARS = pl.BlockSpec(memory_space=pltpu.SMEM)
ACROSS = (((1,), (1,)), ((), ()))
OVER_TOKENS = (((0,), (0,)), ((), ()))
PARAMS = pltpu.CompilerParams(vmem_limit_bytes=12 << 20)
F32 = jnp.float32


def spread_kernel(w_ref, out_ref, sems):
    copies = [
        pltpu.make_async_copy(w_ref, out_ref.at[pl.ds(2 * i, 2)], sems.at[i]) for i in range(out_ref.shape[0] // 2)
    ]
    for copy in copies:
        copy.start()
    for copy in copies:
        copy.wait()


def spread(w, n_dp):
    return pl.pallas_call(
        spread_kernel,
        out_shape=pltpu.HBM((n_dp,) + w.shape[1:], w.dtype),
        in_specs=[WHOLE],
        out_specs=ANYWHERE,
        scratch_shapes=[pltpu.SemaphoreType.DMA((n_dp // 2,))],
        compiler_params=PARAMS,
        cost_estimate=pl.CostEstimate(flops=0, bytes_accessed=n_dp * w.size, transcendentals=0),
    )(w)


def fetch(core, x_ref, g_ref, taken_ref, xs, gs, sems):
    tokens, model = x_ref.shape[1:]
    chunks = sems.shape[0]
    own, others = pl.ds(0, tokens), pl.ds(tokens, tokens)
    copies = []
    for j in range(chunks):
        cols = pl.ds(j * (model // chunks), model // chunks)
        copies.append([
            pltpu.make_async_copy(x_ref.at[core, :, cols], xs.at[own, cols], sems.at[j, 0]),
            pltpu.make_async_copy(taken_ref.at[0, :, cols], xs.at[others, cols], sems.at[j, 1]),
            pltpu.make_async_copy(g_ref.at[core, :, cols], gs.at[own, cols], sems.at[j, 2]),
            pltpu.make_async_copy(taken_ref.at[1, :, cols], gs.at[others, cols], sems.at[j, 3]),
        ])
        for copy in copies[-1]:
            copy.start()
    return copies


def adapter_kernel(
    count, core_ref, at_ref, x_ref, g_ref, taken_ref, w_ref, part_ref, up_ref, down_ref, up_send, down_send, edge_ref,
    xs, gs, ps, ms, loads, part_stores, stores, edge_sem
):
    is_down = core_ref[0] == 0
    slices, _, rank, width = w_ref.shape
    tokens, model = up_ref.shape
    chunks = loads.shape[0]
    per = slices // chunks
    own, others = pl.ds(0, tokens), pl.ds(tokens, tokens)
    fetches = fetch(core_ref[0], x_ref, g_ref, taken_ref, xs, gs, loads)

    u = jnp.zeros((2 * tokens, rank), F32)
    v = jnp.zeros((2 * tokens, rank), F32)
    squares = jnp.zeros((2 * tokens, 128), F32)
    for i in range(slices):
        if i % per == 0:
            for copy in fetches[i // per]:
                copy.wait()
        cols = pl.ds(i * width, width)
        x = xs[:, cols]
        u += lax.dot_general(x, w_ref[i, 0], ACROSS, preferred_element_type=F32)
        v += lax.dot_general(gs[:, cols], w_ref[i, 1], ACROSS, preferred_element_type=F32)
        xf = x.astype(F32)
        for j in range(width // 128):
            piece = xf[:, j * 128:(j + 1) * 128]
            squares += piece * piece
    scale = lax.rsqrt(jnp.sum(squares, axis=1, keepdims=True) / model + 1e-05)
    pre = scale * u
    sig = jax.nn.sigmoid(pre)
    hidden = (pre * sig).astype(jnp.bfloat16)
    dpre = v * (sig * (1.0 + pre * (1.0 - sig)))
    inner = jnp.sum(dpre * u, axis=1, keepdims=True) / model
    scaled = (scale * dpre).astype(jnp.bfloat16)
    back = inner * scale * scale * scale

    stored = []
    for i in range(slices):
        cols = pl.ds(i * width, width)
        ps[i, 0] = lax.dot_general(scaled, xs[:, cols], OVER_TOKENS, preferred_element_type=F32).astype(ps.dtype)
        ps[i, 1] = lax.dot_general(hidden, gs[:, cols], OVER_TOKENS, preferred_element_type=F32).astype(ps.dtype)
        xf, gf = xs[:, cols].astype(F32), gs[:, cols].astype(F32)
        y = (xf + jnp.dot(hidden, w_ref[i, 1], preferred_element_type=F32)).astype(ms.dtype)
        dx = (gf + jnp.dot(scaled, w_ref[i, 0], preferred_element_type=F32) - xf * back).astype(ms.dtype)
        ms[0, :, cols] = jnp.where(is_down, y, dx)
        ms[1, :, cols] = jnp.where(is_down, dx, y)
        if i % per == per - 1:
            j = i // per
            some = pl.ds(j * per, per)
            cols = pl.ds(j * (model // chunks), model // chunks)
            for copy in (
                pltpu.make_async_copy(ps.at[some], part_ref.at[some], part_stores.at[j]),
                pltpu.make_async_copy(ms.at[0, own, cols], up_ref.at[:, cols], stores.at[j, 0]),
                pltpu.make_async_copy(ms.at[1, own, cols], down_ref.at[:, cols], stores.at[j, 1]),
                pltpu.make_async_copy(ms.at[0, others, cols], up_send.at[:, cols], stores.at[j, 2]),
                pltpu.make_async_copy(ms.at[1, others, cols], down_send.at[:, cols], stores.at[j, 3]),
            ):
                copy.start()
                stored.append(copy)
    for way, position in ((0, count // 2 - 1), (1, count // 2)):
        @pl.when(at_ref[0] == position)
        def _():
            copy = pltpu.make_async_copy(ms.at[way, others], edge_ref, edge_sem)
            copy.start()
            copy.wait()
    for copy in stored:
        copy.wait()


def adapter(count, core, section, x, g, taken, w):
    tokens, model = x.shape[1:]
    one = pltpu.HBM((tokens, model), x.dtype)
    both = pltpu.VMEM((2 * tokens, model), x.dtype)
    return pl.pallas_call(
        functools.partial(adapter_kernel, count),
        out_shape=(pltpu.HBM(w.shape, w.dtype),) + (one,) * 5,
        in_specs=[SCALARS] * 2 + [ANYWHERE] * 3 + [WHOLE],
        out_specs=(ANYWHERE,) * 6,
        scratch_shapes=[
            both,
            both,
            pltpu.VMEM(w.shape, w.dtype),
            pltpu.VMEM((2, 2 * tokens, model), x.dtype),
            pltpu.SemaphoreType.DMA((4, 4)),
            pltpu.SemaphoreType.DMA((4,)),
            pltpu.SemaphoreType.DMA((4, 4)),
            pltpu.SemaphoreType.DMA,
        ],
        compiler_params=PARAMS,
        cost_estimate=pl.CostEstimate(flops=12 * tokens * w.size, bytes_accessed=12 << 20, transcendentals=0),
    )(core, section, x, g, taken, w)


def crossing_kernel(count, at_ref, up_ref, down_ref, out_ref, sem):
    for arrived, position in ((up_ref, count // 2), (down_ref, count // 2 - 1)):
        @pl.when(at_ref[0] == position)
        def _():
            copy = pltpu.make_async_copy(arrived, out_ref, sem)
            copy.start()
            copy.wait()


def crossing(count, section, up, down):
    return pl.pallas_call(
        functools.partial(crossing_kernel, count),
        out_shape=pltpu.HBM(up.shape, up.dtype),
        in_specs=[SCALARS] + [ANYWHERE] * 2,
        out_specs=ANYWHERE,
        scratch_shapes=[pltpu.SemaphoreType.DMA],
        compiler_params=PARAMS,
        cost_estimate=pl.CostEstimate(flops=0, bytes_accessed=4 * up.size, transcendentals=0),
    )(section, up, down)


def finish_kernel(
    count, core_ref, at_ref, up_own, down_own, up_got, down_got, crossed_own, crossed_got, next_ref, prev_ref, sems
):
    core, section = core_ref[0], at_ref[0]
    half = count // 2

    def put(i, src, on_down, on_up):
        @pl.when(core == 0)
        def _():
            pltpu.make_async_copy(src, on_down, sems.at[i]).start()

        @pl.when(core != 0)
        def _():
            pltpu.make_async_copy(src, on_up, sems.at[i]).start()

    places = (
        (next_ref.at[0], prev_ref.at[1]),
        (prev_ref.at[0], next_ref.at[1]),
        (prev_ref.at[1], next_ref.at[0]),
        (next_ref.at[1], prev_ref.at[0]),
    )
    for way, position, own, got in ((0, half, up_own, up_got), (1, half - 1, down_own, down_got)):
        @pl.when(section == position)
        def _():
            put(way, crossed_own, *places[way])
            put(way + 2, crossed_got, *places[way + 2])

        @pl.when(section != position)
        def _():
            put(way, own, *places[way])
            put(way + 2, got, *places[way + 2])

    for i in range(4):
        pltpu.make_async_copy(crossed_own, next_ref.at[0], sems.at[i]).wait()


def finish(count, core, section, *arrived):
    tokens, model = arrived[0].shape
    pair = pltpu.HBM((2, tokens, model), arrived[0].dtype)
    return pl.pallas_call(
        functools.partial(finish_kernel, count),
        out_shape=(pair, pair),
        in_specs=[SCALARS] * 2 + [ANYWHERE] * 6,
        out_specs=(ANYWHERE,) * 2,
        scratch_shapes=[pltpu.SemaphoreType.DMA((4,))],
        compiler_params=PARAMS,
        cost_estimate=pl.CostEstimate(flops=0, bytes_accessed=16 * tokens * model, transcendentals=0),
    )(core, section, *arrived)


def add_kernel(sums_ref, partner_ref, out_ref):
    out_ref[0] = sums_ref[0] + partner_ref[1].astype(F32)
    out_ref[1] = sums_ref[1] + partner_ref[0].astype(F32)


def add_mirrored(sums, partner):
    return pl.pallas_call(
        add_kernel,
        out_shape=jax.ShapeDtypeStruct(sums.shape, F32),
        in_specs=[WHOLE] * 2,
        out_specs=WHOLE,
        compiler_params=PARAMS,
        cost_estimate=pl.CostEstimate(flops=4_000_000_000, bytes_accessed=2 << 20, transcendentals=0),
    )(sums, partner)


def moved(value, routes, n_dp):
    pairs = [(a * n_dp + d, b * n_dp + (d ^ turn)) for a, b, turn in routes for d in range(n_dp)]
    return lax.ppermute(value, ("section", "dp"), pairs)


def shards(section_inputs, out_grads, adapters):
    n_dp = lax.axis_size("dp")
    count = lax.axis_size("section")
    half = count // 2
    core = jnp.full((1,), lax.axis_index("dp") % 2, jnp.int32)
    section = jnp.full((1,), lax.axis_index("section"), jnp.int32)
    is_down = core[0] == 0
    swap = [(i, i ^ 1) for i in range(n_dp)]
    inputs, grads = section_inputs[:, 0], out_grads[:, 0]

    gathered = lax.all_to_all(spread(adapters[:, 0], n_dp), "dp", 0, 0, tiled=True)
    given = jnp.stack([jnp.where(is_down, inputs[1], inputs[0]), jnp.where(is_down, grads[1], grads[0])])
    taken = lax.ppermute(given, "dp", swap)
    x, g, taken = (pltpu.with_memory_space_constraint(a, pltpu.HBM) for a in (inputs, grads, taken))
    parts, up_own, down_own, up_send, down_send, edge = adapter(count, core, section, x, g, taken, gathered)

    terms = lax.all_to_all(parts, "dp", 0, 0, tiled=True)
    sums = jnp.sum(terms.reshape((n_dp // 2, 2) + terms.shape[1:]).astype(F32), axis=0)

    group = n_dp // 2
    ups = [(i, i + 1) for i in range(count - 1) if i != half - 1]
    downs = [(i, i - 1) for i in range(1, count) if i != half]
    up_own = moved(up_own, [(a, b, 0) for a, b in ups] + [(half - 1, half, group)], n_dp)
    down_own = moved(down_own, [(a, b, 0) for a, b in downs] + [(half, half - 1, group)], n_dp)
    near = moved(edge, [(half - 1, 0, 1), (half, count - 1, 1)], n_dp)
    up_got = moved(up_send, [(a, b, 1) for a, b in ups], n_dp)
    down_got = moved(down_send, [(a, b, 1) for a, b in downs], n_dp)

    narrow = sums.astype(jnp.bfloat16)
    narrow, up_own, down_own, up_got, down_got = lax.optimization_barrier((narrow, up_own, down_own, up_got, down_got))
    partner = lax.ppermute(narrow, "section", [(i, count - 1 - i) for i in range(count)])
    crossed_own = moved(crossing(count, section, up_own, down_own), [(half, half, group), (half - 1, half - 1, group)], n_dp)
    crossed_got = moved(near, [(0, half, 0), (count - 1, half - 1, 0)], n_dp)
    summed = add_mirrored(sums, partner)
    next_inputs, prev_grads = finish(
        count, core, section, up_own, down_own, up_got, down_got, crossed_own, crossed_got
    )
    return (next_inputs[:, None], prev_grads[:, None], summed[:, None])


def solution(mesh):
    in_specs = (
        P(None, "section", "dp", None),
        P(None, "section", "dp", None),
        P(None, "section", None, None, "dp"),
    )
    out_specs = (
        P(None, "section", "dp", None),
        P(None, "section", "dp", None),
        P(None, "section", None, None, "dp"),
    )
    return jax.shard_map(shards, mesh=mesh, in_specs=in_specs, out_specs=out_specs, check_vma=False)
```

time: 118 us -> 117 us (level)
  the two profiles are of different devices: /device:TPU:226 before, /device:TPU:1 now
where the time goes in v6:
time: 117 us; the launch traced here: 116 us
  waiting for transfers between devices  62 us (53%)
  starting transfers between devices  40.6 us (35%)
  Pallas kernels  8.29 us (7%)
  other arithmetic  3.39 us (3%)
    all_to_all x1, waiting for transfers between devices, shards(): lax.all_to_all(spread(adapters[:, 0], n_dp), 'dp', 0, 0, tiled=True)  21.5 us
    ppermute x1, waiting for transfers between devices, shards(): lax.ppermute(narrow, 'section', [(i, count - 1 - i) for i in range(count)])  19.9 us
    all_to_all x1, waiting for transfers between devices, shards(): terms = lax.all_to_all(parts, 'dp', 0, 0, tiled=True)  18.1 us
    ppermute x7, starting transfers between devices, moved(): return lax.ppermute(value, ('section', 'dp'), pairs)  12.7 us
    all_to_all x1, starting transfers between devices, shards(): lax.all_to_all(spread(adapters[:, 0], n_dp), 'dp', 0, 0, tiled=True)  10.5 us
    ppermute x1, starting transfers between devices, shards(): lax.ppermute(narrow, 'section', [(i, count - 1 - i) for i in range(count)])  9.84 us
    all_to_all x1, starting transfers between devices, shards(): terms = lax.all_to_all(parts, 'dp', 0, 0, tiled=True)  5.29 us
    pallas_call x1, Pallas kernels, adapter(): pl.pallas_call(functools.partial(adapter_kernel, count), out_shape=(pltpu...  4.67 us
  transfers between devices with their start and end apart: 11, of which 4 were waited for; matrix products, arithmetic and copies ran while one was open for 3% of the time, Pallas kernels for 1%

profile of v6, /device:TPU:1, one launch (start us, length us, event | category | flops | bytes accessed | tf_op | source)
XLA Modules:
  0.0 116.1 jit_solution(2916838120559735139)
XLA Ops:
  0.6 0.0 copy-start
  0.6 0.9 copy-done
  1.6 1.4 %shard_map.58 = bf16[16,2,64,512]{3,2,1,0:T(8,128)(2,1)} custom-call(bf16[2,2,64,512]{3,2,1,0:T(8,128)(2,1)S(1)} %bitcast.20), custom_call_target="tpu_custom_call" | custom-call | bytes 2097152 | tf_op jit(solution)/shard_map/pallas_call | solution.py:30
  3.0 0.0 copy-start.1
  3.0 10.5 %all-to-all-start = ((bf16[16,2,64,512]{3,2,1,0:T(8,128)(2,1)}), bf16[16,2,64,512]{3,2,1,0:T(8,128)(2,1)S(1)}, u32[]{:S(2)}, u32[]{:S(2)}) async-start(bf16[16,2,64,512]{3,2,1,0:T(8,128)(2,1)} %shard_map.58), calls=%async_computation | async-start | bytes 4194304 | tf_op jit(solution)/shard_map/all_to_all | solution.py:254
  13.5 0.0 copy-done.1
  13.5 1.3 %select_bitcast_fusion = (bf16[1,32,8192]{2,1,0:T(8,128)(2,1)S(1)}, bf16[1,32,8192]{2,1,0:T(8,128)(2,1)S(1)}) fusion(bf16[2,1,32,8192]{3,2,1,0:T(8,128)(2,1)} %param.4, pred[]{:T(512)S(6)} %eq.5, bf16[2,1,32,8192]{3,2,1,0:T(8,128)(2,1)S(1)} %copy-done.1), kind=kLoop, calls=%fused_computation.2 | loop fusion | flops 524288 | bytes 3145729 | tf_op jit(solution)/shard_map/jit(_where)/select_n | solution.py:255
  14.9 0.1 pad_maximum_fusion
  15.0 2.1 %collective-permute-start = (bf16[2,32,8192]{2,1,0:T(8,128)(2,1)S(1)}, bf16[2,32,8192]{2,1,0:T(8,128)(2,1)}, u32[]{:S(2)}, u32[]{:S(2)}) collective-permute-start(bf16[2,32,8192]{2,1,0:T(8,128)(2,1)S(1)} %pad_maximum_fusion), channel_id=1, source_target_pairs={{0,1},{1,0},{2,3},{3,2},{4,5},{5,4},{6,7},{7,6},{8,9},{9,8},{10,11... | collective-permute-start | bytes 3145736 | tf_op jit(solution)/shard_map/ppermute | solution.py:256
  17.1 2.5 %collective-permute-done.taken_ref = bf16[2,32,8192]{2,1,0:T(8,128)(2,1)} collective-permute-done((bf16[2,32,8192]{2,1,0:T(8,128)(2,1)S(1)}, bf16[2,32,8192]{2,1,0:T(8,128)(2,1)}, u32[]{:S(2)}, u32[]{:S(2)}) %collective-permute-start) | collective-permute-done | bytes 1048608 | tf_op jit(solution)/shard_map/ppermute | solution.py:256
  19.7 21.5 %all-to-all-done.w_ref = bf16[16,2,64,512]{3,2,1,0:T(8,128)(2,1)S(1)} async-done(((bf16[16,2,64,512]{3,2,1,0:T(8,128)(2,1)}), bf16[16,2,64,512]{3,2,1,0:T(8,128)(2,1)S(1)}, u32[]{:S(2)}, u32[]{:S(2)}) %all-to-all-start) | async-done | bytes 2097184 | tf_op jit(solution)/shard_map/all_to_all | solution.py:254
  41.1 4.7 %shard_map.59 = (bf16[16,2,64,512]{3,2,1,0:T(8,128)(2,1)}, bf16[32,8192]{1,0:T(8,128)(2,1)}, bf16[32,8192]{1,0:T(8,128)(2,1)}, bf16[32,8192]{1,0:T(8,128)(2,1)},...) custom-call(s32[1]{0:T(128)} %bitcast.core_ref, s32[1]{0:T(128)} %bitcast.1.at_ref, bf16[2,32,8192]{2,1,0:T(8,128)(2,1)} %bitcast.21, ...), custom_call_target="tpu_custom_call" | custom-call | flops 402653184 | bytes 12582912 | tf_op jit(solution)/shard_map/pallas_call | solution.py:132
  45.8 0.0 copy-start.3
  45.8 0.0 copy-start.2
  45.8 5.3 %all-to-all-start.1 = ((bf16[16,2,64,512]{3,2,1,0:T(8,128)(2,1)}), bf16[16,2,64,512]{3,2,1,0:T(8,128)(2,1)}, u32[]{:S(2)}, u32[]{:S(2)}) async-start(bf16[16,2,64,512]{3,2,1,0:T(8,128)(2,1)} %get-tuple-element.16), calls=%async_computation.1 | async-start | bytes 4194304 | tf_op jit(solution)/shard_map/all_to_all | solution.py:260
  51.1 1.3 %collective-permute-start.1 = (bf16[32,8192]{1,0:T(8,128)(2,1)}, bf16[32,8192]{1,0:T(8,128)(2,1)S(1)}, u32[]{:S(2)}, u32[]{:S(2)}) collective-permute-start(bf16[32,8192]{1,0:T(8,128)(2,1)} %get-tuple-element.17), channel_id=1, source_target_pairs={{0,16},{1,17},{2,18},{3,19},{4,20},{5,21},{6,22},{7,23},{8,24},{9,... | collective-permute-start | bytes 1572872 | tf_op jit(solution)/shard_map/ppermute | solution.py:241
  52.4 1.3 %collective-permute-start.2 = (bf16[32,8192]{1,0:T(8,128)(2,1)}, bf16[32,8192]{1,0:T(8,128)(2,1)S(1)}, u32[]{:S(2)}, u32[]{:S(2)}) collective-permute-start(bf16[32,8192]{1,0:T(8,128)(2,1)} %get-tuple-element.18), channel_id=1, source_target_pairs={{16,0},{17,1},{18,2},{19,3},{20,4},{21,5},{22,6},{23,7},{24,8},{25... | collective-permute-start | bytes 1572872 | tf_op jit(solution)/shard_map/ppermute | solution.py:241
  53.7 4.3 %collective-permute-start.3 = (bf16[32,8192]{1,0:T(8,128)(2,1)}, bf16[32,8192]{1,0:T(8,128)(2,1)S(1)}, u32[]{:S(2)}, u32[]{:S(2)}) collective-permute-start(bf16[32,8192]{1,0:T(8,128)(2,1)} %get-tuple-element.19), channel_id=1, source_target_pairs={{0,17},{1,16},{2,19},{3,18},{4,21},{5,20},{6,23},{7,22},{8,25},{9,... | collective-permute-start | bytes 1572872 | tf_op jit(solution)/shard_map/ppermute | solution.py:241
  58.1 0.0 copy-done.3
  58.1 1.3 %collective-permute-start.4 = (bf16[32,8192]{1,0:T(8,128)(2,1)S(1)}, bf16[32,8192]{1,0:T(8,128)(2,1)S(1)}, u32[]{:S(2)}, u32[]{:S(2)}) collective-permute-start(bf16[32,8192]{1,0:T(8,128)(2,1)S(1)} %copy-done.3), channel_id=1, source_target_pairs={{16,1},{17,0},{18,3},{19,2},{20,5},{21,4},{22,7},{23,6},{24,9},{25... | collective-permute-start | bytes 1572872 | tf_op jit(solution)/shard_map/ppermute | solution.py:241
  59.4 0.0 copy-done.2
  59.4 1.3 %collective-permute-start.6 = (bf16[32,8192]{1,0:T(8,128)(2,1)S(1)}, bf16[32,8192]{1,0:T(8,128)(2,1)}, u32[]{:S(2)}, u32[]{:S(2)}) collective-permute-start(bf16[32,8192]{1,0:T(8,128)(2,1)S(1)} %copy-done.2), channel_id=1, source_target_pairs={{240,1},{241,0},{242,3},{243,2},{244,5},{245,4},{246,7},{247,6},{2... | collective-permute-start | bytes 1572872 | tf_op jit(solution)/shard_map/ppermute | solution.py:241
  60.7 18.1 %all-to-all-done.1 = bf16[16,2,64,512]{3,2,1,0:T(8,128)(2,1)} async-done(((bf16[16,2,64,512]{3,2,1,0:T(8,128)(2,1)}), bf16[16,2,64,512]{3,2,1,0:T(8,128)(2,1)}, u32[]{:S(2)}, u32[]{:S(2)}) %all-to-all-start.1) | async-done | bytes 2097184 | tf_op jit(solution)/shard_map/all_to_all | solution.py:260
  78.8 2.0 %convert_reduce_fusion.sums_ref = f32[2,2,64,512]{3,2,1,0:T(8,128)S(1)} fusion(bf16[8,2,2,64,512]{4,3,2,1,0:T(8,128)(2,1)} %bitcast.14), kind=kLoop, calls=%fused_computation | loop fusion | flops 1966080 | bytes 2621440 | tf_op jit(solution)/shard_map/reduce_sum | solution.py:261
  80.8 0.0 collective-permute-done.1.up_ref.up_own
  80.8 0.0 collective-permute-done.2.down_ref.down_own
  80.8 0.0 collective-permute-done.3.up_got
  80.8 0.0 collective-permute-done.4.down_got
  80.8 9.8 %collective-permute-start.8 = (bf16[2,2,64,512]{3,2,1,0:T(8,128)(2,1)S(1)}, bf16[2,2,64,512]{3,2,1,0:T(8,128)(2,1)S(1)}, u32[]{:S(2)}, u32[]{:S(2)}) collective-permute-start(bf16[2,2,64,512]{3,2,1,0:T(8,128)(2,1)S(1)} %convert_element_type.11), channel_id=1, source_target_pairs={{0,496},{16,480},{32,464},{48,448},{64,432},{80,416},{96,400},{112... | collective-permute-start | bytes 786440 | tf_op jit(solution)/shard_map/ppermute | solution.py:274
  90.7 0.0 collective-permute-done.6
  90.7 2.5 %collective-permute-start.7 = (bf16[32,8192]{1,0:T(8,128)(2,1)}, bf16[32,8192]{1,0:T(8,128)(2,1)S(1)}, u32[]{:S(2)}, u32[]{:S(2)}) collective-permute-start(bf16[32,8192]{1,0:T(8,128)(2,1)} %collective-permute-done.6), channel_id=1, source_target_pairs={{0,256},{1,257},{2,258},{3,259},{4,260},{5,261},{6,262},{7,263},{8... | collective-permute-start | bytes 1572872 | tf_op jit(solution)/shard_map/ppermute | solution.py:241
  93.2 0.7 collective-permute-start.5
  93.9 19.9 %collective-permute-done.8.partner_ref = bf16[2,2,64,512]{3,2,1,0:T(8,128)(2,1)S(1)} collective-permute-done((bf16[2,2,64,512]{3,2,1,0:T(8,128)(2,1)S(1)}, bf16[2,2,64,512]{3,2,1,0:T(8,128)(2,1)S(1)}, u32[]{:S(2)}, u32[]{:S(2)}) %collective-permute-start.8) | collective-permute-done | bytes 262176 | tf_op jit(solution)/shard_map/ppermute | solution.py:274
  113.9 0.8 shard_map.62
  114.7 0.0 collective-permute-done.7.crossed_got
  114.7 0.0 collective-permute-done.5.crossed_own
  114.7 1.3 %shard_map.61 = (bf16[2,32,8192]{2,1,0:T(8,128)(2,1)}, bf16[2,32,8192]{2,1,0:T(8,128)(2,1)}) custom-call(s32[1]{0:T(128)} %bitcast.core_ref, s32[1]{0:T(128)} %bitcast.1.at_ref, bf16[32,8192]{1,0:T(8,128)(2,1)S(1)} %collective-permute-done.1.up_ref.up_own, bf16[32,8192]{1,0:T(8,128)(2,1)S(1)} %collective-permute-done.2.down_ref.down_own, ...), custom_call_target="tpu_custom_call" | custom-call | bytes 4194304 | tf_op jit(solution)/shard_map/pallas_call | solution.py:212
  (2 shorter events, 0.1 us)
Async XLA Ops:
  0.6 1.0 copy-start
  3.0 10.5 %copy-start.1 = (bf16[2,1,32,8192]{3,2,1,0:T(8,128)(2,1)S(1)}, bf16[2,1,32,8192]{3,2,1,0:T(8,128)(2,1)}, u32[]{:S(2)}) copy-start(bf16[2,1,32,8192]{3,2,1,0:T(8,128)(2,1)} %param.3) | copy-start | bytes 3145732
  3.0 38.1 %all-to-all-start = ((bf16[16,2,64,512]{3,2,1,0:T(8,128)(2,1)}), bf16[16,2,64,512]{3,2,1,0:T(8,128)(2,1)S(1)}, u32[]{:S(2)}, u32[]{:S(2)}) async-start(bf16[16,2,64,512]{3,2,1,0:T(8,128)(2,1)} %shard_map.58), calls=%async_computation | async-start | bytes 4194304 | tf_op jit(solution)/shard_map/all_to_all | solution.py:254
  15.0 4.7 %collective-permute-start = (bf16[2,32,8192]{2,1,0:T(8,128)(2,1)S(1)}, bf16[2,32,8192]{2,1,0:T(8,128)(2,1)}, u32[]{:S(2)}, u32[]{:S(2)}) collective-permute-start(bf16[2,32,8192]{2,1,0:T(8,128)(2,1)S(1)} %pad_maximum_fusion), channel_id=1, source_target_pairs={{0,1},{1,0},{2,3},{3,2},{4,5},{5,4},{6,7},{7,6},{8,9},{9,8},{10,11... | collective-permute-start | bytes 3145736 | tf_op jit(solution)/shard_map/ppermute | solution.py:256
  45.8 12.3 %copy-start.3 = (bf16[32,8192]{1,0:T(8,128)(2,1)S(1)}, bf16[32,8192]{1,0:T(8,128)(2,1)}, u32[]{:S(2)}) copy-start(bf16[32,8192]{1,0:T(8,128)(2,1)} %get-tuple-element.20) | copy-start | bytes 1572868
  45.8 13.6 %copy-start.2 = (bf16[32,8192]{1,0:T(8,128)(2,1)S(1)}, bf16[32,8192]{1,0:T(8,128)(2,1)}, u32[]{:S(2)}) copy-start(bf16[32,8192]{1,0:T(8,128)(2,1)} %get-tuple-element.25) | copy-start | bytes 1572868
  45.8 33.0 %all-to-all-start.1 = ((bf16[16,2,64,512]{3,2,1,0:T(8,128)(2,1)}), bf16[16,2,64,512]{3,2,1,0:T(8,128)(2,1)}, u32[]{:S(2)}, u32[]{:S(2)}) async-start(bf16[16,2,64,512]{3,2,1,0:T(8,128)(2,1)} %get-tuple-element.16), calls=%async_computation.1 | async-start | bytes 4194304 | tf_op jit(solution)/shard_map/all_to_all | solution.py:260
  51.1 29.7 %collective-permute-start.1 = (bf16[32,8192]{1,0:T(8,128)(2,1)}, bf16[32,8192]{1,0:T(8,128)(2,1)S(1)}, u32[]{:S(2)}, u32[]{:S(2)}) collective-permute-start(bf16[32,8192]{1,0:T(8,128)(2,1)} %get-tuple-element.17), channel_id=1, source_target_pairs={{0,16},{1,17},{2,18},{3,19},{4,20},{5,21},{6,22},{7,23},{8,24},{9,... | collective-permute-start | bytes 1572872 | tf_op jit(solution)/shard_map/ppermute | solution.py:241
  52.4 28.4 %collective-permute-start.2 = (bf16[32,8192]{1,0:T(8,128)(2,1)}, bf16[32,8192]{1,0:T(8,128)(2,1)S(1)}, u32[]{:S(2)}, u32[]{:S(2)}) collective-permute-start(bf16[32,8192]{1,0:T(8,128)(2,1)} %get-tuple-element.18), channel_id=1, source_target_pairs={{16,0},{17,1},{18,2},{19,3},{20,4},{21,5},{22,6},{23,7},{24,8},{25... | collective-permute-start | bytes 1572872 | tf_op jit(solution)/shard_map/ppermute | solution.py:241
  53.7 27.1 %collective-permute-start.3 = (bf16[32,8192]{1,0:T(8,128)(2,1)}, bf16[32,8192]{1,0:T(8,128)(2,1)S(1)}, u32[]{:S(2)}, u32[]{:S(2)}) collective-permute-start(bf16[32,8192]{1,0:T(8,128)(2,1)} %get-tuple-element.19), channel_id=1, source_target_pairs={{0,17},{1,16},{2,19},{3,18},{4,21},{5,20},{6,23},{7,22},{8,25},{9,... | collective-permute-start | bytes 1572872 | tf_op jit(solution)/shard_map/ppermute | solution.py:241
  58.1 22.7 %collective-permute-start.4 = (bf16[32,8192]{1,0:T(8,128)(2,1)S(1)}, bf16[32,8192]{1,0:T(8,128)(2,1)S(1)}, u32[]{:S(2)}, u32[]{:S(2)}) collective-permute-start(bf16[32,8192]{1,0:T(8,128)(2,1)S(1)} %copy-done.3), channel_id=1, source_target_pairs={{16,1},{17,0},{18,3},{19,2},{20,5},{21,4},{22,7},{23,6},{24,9},{25... | collective-permute-start | bytes 1572872 | tf_op jit(solution)/shard_map/ppermute | solution.py:241
  59.4 31.3 %collective-permute-start.6 = (bf16[32,8192]{1,0:T(8,128)(2,1)S(1)}, bf16[32,8192]{1,0:T(8,128)(2,1)}, u32[]{:S(2)}, u32[]{:S(2)}) collective-permute-start(bf16[32,8192]{1,0:T(8,128)(2,1)S(1)} %copy-done.2), channel_id=1, source_target_pairs={{240,1},{241,0},{242,3},{243,2},{244,5},{245,4},{246,7},{247,6},{2... | collective-permute-start | bytes 1572872 | tf_op jit(solution)/shard_map/ppermute | solution.py:241
  80.8 33.0 %collective-permute-start.8 = (bf16[2,2,64,512]{3,2,1,0:T(8,128)(2,1)S(1)}, bf16[2,2,64,512]{3,2,1,0:T(8,128)(2,1)S(1)}, u32[]{:S(2)}, u32[]{:S(2)}) collective-permute-start(bf16[2,2,64,512]{3,2,1,0:T(8,128)(2,1)S(1)} %convert_element_type.11), channel_id=1, source_target_pairs={{0,496},{16,480},{32,464},{48,448},{64,432},{80,416},{96,400},{112... | collective-permute-start | bytes 786440 | tf_op jit(solution)/shard_map/ppermute | solution.py:274
  90.7 24.0 %collective-permute-start.7 = (bf16[32,8192]{1,0:T(8,128)(2,1)}, bf16[32,8192]{1,0:T(8,128)(2,1)S(1)}, u32[]{:S(2)}, u32[]{:S(2)}) collective-permute-start(bf16[32,8192]{1,0:T(8,128)(2,1)} %collective-permute-done.6), channel_id=1, source_target_pairs={{0,256},{1,257},{2,258},{3,259},{4,260},{5,261},{6,262},{7,263},{8... | collective-permute-start | bytes 1572872 | tf_op jit(solution)/shard_map/ppermute | solution.py:241
  93.2 21.5 %collective-permute-start.5 = (bf16[32,8192]{1,0:T(8,128)(2,1)}, bf16[32,8192]{1,0:T(8,128)(2,1)S(1)}, u32[]{:S(2)}, u32[]{:S(2)}) collective-permute-start(bf16[32,8192]{1,0:T(8,128)(2,1)} %shard_map.60), channel_id=1, source_target_pairs={{256,264},{257,265},{258,266},{259,267},{260,268},{261,269},{262,2... | collective-permute-start | bytes 1572872 | tf_op jit(solution)/shard_map/ppermute | solution.py:241

commit v7 on v6

--- a/solution.py
+++ b/solution.py
@@ -14,6 +14,10 @@
 OVER_TOKENS = (((0,), (0,)), ((), ()))
 PARAMS = pltpu.CompilerParams(vmem_limit_bytes=12 << 20)
 F32 = jnp.float32
+
+
+def in_hbm(array):
+    return pltpu.with_memory_space_constraint(array, pltpu.HBM)
 
 
 def spread_kernel(w_ref, out_ref, sems):
@@ -30,12 +34,12 @@
     return pl.pallas_call(
         spread_kernel,
         out_shape=pltpu.HBM((n_dp,) + w.shape[1:], w.dtype),
-        in_specs=[WHOLE],
+        in_specs=[ANYWHERE],
         out_specs=ANYWHERE,
         scratch_shapes=[pltpu.SemaphoreType.DMA((n_dp // 2,))],
         compiler_params=PARAMS,
         cost_estimate=pl.CostEstimate(flops=0, bytes_accessed=n_dp * w.size, transcendentals=0),
-    )(w)
+    )(in_hbm(w))
 
 
 def fetch(core, x_ref, g_ref, taken_ref, xs, gs, sems):
@@ -139,9 +143,9 @@
             both,
             pltpu.VMEM(w.shape, w.dtype),
             pltpu.VMEM((2, 2 * tokens, model), x.dtype),
-            pltpu.SemaphoreType.DMA((4, 4)),
-            pltpu.SemaphoreType.DMA((4,)),
-            pltpu.SemaphoreType.DMA((4, 4)),
+            pltpu.SemaphoreType.DMA((8, 4)),
+            pltpu.SemaphoreType.DMA((8,)),
+            pltpu.SemaphoreType.DMA((8, 4)),
             pltpu.SemaphoreType.DMA,
         ],
         compiler_params=PARAMS,
@@ -217,7 +221,7 @@
         scratch_shapes=[pltpu.SemaphoreType.DMA((4,))],
         compiler_params=PARAMS,
         cost_estimate=pl.CostEstimate(flops=0, bytes_accessed=16 * tokens * model, transcendentals=0),
-    )(core, section, *arrived)
+    )(core, section, *arrived[:2], *(in_hbm(a) for a in arrived[2:4]), *arrived[4:])
 
 
 def add_kernel(sums_ref, partner_ref, out_ref):
@@ -254,7 +258,7 @@
     gathered = lax.all_to_all(spread(adapters[:, 0], n_dp), "dp", 0, 0, tiled=True)
     given = jnp.stack([jnp.where(is_down, inputs[1], inputs[0]), jnp.where(is_down, grads[1], grads[0])])
     taken = lax.ppermute(given, "dp", swap)
-    x, g, taken = (pltpu.with_memory_space_constraint(a, pltpu.HBM) for a in (inputs, grads, taken))
+    x, g, taken = (in_hbm(a) for a in (inputs, grads, taken))
     parts, up_own, down_own, up_send, down_send, edge = adapter(count, core, section, x, g, taken, gathered)
 
     terms = lax.all_to_all(parts, "dp", 0, 0, tiled=True)

time: 117 us -> 209 us (1.79)
  Pallas kernels: 8.29 us -> 103 us
    pallas_call x1, Pallas kernels: 1.41 us -> 64.7 us  [spread(): pl.pallas_call(spread_kernel, out_shape=pltpu.HBM((n_dp,) + w.shape[1:],...]
    pallas_call x1, Pallas kernels: 1.35 us -> 32.9 us  [finish(): pl.pallas_call(functools.partial(finish_kernel, count), out_shape=(pair,...]
  transfers between devices with their start and end apart: 11 -> 11, of which waited for: 4 -> 5; matrix products, arithmetic and copies ran while one was open for 3% -> 1% of each run, Pallas kernels for 1% -> 0%
where the time goes in v7:
time: 209 us; the launch traced here: 208 us
  Pallas kernels  103 us (49%)
  waiting for transfers between devices  61.4 us (29%)
  starting transfers between devices  40.5 us (19%)
    pallas_call x1, Pallas kernels, spread(): pl.pallas_call(spread_kernel, out_shape=pltpu.HBM((n_dp,) + w.shape[1:],...  64.7 us
    pallas_call x1, Pallas kernels, finish(): pl.pallas_call(functools.partial(finish_kernel, count), out_shape=(pair,...  32.9 us
    all_to_all x1, waiting for transfers between devices, shards(): lax.all_to_all(spread(adapters[:, 0], n_dp), 'dp', 0, 0, tiled=True)  21.5 us
    ppermute x1, waiting for transfers between devices, shards(): lax.ppermute(narrow, 'section', [(i, count - 1 - i) for i in range(count)])  19.3 us
    all_to_all x1, waiting for transfers between devices, shards(): terms = lax.all_to_all(parts, 'dp', 0, 0, tiled=True)  17.4 us
    ppermute x7, starting transfers between devices, moved(): return lax.ppermute(value, ('section', 'dp'), pairs)  13.5 us
    all_to_all x1, starting transfers between devices, shards(): lax.all_to_all(spread(adapters[:, 0], n_dp), 'dp', 0, 0, tiled=True)  10.5 us
    ppermute x1, starting transfers between devices, shards(): lax.ppermute(narrow, 'section', [(i, count - 1 - i) for i in range(count)])  9.16 us
  transfers between devices with their start and end apart: 11, of which 5 were waited for; matrix products, arithmetic and copies ran while one was open for 1% of the time, Pallas kernels for 0%

profile of v7, /device:TPU:1, one launch (start us, length us, event | category | flops | bytes accessed | tf_op | source)
XLA Modules:
  0.0 207.7 jit_solution(2249957848593782905)
XLA Ops:
  0.6 64.7 %shard_map.58 = bf16[16,2,64,512]{3,2,1,0:T(8,128)(2,1)} custom-call(bf16[2,2,64,512]{3,2,1,0:T(8,128)(2,1)} %bitcast.23), custom_call_target="tpu_custom_call" | custom-call | bytes 2097152 | tf_op jit(solution)/shard_map/pallas_call | solution.py:34
  65.3 0.0 copy-start
  65.3 10.5 %all-to-all-start = ((bf16[16,2,64,512]{3,2,1,0:T(8,128)(2,1)}), bf16[16,2,64,512]{3,2,1,0:T(8,128)(2,1)S(1)}, u32[]{:S(2)}, u32[]{:S(2)}) async-start(bf16[16,2,64,512]{3,2,1,0:T(8,128)(2,1)} %shard_map.58), calls=%async_computation | async-start | bytes 4194304 | tf_op jit(solution)/shard_map/all_to_all | solution.py:258
  75.9 0.0 copy-done
  75.9 1.3 select_bitcast_fusion
  77.2 0.1 pad_maximum_fusion
  77.3 2.1 %collective-permute-start = (bf16[2,32,8192]{2,1,0:T(8,128)(2,1)S(1)}, bf16[2,32,8192]{2,1,0:T(8,128)(2,1)}, u32[]{:S(2)}, u32[]{:S(2)}) collective-permute-start(bf16[2,32,8192]{2,1,0:T(8,128)(2,1)S(1)} %pad_maximum_fusion), channel_id=1, source_target_pairs={{0,1},{1,0},{2,3},{3,2},{4,5},{5,4},{6,7},{7,6},{8,9},{9,8},{10,11... | collective-permute-start | bytes 3145736 | tf_op jit(solution)/shard_map/ppermute | solution.py:260
  79.5 2.5 %collective-permute-done.taken_ref = bf16[2,32,8192]{2,1,0:T(8,128)(2,1)} collective-permute-done((bf16[2,32,8192]{2,1,0:T(8,128)(2,1)S(1)}, bf16[2,32,8192]{2,1,0:T(8,128)(2,1)}, u32[]{:S(2)}, u32[]{:S(2)}) %collective-permute-start) | collective-permute-done | bytes 1048608 | tf_op jit(solution)/shard_map/ppermute | solution.py:260
  82.0 21.5 %all-to-all-done.w_ref = bf16[16,2,64,512]{3,2,1,0:T(8,128)(2,1)S(1)} async-done(((bf16[16,2,64,512]{3,2,1,0:T(8,128)(2,1)}), bf16[16,2,64,512]{3,2,1,0:T(8,128)(2,1)S(1)}, u32[]{:S(2)}, u32[]{:S(2)}) %all-to-all-start) | async-done | bytes 2097184 | tf_op jit(solution)/shard_map/all_to_all | solution.py:258
  103.4 4.8 %shard_map.59 = (bf16[16,2,64,512]{3,2,1,0:T(8,128)(2,1)}, bf16[32,8192]{1,0:T(8,128)(2,1)}, bf16[32,8192]{1,0:T(8,128)(2,1)}, bf16[32,8192]{1,0:T(8,128)(2,1)},...) custom-call(s32[1]{0:T(128)} %bitcast.core_ref, s32[1]{0:T(128)} %bitcast.1.at_ref, bf16[2,32,8192]{2,1,0:T(8,128)(2,1)} %bitcast.21, ...), custom_call_target="tpu_custom_call" | custom-call | flops 402653184 | bytes 12582912 | tf_op jit(solution)/shard_map/pallas_call | solution.py:136
  108.3 5.2 %all-to-all-start.1 = ((bf16[16,2,64,512]{3,2,1,0:T(8,128)(2,1)}), bf16[16,2,64,512]{3,2,1,0:T(8,128)(2,1)S(1)}, u32[]{:S(2)}, u32[]{:S(2)}) async-start(bf16[16,2,64,512]{3,2,1,0:T(8,128)(2,1)} %get-tuple-element.16), calls=%async_computation.1 | async-start | bytes 4194304 | tf_op jit(solution)/shard_map/all_to_all | solution.py:264
  113.5 1.3 collective-permute-start.1
  114.8 1.3 collective-permute-start.2
  116.1 5.1 %collective-permute-start.3 = (bf16[32,8192]{1,0:T(8,128)(2,1)}, bf16[32,8192]{1,0:T(8,128)(2,1)}, u32[]{:S(2)}, u32[]{:S(2)}) collective-permute-start(bf16[32,8192]{1,0:T(8,128)(2,1)} %get-tuple-element.19), channel_id=1, source_target_pairs={{0,17},{1,16},{2,19},{3,18},{4,21},{5,20},{6,23},{7,22},{8,25},{9,... | collective-permute-start | bytes 1572872 | tf_op jit(solution)/shard_map/ppermute | solution.py:245
  121.1 1.3 collective-permute-start.4
  122.4 1.3 collective-permute-start.6
  123.7 17.4 %all-to-all-done.1 = bf16[16,2,64,512]{3,2,1,0:T(8,128)(2,1)S(1)} async-done(((bf16[16,2,64,512]{3,2,1,0:T(8,128)(2,1)}), bf16[16,2,64,512]{3,2,1,0:T(8,128)(2,1)S(1)}, u32[]{:S(2)}, u32[]{:S(2)}) %all-to-all-start.1) | async-done | bytes 2097184 | tf_op jit(solution)/shard_map/all_to_all | solution.py:264
  141.1 0.3 convert_reduce_fusion.sums_ref
  141.5 0.0 collective-permute-done.1.up_ref.up_own
  141.5 0.0 collective-permute-done.2.down_ref.down_own
  141.5 0.0 collective-permute-done.3.up_got
  141.5 0.7 collective-permute-done.4.down_got
  142.2 9.2 %collective-permute-start.8 = (bf16[2,2,64,512]{3,2,1,0:T(8,128)(2,1)S(1)}, bf16[2,2,64,512]{3,2,1,0:T(8,128)(2,1)S(1)}, u32[]{:S(2)}, u32[]{:S(2)}) collective-permute-start(bf16[2,2,64,512]{3,2,1,0:T(8,128)(2,1)S(1)} %convert_element_type.11), channel_id=1, source_target_pairs={{0,496},{16,480},{32,464},{48,448},{64,432},{80,416},{96,400},{112... | collective-permute-start | bytes 786440 | tf_op jit(solution)/shard_map/ppermute | solution.py:278
  151.4 0.0 collective-permute-done.6
  151.4 2.5 %collective-permute-start.7 = (bf16[32,8192]{1,0:T(8,128)(2,1)}, bf16[32,8192]{1,0:T(8,128)(2,1)S(1)}, u32[]{:S(2)}, u32[]{:S(2)}) collective-permute-start(bf16[32,8192]{1,0:T(8,128)(2,1)} %collective-permute-done.6), channel_id=1, source_target_pairs={{0,256},{1,257},{2,258},{3,259},{4,260},{5,261},{6,262},{7,263},{8... | collective-permute-start | bytes 1572872 | tf_op jit(solution)/shard_map/ppermute | solution.py:245
  153.9 0.7 collective-permute-start.5
  154.6 19.3 %collective-permute-done.8.partner_ref = bf16[2,2,64,512]{3,2,1,0:T(8,128)(2,1)S(1)} collective-permute-done((bf16[2,2,64,512]{3,2,1,0:T(8,128)(2,1)S(1)}, bf16[2,2,64,512]{3,2,1,0:T(8,128)(2,1)S(1)}, u32[]{:S(2)}, u32[]{:S(2)}) %collective-permute-start.8) | collective-permute-done | bytes 262176 | tf_op jit(solution)/shard_map/ppermute | solution.py:278
  174.0 0.8 shard_map.62
  174.8 0.0 collective-permute-done.7.crossed_got
  174.8 0.0 collective-permute-done.5.crossed_own
  174.8 32.9 %shard_map.61 = (bf16[2,32,8192]{2,1,0:T(8,128)(2,1)}, bf16[2,32,8192]{2,1,0:T(8,128)(2,1)}) custom-call(s32[1]{0:T(128)} %bitcast.core_ref, s32[1]{0:T(128)} %bitcast.1.at_ref, bf16[32,8192]{1,0:T(8,128)(2,1)S(1)} %collective-permute-done.1.up_ref.up_own, bf16[32,8192]{1,0:T(8,128)(2,1)S(1)} %collective-permute-done.2.down_ref.down_own, ...), custom_call_target="tpu_custom_call" | custom-call | bytes 4194304 | tf_op jit(solution)/shard_map/pallas_call | solution.py:216
  (2 shorter events, 0.1 us)
Async XLA Ops:
  65.3 10.5 %copy-start = (bf16[2,1,32,8192]{3,2,1,0:T(8,128)(2,1)S(1)}, bf16[2,1,32,8192]{3,2,1,0:T(8,128)(2,1)}, u32[]{:S(2)}) copy-start(bf16[2,1,32,8192]{3,2,1,0:T(8,128)(2,1)} %param.3) | copy-start | bytes 3145732
  65.3 38.1 %all-to-all-start = ((bf16[16,2,64,512]{3,2,1,0:T(8,128)(2,1)}), bf16[16,2,64,512]{3,2,1,0:T(8,128)(2,1)S(1)}, u32[]{:S(2)}, u32[]{:S(2)}) async-start(bf16[16,2,64,512]{3,2,1,0:T(8,128)(2,1)} %shard_map.58), calls=%async_computation | async-start | bytes 4194304 | tf_op jit(solution)/shard_map/all_to_all | solution.py:258
  77.3 4.7 %collective-permute-start = (bf16[2,32,8192]{2,1,0:T(8,128)(2,1)S(1)}, bf16[2,32,8192]{2,1,0:T(8,128)(2,1)}, u32[]{:S(2)}, u32[]{:S(2)}) collective-permute-start(bf16[2,32,8192]{2,1,0:T(8,128)(2,1)S(1)} %pad_maximum_fusion), channel_id=1, source_target_pairs={{0,1},{1,0},{2,3},{3,2},{4,5},{5,4},{6,7},{7,6},{8,9},{9,8},{10,11... | collective-permute-start | bytes 3145736 | tf_op jit(solution)/shard_map/ppermute | solution.py:260
  108.3 32.9 %all-to-all-start.1 = ((bf16[16,2,64,512]{3,2,1,0:T(8,128)(2,1)}), bf16[16,2,64,512]{3,2,1,0:T(8,128)(2,1)S(1)}, u32[]{:S(2)}, u32[]{:S(2)}) async-start(bf16[16,2,64,512]{3,2,1,0:T(8,128)(2,1)} %get-tuple-element.16), calls=%async_computation.1 | async-start | bytes 4194304 | tf_op jit(solution)/shard_map/all_to_all | solution.py:264
  113.5 28.0 %collective-permute-start.1 = (bf16[32,8192]{1,0:T(8,128)(2,1)}, bf16[32,8192]{1,0:T(8,128)(2,1)S(1)}, u32[]{:S(2)}, u32[]{:S(2)}) collective-permute-start(bf16[32,8192]{1,0:T(8,128)(2,1)} %get-tuple-element.17), channel_id=1, source_target_pairs={{0,16},{1,17},{2,18},{3,19},{4,20},{5,21},{6,22},{7,23},{8,24},{9,... | collective-permute-start | bytes 1572872 | tf_op jit(solution)/shard_map/ppermute | solution.py:245
  114.8 26.7 %collective-permute-start.2 = (bf16[32,8192]{1,0:T(8,128)(2,1)}, bf16[32,8192]{1,0:T(8,128)(2,1)S(1)}, u32[]{:S(2)}, u32[]{:S(2)}) collective-permute-start(bf16[32,8192]{1,0:T(8,128)(2,1)} %get-tuple-element.18), channel_id=1, source_target_pairs={{16,0},{17,1},{18,2},{19,3},{20,4},{21,5},{22,6},{23,7},{24,8},{25... | collective-permute-start | bytes 1572872 | tf_op jit(solution)/shard_map/ppermute | solution.py:245
  116.1 25.4 %collective-permute-start.3 = (bf16[32,8192]{1,0:T(8,128)(2,1)}, bf16[32,8192]{1,0:T(8,128)(2,1)}, u32[]{:S(2)}, u32[]{:S(2)}) collective-permute-start(bf16[32,8192]{1,0:T(8,128)(2,1)} %get-tuple-element.19), channel_id=1, source_target_pairs={{0,17},{1,16},{2,19},{3,18},{4,21},{5,20},{6,23},{7,22},{8,25},{9,... | collective-permute-start | bytes 1572872 | tf_op jit(solution)/shard_map/ppermute | solution.py:245
  121.1 21.0 %collective-permute-start.4 = (bf16[32,8192]{1,0:T(8,128)(2,1)}, bf16[32,8192]{1,0:T(8,128)(2,1)}, u32[]{:S(2)}, u32[]{:S(2)}) collective-permute-start(bf16[32,8192]{1,0:T(8,128)(2,1)} %get-tuple-element.20), channel_id=1, source_target_pairs={{16,1},{17,0},{18,3},{19,2},{20,5},{21,4},{22,7},{23,6},{24,9},{25... | collective-permute-start | bytes 1572872 | tf_op jit(solution)/shard_map/ppermute | solution.py:245
  122.4 28.9 %collective-permute-start.6 = (bf16[32,8192]{1,0:T(8,128)(2,1)}, bf16[32,8192]{1,0:T(8,128)(2,1)}, u32[]{:S(2)}, u32[]{:S(2)}) collective-permute-start(bf16[32,8192]{1,0:T(8,128)(2,1)} %get-tuple-element.25), channel_id=1, source_target_pairs={{240,1},{241,0},{242,3},{243,2},{244,5},{245,4},{246,7},{247,6},{2... | collective-permute-start | bytes 1572872 | tf_op jit(solution)/shard_map/ppermute | solution.py:245
  142.2 31.8 %collective-permute-start.8 = (bf16[2,2,64,512]{3,2,1,0:T(8,128)(2,1)S(1)}, bf16[2,2,64,512]{3,2,1,0:T(8,128)(2,1)S(1)}, u32[]{:S(2)}, u32[]{:S(2)}) collective-permute-start(bf16[2,2,64,512]{3,2,1,0:T(8,128)(2,1)S(1)} %convert_element_type.11), channel_id=1, source_target_pairs={{0,496},{16,480},{32,464},{48,448},{64,432},{80,416},{96,400},{112... | collective-permute-start | bytes 786440 | tf_op jit(solution)/shard_map/ppermute | solution.py:278
  151.4 23.4 %collective-permute-start.7 = (bf16[32,8192]{1,0:T(8,128)(2,1)}, bf16[32,8192]{1,0:T(8,128)(2,1)S(1)}, u32[]{:S(2)}, u32[]{:S(2)}) collective-permute-start(bf16[32,8192]{1,0:T(8,128)(2,1)} %collective-permute-done.6), channel_id=1, source_target_pairs={{0,256},{1,257},{2,258},{3,259},{4,260},{5,261},{6,262},{7,263},{8... | collective-permute-start | bytes 1572872 | tf_op jit(solution)/shard_map/ppermute | solution.py:245
  153.9 20.9 %collective-permute-start.5 = (bf16[32,8192]{1,0:T(8,128)(2,1)}, bf16[32,8192]{1,0:T(8,128)(2,1)S(1)}, u32[]{:S(2)}, u32[]{:S(2)}) collective-permute-start(bf16[32,8192]{1,0:T(8,128)(2,1)} %shard_map.60), channel_id=1, source_target_pairs={{256,264},{257,265},{258,266},{259,267},{260,268},{261,269},{262,2... | collective-permute-start | bytes 1572872 | tf_op jit(solution)/shard_map/ppermute | solution.py:245

commit v8 on v6

--- a/solution.py
+++ b/solution.py
@@ -14,6 +14,10 @@
 OVER_TOKENS = (((0,), (0,)), ((), ()))
 PARAMS = pltpu.CompilerParams(vmem_limit_bytes=12 << 20)
 F32 = jnp.float32
+
+
+def in_hbm(array):
+    return pltpu.with_memory_space_constraint(array, pltpu.HBM)
 
 
 def spread_kernel(w_ref, out_ref, sems):
@@ -170,54 +174,78 @@
     )(section, up, down)
 
 
-def finish_kernel(
-    count, core_ref, at_ref, up_own, down_own, up_got, down_got, crossed_own, crossed_got, next_ref, prev_ref, sems
-):
-    core, section = core_ref[0], at_ref[0]
-    half = count // 2
-
-    def put(i, src, on_down, on_up):
-        @pl.when(core == 0)
-        def _():
-            pltpu.make_async_copy(src, on_down, sems.at[i]).start()
-
-        @pl.when(core != 0)
-        def _():
-            pltpu.make_async_copy(src, on_up, sems.at[i]).start()
-
-    places = (
+def places(next_ref, prev_ref):
+    return (
         (next_ref.at[0], prev_ref.at[1]),
         (prev_ref.at[0], next_ref.at[1]),
         (prev_ref.at[1], next_ref.at[0]),
         (next_ref.at[1], prev_ref.at[0]),
     )
-    for way, position, own, got in ((0, half, up_own, up_got), (1, half - 1, down_own, down_got)):
+
+
+def put(core, src, place, sem):
+    for on, dst in enumerate(place):
+        @pl.when(core == on)
+        def _():
+            pltpu.make_async_copy(src, dst, sem).start()
+
+
+def assemble_kernel(core_ref, up_own, down_own, up_got, down_got, next_ref, prev_ref, stage, loads, sems):
+    core = core_ref[0]
+    where = places(next_ref, prev_ref)
+    staging = [pltpu.make_async_copy(src, stage.at[i], loads.at[i]) for i, src in enumerate((up_got, down_got))]
+    for copy in staging:
+        copy.start()
+    for i, src in enumerate((up_own, down_own)):
+        put(core, src, where[i], sems.at[i])
+    for i, copy in enumerate(staging):
+        copy.wait()
+        put(core, stage.at[i], where[2 + i], sems.at[2 + i])
+    for i in range(4):
+        pltpu.make_async_copy(stage.at[0], next_ref.at[0], sems.at[i]).wait()
+
+
+def assemble(core, up_own, down_own, up_got, down_got):
+    pair = pltpu.HBM((2,) + up_own.shape, up_own.dtype)
+    return pl.pallas_call(
+        assemble_kernel,
+        out_shape=(pair, pair),
+        in_specs=[SCALARS, WHOLE, WHOLE, ANYWHERE, ANYWHERE],
+        out_specs=(ANYWHERE,) * 2,
+        scratch_shapes=[
+            pltpu.VMEM((2,) + up_own.shape, up_own.dtype),
+            pltpu.SemaphoreType.DMA((2,)),
+            pltpu.SemaphoreType.DMA((4,)),
+        ],
+        compiler_params=PARAMS,
+        cost_estimate=pl.CostEstimate(flops=0, bytes_accessed=16 * up_own.size, transcendentals=0),
+    )(core, up_own, down_own, in_hbm(up_got), in_hbm(down_got))
+
+
+def amend_kernel(count, core_ref, at_ref, own_ref, got_ref, next_in, prev_in, next_ref, prev_ref, sems):
+    core, section = core_ref[0], at_ref[0]
+    where = places(next_ref, prev_ref)
+    for way, position in ((0, count // 2), (1, count // 2 - 1)):
         @pl.when(section == position)
         def _():
-            put(way, crossed_own, *places[way])
-            put(way + 2, crossed_got, *places[way + 2])
-
-        @pl.when(section != position)
-        def _():
-            put(way, own, *places[way])
-            put(way + 2, got, *places[way + 2])
-
-    for i in range(4):
-        pltpu.make_async_copy(crossed_own, next_ref.at[0], sems.at[i]).wait()
-
-
-def finish(count, core, section, *arrived):
-    tokens, model = arrived[0].shape
-    pair = pltpu.HBM((2, tokens, model), arrived[0].dtype)
-    return pl.pallas_call(
-        functools.partial(finish_kernel, count),
+            put(core, own_ref, where[way], sems.at[0])
+            put(core, got_ref, where[2 + way], sems.at[1])
+            pltpu.make_async_copy(own_ref, next_ref.at[0], sems.at[0]).wait()
+            pltpu.make_async_copy(got_ref, next_ref.at[0], sems.at[1]).wait()
+
+
+def amend(count, core, section, crossed_own, crossed_got, next_inputs, prev_grads):
+    pair = pltpu.HBM(next_inputs.shape, next_inputs.dtype)
+    return pl.pallas_call(
+        functools.partial(amend_kernel, count),
         out_shape=(pair, pair),
-        in_specs=[SCALARS] * 2 + [ANYWHERE] * 6,
+        in_specs=[SCALARS] * 2 + [WHOLE] * 2 + [ANYWHERE] * 2,
         out_specs=(ANYWHERE,) * 2,
-        scratch_shapes=[pltpu.SemaphoreType.DMA((4,))],
-        compiler_params=PARAMS,
-        cost_estimate=pl.CostEstimate(flops=0, bytes_accessed=16 * tokens * model, transcendentals=0),
-    )(core, section, *arrived)
+        scratch_shapes=[pltpu.SemaphoreType.DMA((2,))],
+        input_output_aliases={4: 0, 5: 1},
+        compiler_params=PARAMS,
+        cost_estimate=pl.CostEstimate(flops=0, bytes_accessed=8 * crossed_own.size, transcendentals=0),
+    )(core, section, crossed_own, crossed_got, in_hbm(next_inputs), in_hbm(prev_grads))
 
 
 def add_kernel(sums_ref, partner_ref, out_ref):
@@ -254,7 +282,7 @@
     gathered = lax.all_to_all(spread(adapters[:, 0], n_dp), "dp", 0, 0, tiled=True)
     given = jnp.stack([jnp.where(is_down, inputs[1], inputs[0]), jnp.where(is_down, grads[1], grads[0])])
     taken = lax.ppermute(given, "dp", swap)
-    x, g, taken = (pltpu.with_memory_space_constraint(a, pltpu.HBM) for a in (inputs, grads, taken))
+    x, g, taken = (in_hbm(a) for a in (inputs, grads, taken))
     parts, up_own, down_own, up_send, down_send, edge = adapter(count, core, section, x, g, taken, gathered)
 
     terms = lax.all_to_all(parts, "dp", 0, 0, tiled=True)
@@ -274,10 +302,10 @@
     partner = lax.ppermute(narrow, "section", [(i, count - 1 - i) for i in range(count)])
     crossed_own = moved(crossing(count, section, up_own, down_own), [(half, half, group), (half - 1, half - 1, group)], n_dp)
     crossed_got = moved(near, [(0, half, 0), (count - 1, half - 1, 0)], n_dp)
+    next_inputs, prev_grads = assemble(core, up_own, down_own, up_got, down_got)
+    partner, next_inputs, prev_grads = lax.optimization_barrier((partner, next_inputs, prev_grads))
     summed = add_mirrored(sums, partner)
-    next_inputs, prev_grads = finish(
-        count, core, section, up_own, down_own, up_got, down_got, crossed_own, crossed_got
-    )
+    next_inputs, prev_grads = amend(count, core, section, crossed_own, crossed_got, next_inputs, prev_grads)
     return (next_inputs[:, None], prev_grads[:, None], summed[:, None])
 
 

time: 117 us -> 114 us (0.974)
  waiting for transfers between devices: 62 us -> 59 us
  other arithmetic: 3.39 us -> 1.73 us
    ppermute x1, waiting for transfers between devices: 19.9 us -> 16.9 us  [shards(): lax.ppermute(narrow, 'section', [(i, count - 1 - i) for i in range(count)])]
    reduce_sum x1, other arithmetic: 1.95 us -> 0.29 us  [shards(): jnp.sum(terms.reshape((n_dp // 2, 2) + terms.shape[1:]).astype(F32), axis=0)]
    pallas_call x1 -> x2, Pallas kernels: 1.35 us -> 2.45 us  [the longest x1 2.43 us: assemble(): pl.pallas_call(assemble_kernel, out_shape=(pair, pair), in_specs=[SCALARS...]
  transfers between devices with their start and end apart: 11 -> 11, of which waited for: 4 -> 5; matrix products, arithmetic and copies ran while one was open for 3% -> 2% of each run, Pallas kernels for 1% -> 3%
where the time goes in v8:
time: 114 us; the launch traced here: 112 us
  waiting for transfers between devices  59 us (52%)
  starting transfers between devices  40.4 us (35%)
  Pallas kernels  9.42 us (8%)
  other arithmetic  1.73 us (2%)
    all_to_all x1, waiting for transfers between devices, shards(): lax.all_to_all(spread(adapters[:, 0], n_dp), 'dp', 0, 0, tiled=True)  21.5 us
    all_to_all x1, waiting for transfers between devices, shards(): terms = lax.all_to_all(parts, 'dp', 0, 0, tiled=True)  17.4 us
    ppermute x1, waiting for transfers between devices, shards(): lax.ppermute(narrow, 'section', [(i, count - 1 - i) for i in range(count)])  16.9 us
    ppermute x7, starting transfers between devices, moved(): return lax.ppermute(value, ('section', 'dp'), pairs)  13.4 us
    all_to_all x1, starting transfers between devices, shards(): lax.all_to_all(spread(adapters[:, 0], n_dp), 'dp', 0, 0, tiled=True)  10.5 us
    ppermute x1, starting transfers between devices, shards(): lax.ppermute(narrow, 'section', [(i, count - 1 - i) for i in range(count)])  9.16 us
    all_to_all x1, starting transfers between devices, shards(): terms = lax.all_to_all(parts, 'dp', 0, 0, tiled=True)  5.17 us
    pallas_call x1, Pallas kernels, adapter(): pl.pallas_call(functools.partial(adapter_kernel, count), out_shape=(pltpu...  4.71 us
  transfers between devices with their start and end apart: 11, of which 5 were waited for; matrix products, arithmetic and copies ran while one was open for 2% of the time, Pallas kernels for 3%

profile of v8, /device:TPU:1, one launch (start us, length us, event | category | flops | bytes accessed | tf_op | source)
XLA Modules:
  0.0 112.4 jit_solution(6471953760399660576)
XLA Ops:
  0.6 0.0 copy-start
  0.6 0.9 copy-done
  1.6 1.4 %shard_map.58 = bf16[16,2,64,512]{3,2,1,0:T(8,128)(2,1)} custom-call(bf16[2,2,64,512]{3,2,1,0:T(8,128)(2,1)S(1)} %bitcast.20), custom_call_target="tpu_custom_call" | custom-call | bytes 2097152 | tf_op jit(solution)/shard_map/pallas_call | solution.py:34
  3.0 0.0 copy-start.1
  3.0 10.5 %all-to-all-start = ((bf16[16,2,64,512]{3,2,1,0:T(8,128)(2,1)}), bf16[16,2,64,512]{3,2,1,0:T(8,128)(2,1)S(1)}, u32[]{:S(2)}, u32[]{:S(2)}) async-start(bf16[16,2,64,512]{3,2,1,0:T(8,128)(2,1)} %shard_map.58), calls=%async_computation | async-start | bytes 4194304 | tf_op jit(solution)/shard_map/all_to_all | solution.py:282
  13.5 0.0 copy-done.1
  13.5 1.3 %select_bitcast_fusion = (bf16[1,32,8192]{2,1,0:T(8,128)(2,1)S(1)}, bf16[1,32,8192]{2,1,0:T(8,128)(2,1)S(1)}) fusion(bf16[2,1,32,8192]{3,2,1,0:T(8,128)(2,1)} %param.4, pred[]{:T(512)S(6)} %eq.5, bf16[2,1,32,8192]{3,2,1,0:T(8,128)(2,1)S(1)} %copy-done.1), kind=kLoop, calls=%fused_computation.2 | loop fusion | flops 524288 | bytes 3145729 | tf_op jit(solution)/shard_map/jit(_where)/select_n | solution.py:283
  14.8 0.1 pad_maximum_fusion
  15.0 2.1 %collective-permute-start = (bf16[2,32,8192]{2,1,0:T(8,128)(2,1)S(1)}, bf16[2,32,8192]{2,1,0:T(8,128)(2,1)}, u32[]{:S(2)}, u32[]{:S(2)}) collective-permute-start(bf16[2,32,8192]{2,1,0:T(8,128)(2,1)S(1)} %pad_maximum_fusion), channel_id=1, source_target_pairs={{0,1},{1,0},{2,3},{3,2},{4,5},{5,4},{6,7},{7,6},{8,9},{9,8},{10,11... | collective-permute-start | bytes 3145736 | tf_op jit(solution)/shard_map/ppermute | solution.py:284
  17.1 2.5 %collective-permute-done.taken_ref = bf16[2,32,8192]{2,1,0:T(8,128)(2,1)} collective-permute-done((bf16[2,32,8192]{2,1,0:T(8,128)(2,1)S(1)}, bf16[2,32,8192]{2,1,0:T(8,128)(2,1)}, u32[]{:S(2)}, u32[]{:S(2)}) %collective-permute-start) | collective-permute-done | bytes 1048608 | tf_op jit(solution)/shard_map/ppermute | solution.py:284
  19.6 21.5 %all-to-all-done.w_ref = bf16[16,2,64,512]{3,2,1,0:T(8,128)(2,1)S(1)} async-done(((bf16[16,2,64,512]{3,2,1,0:T(8,128)(2,1)}), bf16[16,2,64,512]{3,2,1,0:T(8,128)(2,1)S(1)}, u32[]{:S(2)}, u32[]{:S(2)}) %all-to-all-start) | async-done | bytes 2097184 | tf_op jit(solution)/shard_map/all_to_all | solution.py:282
  41.1 4.7 %shard_map.59 = (bf16[16,2,64,512]{3,2,1,0:T(8,128)(2,1)}, bf16[32,8192]{1,0:T(8,128)(2,1)}, bf16[32,8192]{1,0:T(8,128)(2,1)}, bf16[32,8192]{1,0:T(8,128)(2,1)},...) custom-call(s32[1]{0:T(128)} %bitcast.core_ref, s32[1]{0:T(128)} %bitcast.1.at_ref, bf16[2,32,8192]{2,1,0:T(8,128)(2,1)} %bitcast.22, ...), custom_call_target="tpu_custom_call" | custom-call | flops 402653184 | bytes 12582912 | tf_op jit(solution)/shard_map/pallas_call | solution.py:136
  45.8 5.2 %all-to-all-start.1 = ((bf16[16,2,64,512]{3,2,1,0:T(8,128)(2,1)}), bf16[16,2,64,512]{3,2,1,0:T(8,128)(2,1)S(1)}, u32[]{:S(2)}, u32[]{:S(2)}) async-start(bf16[16,2,64,512]{3,2,1,0:T(8,128)(2,1)} %get-tuple-element.21), calls=%async_computation.1 | async-start | bytes 4194304 | tf_op jit(solution)/shard_map/all_to_all | solution.py:288
  51.0 1.3 %collective-permute-start.1 = (bf16[32,8192]{1,0:T(8,128)(2,1)}, bf16[32,8192]{1,0:T(8,128)(2,1)S(1)}, u32[]{:S(2)}, u32[]{:S(2)}) collective-permute-start(bf16[32,8192]{1,0:T(8,128)(2,1)} %get-tuple-element.22), channel_id=1, source_target_pairs={{0,16},{1,17},{2,18},{3,19},{4,20},{5,21},{6,22},{7,23},{8,24},{9,... | collective-permute-start | bytes 1572872 | tf_op jit(solution)/shard_map/ppermute | solution.py:269
  52.3 1.3 %collective-permute-start.2 = (bf16[32,8192]{1,0:T(8,128)(2,1)}, bf16[32,8192]{1,0:T(8,128)(2,1)S(1)}, u32[]{:S(2)}, u32[]{:S(2)}) collective-permute-start(bf16[32,8192]{1,0:T(8,128)(2,1)} %get-tuple-element.23), channel_id=1, source_target_pairs={{16,0},{17,1},{18,2},{19,3},{20,4},{21,5},{22,6},{23,7},{24,8},{25... | collective-permute-start | bytes 1572872 | tf_op jit(solution)/shard_map/ppermute | solution.py:269
  53.6 5.1 %collective-permute-start.3 = (bf16[32,8192]{1,0:T(8,128)(2,1)}, bf16[32,8192]{1,0:T(8,128)(2,1)}, u32[]{:S(2)}, u32[]{:S(2)}) collective-permute-start(bf16[32,8192]{1,0:T(8,128)(2,1)} %get-tuple-element.24), channel_id=1, source_target_pairs={{0,17},{1,16},{2,19},{3,18},{4,21},{5,20},{6,23},{7,22},{8,25},{9,... | collective-permute-start | bytes 1572872 | tf_op jit(solution)/shard_map/ppermute | solution.py:269
  58.7 1.3 %collective-permute-start.4 = (bf16[32,8192]{1,0:T(8,128)(2,1)}, bf16[32,8192]{1,0:T(8,128)(2,1)}, u32[]{:S(2)}, u32[]{:S(2)}) collective-permute-start(bf16[32,8192]{1,0:T(8,128)(2,1)} %get-tuple-element.25), channel_id=1, source_target_pairs={{16,1},{17,0},{18,3},{19,2},{20,5},{21,4},{22,7},{23,6},{24,9},{25... | collective-permute-start | bytes 1572872 | tf_op jit(solution)/shard_map/ppermute | solution.py:269
  60.0 1.3 %collective-permute-start.6 = (bf16[32,8192]{1,0:T(8,128)(2,1)}, bf16[32,8192]{1,0:T(8,128)(2,1)}, u32[]{:S(2)}, u32[]{:S(2)}) collective-permute-start(bf16[32,8192]{1,0:T(8,128)(2,1)} %get-tuple-element.28), channel_id=1, source_target_pairs={{240,1},{241,0},{242,3},{243,2},{244,5},{245,4},{246,7},{247,6},{2... | collective-permute-start | bytes 1572872 | tf_op jit(solution)/shard_map/ppermute | solution.py:269
  61.3 17.4 %all-to-all-done.1 = bf16[16,2,64,512]{3,2,1,0:T(8,128)(2,1)S(1)} async-done(((bf16[16,2,64,512]{3,2,1,0:T(8,128)(2,1)}), bf16[16,2,64,512]{3,2,1,0:T(8,128)(2,1)S(1)}, u32[]{:S(2)}, u32[]{:S(2)}) %all-to-all-start.1) | async-done | bytes 2097184 | tf_op jit(solution)/shard_map/all_to_all | solution.py:288
  78.7 0.3 convert_reduce_fusion.sums_ref
  79.0 0.0 collective-permute-done.1.up_ref.up_own
  79.0 0.0 collective-permute-done.2.down_ref.down_own
  79.0 0.0 collective-permute-done.3.up_got
  79.0 0.7 collective-permute-done.4.down_got
  79.7 9.2 %collective-permute-start.8 = (bf16[2,2,64,512]{3,2,1,0:T(8,128)(2,1)S(1)}, bf16[2,2,64,512]{3,2,1,0:T(8,128)(2,1)S(1)}, u32[]{:S(2)}, u32[]{:S(2)}) collective-permute-start(bf16[2,2,64,512]{3,2,1,0:T(8,128)(2,1)S(1)} %convert_element_type.11), channel_id=1, source_target_pairs={{0,496},{16,480},{32,464},{48,448},{64,432},{80,416},{96,400},{112... | collective-permute-start | bytes 786440 | tf_op jit(solution)/shard_map/ppermute | solution.py:302
  88.9 0.0 collective-permute-done.6
  88.9 2.5 %collective-permute-start.7 = (bf16[32,8192]{1,0:T(8,128)(2,1)}, bf16[32,8192]{1,0:T(8,128)(2,1)S(1)}, u32[]{:S(2)}, u32[]{:S(2)}) collective-permute-start(bf16[32,8192]{1,0:T(8,128)(2,1)} %collective-permute-done.6), channel_id=1, source_target_pairs={{0,256},{1,257},{2,258},{3,259},{4,260},{5,261},{6,262},{7,263},{8... | collective-permute-start | bytes 1572872 | tf_op jit(solution)/shard_map/ppermute | solution.py:269
  91.4 0.7 collective-permute-start.5
  92.1 2.4 %shard_map.61 = (bf16[2,32,8192]{2,1,0:T(8,128)(2,1)}, bf16[2,32,8192]{2,1,0:T(8,128)(2,1)}) custom-call(s32[1]{0:T(128)} %bitcast.core_ref, bf16[32,8192]{1,0:T(8,128)(2,1)S(1)} %collective-permute-done.1.up_ref.up_own, bf16[32,8192]{1,0:T(8,128)(2,1)S(1)} %collective-permute-done.2.down_ref.down_own, bf16[32,8192]{1,0:T(8,128)(2,1)} %collective-permute-done.3.up_got, ...), custom_call_target="tpu_custom_call" | custom-call | bytes 4194304 | tf_op jit(solution)/shard_map/pallas_call | solution.py:210
  94.6 16.9 %collective-permute-done.8.partner_ref = bf16[2,2,64,512]{3,2,1,0:T(8,128)(2,1)S(1)} collective-permute-done((bf16[2,2,64,512]{3,2,1,0:T(8,128)(2,1)S(1)}, bf16[2,2,64,512]{3,2,1,0:T(8,128)(2,1)S(1)}, u32[]{:S(2)}, u32[]{:S(2)}) %collective-permute-start.8) | collective-permute-done | bytes 262176 | tf_op jit(solution)/shard_map/ppermute | solution.py:302
  111.5 0.8 shard_map.63
  112.3 0.0 collective-permute-done.7.got_ref
  112.3 0.0 collective-permute-done.5.own_ref
  (3 shorter events, 0.1 us)
Async XLA Ops:
  0.6 1.0 copy-start
  3.0 10.5 %copy-start.1 = (bf16[2,1,32,8192]{3,2,1,0:T(8,128)(2,1)S(1)}, bf16[2,1,32,8192]{3,2,1,0:T(8,128)(2,1)}, u32[]{:S(2)}) copy-start(bf16[2,1,32,8192]{3,2,1,0:T(8,128)(2,1)} %param.3) | copy-start | bytes 3145732
  3.0 38.1 %all-to-all-start = ((bf16[16,2,64,512]{3,2,1,0:T(8,128)(2,1)}), bf16[16,2,64,512]{3,2,1,0:T(8,128)(2,1)S(1)}, u32[]{:S(2)}, u32[]{:S(2)}) async-start(bf16[16,2,64,512]{3,2,1,0:T(8,128)(2,1)} %shard_map.58), calls=%async_computation | async-start | bytes 4194304 | tf_op jit(solution)/shard_map/all_to_all | solution.py:282
  15.0 4.7 %collective-permute-start = (bf16[2,32,8192]{2,1,0:T(8,128)(2,1)S(1)}, bf16[2,32,8192]{2,1,0:T(8,128)(2,1)}, u32[]{:S(2)}, u32[]{:S(2)}) collective-permute-start(bf16[2,32,8192]{2,1,0:T(8,128)(2,1)S(1)} %pad_maximum_fusion), channel_id=1, source_target_pairs={{0,1},{1,0},{2,3},{3,2},{4,5},{5,4},{6,7},{7,6},{8,9},{9,8},{10,11... | collective-permute-start | bytes 3145736 | tf_op jit(solution)/shard_map/ppermute | solution.py:284
  45.8 32.9 %all-to-all-start.1 = ((bf16[16,2,64,512]{3,2,1,0:T(8,128)(2,1)}), bf16[16,2,64,512]{3,2,1,0:T(8,128)(2,1)S(1)}, u32[]{:S(2)}, u32[]{:S(2)}) async-start(bf16[16,2,64,512]{3,2,1,0:T(8,128)(2,1)} %get-tuple-element.21), calls=%async_computation.1 | async-start | bytes 4194304 | tf_op jit(solution)/shard_map/all_to_all | solution.py:288
  51.0 28.0 %collective-permute-start.1 = (bf16[32,8192]{1,0:T(8,128)(2,1)}, bf16[32,8192]{1,0:T(8,128)(2,1)S(1)}, u32[]{:S(2)}, u32[]{:S(2)}) collective-permute-start(bf16[32,8192]{1,0:T(8,128)(2,1)} %get-tuple-element.22), channel_id=1, source_target_pairs={{0,16},{1,17},{2,18},{3,19},{4,20},{5,21},{6,22},{7,23},{8,24},{9,... | collective-permute-start | bytes 1572872 | tf_op jit(solution)/shard_map/ppermute | solution.py:269
  52.3 26.7 %collective-permute-start.2 = (bf16[32,8192]{1,0:T(8,128)(2,1)}, bf16[32,8192]{1,0:T(8,128)(2,1)S(1)}, u32[]{:S(2)}, u32[]{:S(2)}) collective-permute-start(bf16[32,8192]{1,0:T(8,128)(2,1)} %get-tuple-element.23), channel_id=1, source_target_pairs={{16,0},{17,1},{18,2},{19,3},{20,4},{21,5},{22,6},{23,7},{24,8},{25... | collective-permute-start | bytes 1572872 | tf_op jit(solution)/shard_map/ppermute | solution.py:269
  53.6 25.4 %collective-permute-start.3 = (bf16[32,8192]{1,0:T(8,128)(2,1)}, bf16[32,8192]{1,0:T(8,128)(2,1)}, u32[]{:S(2)}, u32[]{:S(2)}) collective-permute-start(bf16[32,8192]{1,0:T(8,128)(2,1)} %get-tuple-element.24), channel_id=1, source_target_pairs={{0,17},{1,16},{2,19},{3,18},{4,21},{5,20},{6,23},{7,22},{8,25},{9,... | collective-permute-start | bytes 1572872 | tf_op jit(solution)/shard_map/ppermute | solution.py:269
  58.7 21.0 %collective-permute-start.4 = (bf16[32,8192]{1,0:T(8,128)(2,1)}, bf16[32,8192]{1,0:T(8,128)(2,1)}, u32[]{:S(2)}, u32[]{:S(2)}) collective-permute-start(bf16[32,8192]{1,0:T(8,128)(2,1)} %get-tuple-element.25), channel_id=1, source_target_pairs={{16,1},{17,0},{18,3},{19,2},{20,5},{21,4},{22,7},{23,6},{24,9},{25... | collective-permute-start | bytes 1572872 | tf_op jit(solution)/shard_map/ppermute | solution.py:269
  60.0 28.9 %collective-permute-start.6 = (bf16[32,8192]{1,0:T(8,128)(2,1)}, bf16[32,8192]{1,0:T(8,128)(2,1)}, u32[]{:S(2)}, u32[]{:S(2)}) collective-permute-start(bf16[32,8192]{1,0:T(8,128)(2,1)} %get-tuple-element.28), channel_id=1, source_target_pairs={{240,1},{241,0},{242,3},{243,2},{244,5},{245,4},{246,7},{247,6},{2... | collective-permute-start | bytes 1572872 | tf_op jit(solution)/shard_map/ppermute | solution.py:269
  79.7 31.8 %collective-permute-start.8 = (bf16[2,2,64,512]{3,2,1,0:T(8,128)(2,1)S(1)}, bf16[2,2,64,512]{3,2,1,0:T(8,128)(2,1)S(1)}, u32[]{:S(2)}, u32[]{:S(2)}) collective-permute-start(bf16[2,2,64,512]{3,2,1,0:T(8,128)(2,1)S(1)} %convert_element_type.11), channel_id=1, source_target_pairs={{0,496},{16,480},{32,464},{48,448},{64,432},{80,416},{96,400},{112... | collective-permute-start | bytes 786440 | tf_op jit(solution)/shard_map/ppermute | solution.py:302
  88.9 23.4 %collective-permute-start.7 = (bf16[32,8192]{1,0:T(8,128)(2,1)}, bf16[32,8192]{1,0:T(8,128)(2,1)S(1)}, u32[]{:S(2)}, u32[]{:S(2)}) collective-permute-start(bf16[32,8192]{1,0:T(8,128)(2,1)} %collective-permute-done.6), channel_id=1, source_target_pairs={{0,256},{1,257},{2,258},{3,259},{4,260},{5,261},{6,262},{7,263},{8... | collective-permute-start | bytes 1572872 | tf_op jit(solution)/shard_map/ppermute | solution.py:269
  91.4 20.9 %collective-permute-start.5 = (bf16[32,8192]{1,0:T(8,128)(2,1)}, bf16[32,8192]{1,0:T(8,128)(2,1)S(1)}, u32[]{:S(2)}, u32[]{:S(2)}) collective-permute-start(bf16[32,8192]{1,0:T(8,128)(2,1)} %shard_map.60), channel_id=1, source_target_pairs={{256,264},{257,265},{258,266},{259,267},{260,268},{261,269},{262,2... | collective-permute-start | bytes 1572872 | tf_op jit(solution)/shard_map/ppermute | solution.py:269

commit v9 on v8

--- a/solution.py
+++ b/solution.py
@@ -298,8 +298,9 @@
     down_got = moved(down_send, [(a, b, 1) for a, b in downs], n_dp)
 
     narrow = sums.astype(jnp.bfloat16)
-    narrow, up_own, down_own, up_got, down_got = lax.optimization_barrier((narrow, up_own, down_own, up_got, down_got))
+    narrow, up_own, down_own = lax.optimization_barrier((narrow, up_own, down_own))
     partner = lax.ppermute(narrow, "section", [(i, count - 1 - i) for i in range(count)])
+    near, up_got, down_got = lax.optimization_barrier((near, up_got, down_got))
     crossed_own = moved(crossing(count, section, up_own, down_own), [(half, half, group), (half - 1, half - 1, group)], n_dp)
     crossed_got = moved(near, [(0, half, 0), (count - 1, half - 1, 0)], n_dp)
     next_inputs, prev_grads = assemble(core, up_own, down_own, up_got, down_got)

time: 114 us -> 114 us (level)
  transfers between devices with their start and end apart: 11 -> 11, of which waited for: 5 -> 4; matrix products, arithmetic and copies ran while one was open for 2% -> 2% of each run, Pallas kernels for 3% -> 3%
where the time goes in v9:
time: 114 us; the launch traced here: 113 us
  waiting for transfers between devices  58.7 us (51%)
  starting transfers between devices  41.3 us (36%)
  Pallas kernels  9.42 us (8%)
  other arithmetic  1.73 us (2%)
    all_to_all x1, waiting for transfers between devices, shards(): lax.all_to_all(spread(adapters[:, 0], n_dp), 'dp', 0, 0, tiled=True)  21.5 us
    ppermute x1, waiting for transfers between devices, shards(): lax.ppermute(narrow, 'section', [(i, count - 1 - i) for i in range(count)])  17.5 us
    all_to_all x1, waiting for transfers between devices, shards(): terms = lax.all_to_all(parts, 'dp', 0, 0, tiled=True)  17.2 us
    ppermute x7, starting transfers between devices, moved(): return lax.ppermute(value, ('section', 'dp'), pairs)  13.6 us
    all_to_all x1, starting transfers between devices, shards(): lax.all_to_all(spread(adapters[:, 0], n_dp), 'dp', 0, 0, tiled=True)  10.5 us
    ppermute x1, starting transfers between devices, shards(): lax.ppermute(narrow, 'section', [(i, count - 1 - i) for i in range(count)])  9.82 us
    all_to_all x1, starting transfers between devices, shards(): terms = lax.all_to_all(parts, 'dp', 0, 0, tiled=True)  5.17 us
    pallas_call x1, Pallas kernels, adapter(): pl.pallas_call(functools.partial(adapter_kernel, count), out_shape=(pltpu...  4.71 us
  transfers between devices with their start and end apart: 11, of which 4 were waited for; matrix products, arithmetic and copies ran while one was open for 2% of the time, Pallas kernels for 3%

profile of v9, /device:TPU:1, one launch (start us, length us, event | category | flops | bytes accessed | tf_op | source)
XLA Modules:
  0.0 112.9 jit_solution(11462678710475376755)
XLA Ops:
  0.6 0.0 copy-start
  0.6 0.9 copy-done
  1.6 1.4 %shard_map.58 = bf16[16,2,64,512]{3,2,1,0:T(8,128)(2,1)} custom-call(bf16[2,2,64,512]{3,2,1,0:T(8,128)(2,1)S(1)} %bitcast.20), custom_call_target="tpu_custom_call" | custom-call | bytes 2097152 | tf_op jit(solution)/shard_map/pallas_call | solution.py:34
  3.0 0.0 copy-start.1
  3.0 10.5 %all-to-all-start = ((bf16[16,2,64,512]{3,2,1,0:T(8,128)(2,1)}), bf16[16,2,64,512]{3,2,1,0:T(8,128)(2,1)S(1)}, u32[]{:S(2)}, u32[]{:S(2)}) async-start(bf16[16,2,64,512]{3,2,1,0:T(8,128)(2,1)} %shard_map.58), calls=%async_computation | async-start | bytes 4194304 | tf_op jit(solution)/shard_map/all_to_all | solution.py:282
  13.5 0.0 copy-done.1
  13.5 1.3 %select_bitcast_fusion = (bf16[1,32,8192]{2,1,0:T(8,128)(2,1)S(1)}, bf16[1,32,8192]{2,1,0:T(8,128)(2,1)S(1)}) fusion(bf16[2,1,32,8192]{3,2,1,0:T(8,128)(2,1)} %param.4, pred[]{:T(512)S(6)} %eq.5, bf16[2,1,32,8192]{3,2,1,0:T(8,128)(2,1)S(1)} %copy-done.1), kind=kLoop, calls=%fused_computation.2 | loop fusion | flops 524288 | bytes 3145729 | tf_op jit(solution)/shard_map/jit(_where)/select_n | solution.py:283
  14.8 0.1 pad_maximum_fusion
  15.0 2.1 %collective-permute-start = (bf16[2,32,8192]{2,1,0:T(8,128)(2,1)S(1)}, bf16[2,32,8192]{2,1,0:T(8,128)(2,1)}, u32[]{:S(2)}, u32[]{:S(2)}) collective-permute-start(bf16[2,32,8192]{2,1,0:T(8,128)(2,1)S(1)} %pad_maximum_fusion), channel_id=1, source_target_pairs={{0,1},{1,0},{2,3},{3,2},{4,5},{5,4},{6,7},{7,6},{8,9},{9,8},{10,11... | collective-permute-start | bytes 3145736 | tf_op jit(solution)/shard_map/ppermute | solution.py:284
  17.1 2.5 %collective-permute-done.taken_ref = bf16[2,32,8192]{2,1,0:T(8,128)(2,1)} collective-permute-done((bf16[2,32,8192]{2,1,0:T(8,128)(2,1)S(1)}, bf16[2,32,8192]{2,1,0:T(8,128)(2,1)}, u32[]{:S(2)}, u32[]{:S(2)}) %collective-permute-start) | collective-permute-done | bytes 1048608 | tf_op jit(solution)/shard_map/ppermute | solution.py:284
  19.6 21.5 %all-to-all-done.w_ref = bf16[16,2,64,512]{3,2,1,0:T(8,128)(2,1)S(1)} async-done(((bf16[16,2,64,512]{3,2,1,0:T(8,128)(2,1)}), bf16[16,2,64,512]{3,2,1,0:T(8,128)(2,1)S(1)}, u32[]{:S(2)}, u32[]{:S(2)}) %all-to-all-start) | async-done | bytes 2097184 | tf_op jit(solution)/shard_map/all_to_all | solution.py:282
  41.1 4.7 %shard_map.59 = (bf16[16,2,64,512]{3,2,1,0:T(8,128)(2,1)}, bf16[32,8192]{1,0:T(8,128)(2,1)}, bf16[32,8192]{1,0:T(8,128)(2,1)}, bf16[32,8192]{1,0:T(8,128)(2,1)},...) custom-call(s32[1]{0:T(128)} %bitcast.core_ref, s32[1]{0:T(128)} %bitcast.1.at_ref, bf16[2,32,8192]{2,1,0:T(8,128)(2,1)} %bitcast.22, ...), custom_call_target="tpu_custom_call" | custom-call | flops 402653184 | bytes 12582912 | tf_op jit(solution)/shard_map/pallas_call | solution.py:136
  45.8 5.2 %all-to-all-start.1 = ((bf16[16,2,64,512]{3,2,1,0:T(8,128)(2,1)}), bf16[16,2,64,512]{3,2,1,0:T(8,128)(2,1)S(1)}, u32[]{:S(2)}, u32[]{:S(2)}) async-start(bf16[16,2,64,512]{3,2,1,0:T(8,128)(2,1)} %get-tuple-element.22), calls=%async_computation.1 | async-start | bytes 4194304 | tf_op jit(solution)/shard_map/all_to_all | solution.py:288
  51.0 1.3 %collective-permute-start.1 = (bf16[32,8192]{1,0:T(8,128)(2,1)}, bf16[32,8192]{1,0:T(8,128)(2,1)S(1)}, u32[]{:S(2)}, u32[]{:S(2)}) collective-permute-start(bf16[32,8192]{1,0:T(8,128)(2,1)} %get-tuple-element.23), channel_id=1, source_target_pairs={{0,16},{1,17},{2,18},{3,19},{4,20},{5,21},{6,22},{7,23},{8,24},{9,... | collective-permute-start | bytes 1572872 | tf_op jit(solution)/shard_map/ppermute | solution.py:269
  52.3 1.3 %collective-permute-start.2 = (bf16[32,8192]{1,0:T(8,128)(2,1)}, bf16[32,8192]{1,0:T(8,128)(2,1)S(1)}, u32[]{:S(2)}, u32[]{:S(2)}) collective-permute-start(bf16[32,8192]{1,0:T(8,128)(2,1)} %get-tuple-element.24), channel_id=1, source_target_pairs={{16,0},{17,1},{18,2},{19,3},{20,4},{21,5},{22,6},{23,7},{24,8},{25... | collective-permute-start | bytes 1572872 | tf_op jit(solution)/shard_map/ppermute | solution.py:269
  53.6 1.3 %collective-permute-start.4 = (bf16[32,8192]{1,0:T(8,128)(2,1)}, bf16[32,8192]{1,0:T(8,128)(2,1)}, u32[]{:S(2)}, u32[]{:S(2)}) collective-permute-start(bf16[32,8192]{1,0:T(8,128)(2,1)} %get-tuple-element.27), channel_id=1, source_target_pairs={{240,1},{241,0},{242,3},{243,2},{244,5},{245,4},{246,7},{247,6},{2... | collective-permute-start | bytes 1572872 | tf_op jit(solution)/shard_map/ppermute | solution.py:269
  54.9 5.3 %collective-permute-start.5 = (bf16[32,8192]{1,0:T(8,128)(2,1)}, bf16[32,8192]{1,0:T(8,128)(2,1)}, u32[]{:S(2)}, u32[]{:S(2)}) collective-permute-start(bf16[32,8192]{1,0:T(8,128)(2,1)} %get-tuple-element.28), channel_id=1, source_target_pairs={{0,17},{1,16},{2,19},{3,18},{4,21},{5,20},{6,23},{7,22},{8,25},{9,... | collective-permute-start | bytes 1572872 | tf_op jit(solution)/shard_map/ppermute | solution.py:269
  60.2 1.3 %collective-permute-start.6 = (bf16[32,8192]{1,0:T(8,128)(2,1)}, bf16[32,8192]{1,0:T(8,128)(2,1)}, u32[]{:S(2)}, u32[]{:S(2)}) collective-permute-start(bf16[32,8192]{1,0:T(8,128)(2,1)} %get-tuple-element.29), channel_id=1, source_target_pairs={{16,1},{17,0},{18,3},{19,2},{20,5},{21,4},{22,7},{23,6},{24,9},{25... | collective-permute-start | bytes 1572872 | tf_op jit(solution)/shard_map/ppermute | solution.py:269
  61.4 17.2 %all-to-all-done.1 = bf16[16,2,64,512]{3,2,1,0:T(8,128)(2,1)S(1)} async-done(((bf16[16,2,64,512]{3,2,1,0:T(8,128)(2,1)}), bf16[16,2,64,512]{3,2,1,0:T(8,128)(2,1)S(1)}, u32[]{:S(2)}, u32[]{:S(2)}) %all-to-all-start.1) | async-done | bytes 2097184 | tf_op jit(solution)/shard_map/all_to_all | solution.py:288
  78.7 0.3 convert_reduce_fusion.sums_ref
  79.0 0.0 collective-permute-done.1.up_ref.up_own
  79.0 0.0 collective-permute-done.2.down_ref.down_own
  79.0 9.8 %collective-permute-start.8 = (bf16[2,2,64,512]{3,2,1,0:T(8,128)(2,1)S(1)}, bf16[2,2,64,512]{3,2,1,0:T(8,128)(2,1)S(1)}, u32[]{:S(2)}, u32[]{:S(2)}) collective-permute-start(bf16[2,2,64,512]{3,2,1,0:T(8,128)(2,1)S(1)} %convert_element_type.11), channel_id=1, source_target_pairs={{0,496},{16,480},{32,464},{48,448},{64,432},{80,416},{96,400},{112... | collective-permute-start | bytes 786440 | tf_op jit(solution)/shard_map/ppermute | solution.py:302
  88.9 0.0 collective-permute-done.4
  88.9 0.0 collective-permute-done.5.up_got
  88.9 0.0 collective-permute-done.6.down_got
  88.9 2.5 %collective-permute-start.7 = (bf16[32,8192]{1,0:T(8,128)(2,1)}, bf16[32,8192]{1,0:T(8,128)(2,1)S(1)}, u32[]{:S(2)}, u32[]{:S(2)}) collective-permute-start(bf16[32,8192]{1,0:T(8,128)(2,1)} %collective-permute-done.4), channel_id=1, source_target_pairs={{0,256},{1,257},{2,258},{3,259},{4,260},{5,261},{6,262},{7,263},{8... | collective-permute-start | bytes 1572872 | tf_op jit(solution)/shard_map/ppermute | solution.py:269
  91.4 0.7 collective-permute-start.3
  92.1 2.4 %shard_map.61 = (bf16[2,32,8192]{2,1,0:T(8,128)(2,1)}, bf16[2,32,8192]{2,1,0:T(8,128)(2,1)}) custom-call(s32[1]{0:T(128)} %bitcast.core_ref, bf16[32,8192]{1,0:T(8,128)(2,1)S(1)} %collective-permute-done.1.up_ref.up_own, bf16[32,8192]{1,0:T(8,128)(2,1)S(1)} %collective-permute-done.2.down_ref.down_own, bf16[32,8192]{1,0:T(8,128)(2,1)} %collective-permute-done.5.up_got, ...), custom_call_target="tpu_custom_call" | custom-call | bytes 4194304 | tf_op jit(solution)/shard_map/pallas_call | solution.py:210
  94.6 17.5 %collective-permute-done.8.partner_ref = bf16[2,2,64,512]{3,2,1,0:T(8,128)(2,1)S(1)} collective-permute-done((bf16[2,2,64,512]{3,2,1,0:T(8,128)(2,1)S(1)}, bf16[2,2,64,512]{3,2,1,0:T(8,128)(2,1)S(1)}, u32[]{:S(2)}, u32[]{:S(2)}) %collective-permute-start.8) | collective-permute-done | bytes 262176 | tf_op jit(solution)/shard_map/ppermute | solution.py:302
  112.0 0.8 shard_map.63
  112.9 0.0 collective-permute-done.7.got_ref
  112.9 0.0 collective-permute-done.3.own_ref
  (3 shorter events, 0.1 us)
Async XLA Ops:
  0.6 1.0 copy-start
  3.0 10.5 %copy-start.1 = (bf16[2,1,32,8192]{3,2,1,0:T(8,128)(2,1)S(1)}, bf16[2,1,32,8192]{3,2,1,0:T(8,128)(2,1)}, u32[]{:S(2)}) copy-start(bf16[2,1,32,8192]{3,2,1,0:T(8,128)(2,1)} %param.3) | copy-start | bytes 3145732
  3.0 38.1 %all-to-all-start = ((bf16[16,2,64,512]{3,2,1,0:T(8,128)(2,1)}), bf16[16,2,64,512]{3,2,1,0:T(8,128)(2,1)S(1)}, u32[]{:S(2)}, u32[]{:S(2)}) async-start(bf16[16,2,64,512]{3,2,1,0:T(8,128)(2,1)} %shard_map.58), calls=%async_computation | async-start | bytes 4194304 | tf_op jit(solution)/shard_map/all_to_all | solution.py:282
  15.0 4.7 %collective-permute-start = (bf16[2,32,8192]{2,1,0:T(8,128)(2,1)S(1)}, bf16[2,32,8192]{2,1,0:T(8,128)(2,1)}, u32[]{:S(2)}, u32[]{:S(2)}) collective-permute-start(bf16[2,32,8192]{2,1,0:T(8,128)(2,1)S(1)} %pad_maximum_fusion), channel_id=1, source_target_pairs={{0,1},{1,0},{2,3},{3,2},{4,5},{5,4},{6,7},{7,6},{8,9},{9,8},{10,11... | collective-permute-start | bytes 3145736 | tf_op jit(solution)/shard_map/ppermute | solution.py:284
  45.8 32.9 %all-to-all-start.1 = ((bf16[16,2,64,512]{3,2,1,0:T(8,128)(2,1)}), bf16[16,2,64,512]{3,2,1,0:T(8,128)(2,1)S(1)}, u32[]{:S(2)}, u32[]{:S(2)}) async-start(bf16[16,2,64,512]{3,2,1,0:T(8,128)(2,1)} %get-tuple-element.22), calls=%async_computation.1 | async-start | bytes 4194304 | tf_op jit(solution)/shard_map/all_to_all | solution.py:288
  51.0 28.0 %collective-permute-start.1 = (bf16[32,8192]{1,0:T(8,128)(2,1)}, bf16[32,8192]{1,0:T(8,128)(2,1)S(1)}, u32[]{:S(2)}, u32[]{:S(2)}) collective-permute-start(bf16[32,8192]{1,0:T(8,128)(2,1)} %get-tuple-element.23), channel_id=1, source_target_pairs={{0,16},{1,17},{2,18},{3,19},{4,20},{5,21},{6,22},{7,23},{8,24},{9,... | collective-permute-start | bytes 1572872 | tf_op jit(solution)/shard_map/ppermute | solution.py:269
  52.3 26.7 %collective-permute-start.2 = (bf16[32,8192]{1,0:T(8,128)(2,1)}, bf16[32,8192]{1,0:T(8,128)(2,1)S(1)}, u32[]{:S(2)}, u32[]{:S(2)}) collective-permute-start(bf16[32,8192]{1,0:T(8,128)(2,1)} %get-tuple-element.24), channel_id=1, source_target_pairs={{16,0},{17,1},{18,2},{19,3},{20,4},{21,5},{22,6},{23,7},{24,8},{25... | collective-permute-start | bytes 1572872 | tf_op jit(solution)/shard_map/ppermute | solution.py:269
  53.6 35.3 %collective-permute-start.4 = (bf16[32,8192]{1,0:T(8,128)(2,1)}, bf16[32,8192]{1,0:T(8,128)(2,1)}, u32[]{:S(2)}, u32[]{:S(2)}) collective-permute-start(bf16[32,8192]{1,0:T(8,128)(2,1)} %get-tuple-element.27), channel_id=1, source_target_pairs={{240,1},{241,0},{242,3},{243,2},{244,5},{245,4},{246,7},{247,6},{2... | collective-permute-start | bytes 1572872 | tf_op jit(solution)/shard_map/ppermute | solution.py:269
  54.9 34.0 %collective-permute-start.5 = (bf16[32,8192]{1,0:T(8,128)(2,1)}, bf16[32,8192]{1,0:T(8,128)(2,1)}, u32[]{:S(2)}, u32[]{:S(2)}) collective-permute-start(bf16[32,8192]{1,0:T(8,128)(2,1)} %get-tuple-element.28), channel_id=1, source_target_pairs={{0,17},{1,16},{2,19},{3,18},{4,21},{5,20},{6,23},{7,22},{8,25},{9,... | collective-permute-start | bytes 1572872 | tf_op jit(solution)/shard_map/ppermute | solution.py:269
  60.2 28.7 %collective-permute-start.6 = (bf16[32,8192]{1,0:T(8,128)(2,1)}, bf16[32,8192]{1,0:T(8,128)(2,1)}, u32[]{:S(2)}, u32[]{:S(2)}) collective-permute-start(bf16[32,8192]{1,0:T(8,128)(2,1)} %get-tuple-element.29), channel_id=1, source_target_pairs={{16,1},{17,0},{18,3},{19,2},{20,5},{21,4},{22,7},{23,6},{24,9},{25... | collective-permute-start | bytes 1572872 | tf_op jit(solution)/shard_map/ppermute | solution.py:269
  79.0 33.0 %collective-permute-start.8 = (bf16[2,2,64,512]{3,2,1,0:T(8,128)(2,1)S(1)}, bf16[2,2,64,512]{3,2,1,0:T(8,128)(2,1)S(1)}, u32[]{:S(2)}, u32[]{:S(2)}) collective-permute-start(bf16[2,2,64,512]{3,2,1,0:T(8,128)(2,1)S(1)} %convert_element_type.11), channel_id=1, source_target_pairs={{0,496},{16,480},{32,464},{48,448},{64,432},{80,416},{96,400},{112... | collective-permute-start | bytes 786440 | tf_op jit(solution)/shard_map/ppermute | solution.py:302
  88.9 24.0 %collective-permute-start.7 = (bf16[32,8192]{1,0:T(8,128)(2,1)}, bf16[32,8192]{1,0:T(8,128)(2,1)S(1)}, u32[]{:S(2)}, u32[]{:S(2)}) collective-permute-start(bf16[32,8192]{1,0:T(8,128)(2,1)} %collective-permute-done.4), channel_id=1, source_target_pairs={{0,256},{1,257},{2,258},{3,259},{4,260},{5,261},{6,262},{7,263},{8... | collective-permute-start | bytes 1572872 | tf_op jit(solution)/shard_map/ppermute | solution.py:269
  91.4 21.5 %collective-permute-start.3 = (bf16[32,8192]{1,0:T(8,128)(2,1)}, bf16[32,8192]{1,0:T(8,128)(2,1)S(1)}, u32[]{:S(2)}, u32[]{:S(2)}) collective-permute-start(bf16[32,8192]{1,0:T(8,128)(2,1)} %shard_map.60), channel_id=1, source_target_pairs={{256,264},{257,265},{258,266},{259,267},{260,268},{261,269},{262,2... | collective-permute-start | bytes 1572872 | tf_op jit(solution)/shard_map/ppermute | solution.py:269

commit v10 on v9

--- a/solution.py
+++ b/solution.py
@@ -62,7 +62,7 @@
 
 def adapter_kernel(
     count, core_ref, at_ref, x_ref, g_ref, taken_ref, w_ref, part_ref, up_ref, down_ref, up_send, down_send, edge_ref,
-    xs, gs, ps, ms, loads, part_stores, stores, edge_sem
+    xs, gs, ps, ms, loads, part_stores, stores, edge_sems
 ):
     is_down = core_ref[0] == 0
     slices, _, rank, width = w_ref.shape
@@ -119,14 +119,18 @@
             ):
                 copy.start()
                 stored.append(copy)
-    for way, position in ((0, count // 2 - 1), (1, count // 2)):
+            for way, position in ((0, count // 2 - 1), (1, count // 2)):
+                @pl.when(at_ref[0] == position)
+                def _():
+                    pltpu.make_async_copy(ms.at[way, others, cols], edge_ref.at[:, cols], edge_sems.at[j]).start()
+    for copy in stored:
+        copy.wait()
+    for position in (count // 2 - 1, count // 2):
         @pl.when(at_ref[0] == position)
         def _():
-            copy = pltpu.make_async_copy(ms.at[way, others], edge_ref, edge_sem)
-            copy.start()
-            copy.wait()
-    for copy in stored:
-        copy.wait()
+            for j in range(chunks):
+                cols = pl.ds(j * (model // chunks), model // chunks)
+                pltpu.make_async_copy(ms.at[0, others, cols], edge_ref.at[:, cols], edge_sems.at[j]).wait()
 
 
 def adapter(count, core, section, x, g, taken, w):
@@ -146,7 +150,7 @@
             pltpu.SemaphoreType.DMA((4, 4)),
             pltpu.SemaphoreType.DMA((4,)),
             pltpu.SemaphoreType.DMA((4, 4)),
-            pltpu.SemaphoreType.DMA,
+            pltpu.SemaphoreType.DMA((4,)),
         ],
         compiler_params=PARAMS,
         cost_estimate=pl.CostEstimate(flops=12 * tokens * w.size, bytes_accessed=12 << 20, transcendentals=0),

time: 114 us -> 114 us (level)
  no operation moved by 1% of the time
where the time goes in v10:
time: 114 us; the launch traced here: 113 us
  waiting for transfers between devices  58.8 us (52%)
  starting transfers between devices  41.2 us (36%)
  Pallas kernels  9.44 us (8%)
  other arithmetic  1.73 us (2%)
    all_to_all x1, waiting for transfers between devices, shards(): lax.all_to_all(spread(adapters[:, 0], n_dp), 'dp', 0, 0, tiled=True)  21.5 us
    ppermute x1, waiting for transfers between devices, shards(): lax.ppermute(narrow, 'section', [(i, count - 1 - i) for i in range(count)])  17.5 us
    all_to_all x1, waiting for transfers between devices, shards(): terms = lax.all_to_all(parts, 'dp', 0, 0, tiled=True)  17.2 us
    ppermute x7, starting transfers between devices, moved(): return lax.ppermute(value, ('section', 'dp'), pairs)  13.6 us
    all_to_all x1, starting transfers between devices, shards(): lax.all_to_all(spread(adapters[:, 0], n_dp), 'dp', 0, 0, tiled=True)  10.5 us
    ppermute x1, starting transfers between devices, shards(): lax.ppermute(narrow, 'section', [(i, count - 1 - i) for i in range(count)])  9.82 us
    all_to_all x1, starting transfers between devices, shards(): terms = lax.all_to_all(parts, 'dp', 0, 0, tiled=True)  5.17 us
    pallas_call x1, Pallas kernels, adapter(): pl.pallas_call(functools.partial(adapter_kernel, count), out_shape=(pltpu...  4.74 us
  transfers between devices with their start and end apart: 11, of which 4 were waited for; matrix products, arithmetic and copies ran while one was open for 2% of the time, Pallas kernels for 3%

profile of v10, /device:TPU:1, one launch (start us, length us, event | category | flops | bytes accessed | tf_op | source)
XLA Modules:
  0.0 112.9 jit_solution(16165611069026796188)
XLA Ops:
  0.6 0.0 copy-start
  0.6 0.9 copy-done
  1.6 1.4 %shard_map.58 = bf16[16,2,64,512]{3,2,1,0:T(8,128)(2,1)} custom-call(bf16[2,2,64,512]{3,2,1,0:T(8,128)(2,1)S(1)} %bitcast.20), custom_call_target="tpu_custom_call" | custom-call | bytes 2097152 | tf_op jit(solution)/shard_map/pallas_call | solution.py:34
  3.0 0.0 copy-start.1
  3.0 10.5 %all-to-all-start = ((bf16[16,2,64,512]{3,2,1,0:T(8,128)(2,1)}), bf16[16,2,64,512]{3,2,1,0:T(8,128)(2,1)S(1)}, u32[]{:S(2)}, u32[]{:S(2)}) async-start(bf16[16,2,64,512]{3,2,1,0:T(8,128)(2,1)} %shard_map.58), calls=%async_computation | async-start | bytes 4194304 | tf_op jit(solution)/shard_map/all_to_all | solution.py:286
  13.5 0.0 copy-done.1
  13.5 1.3 %select_bitcast_fusion = (bf16[1,32,8192]{2,1,0:T(8,128)(2,1)S(1)}, bf16[1,32,8192]{2,1,0:T(8,128)(2,1)S(1)}) fusion(bf16[2,1,32,8192]{3,2,1,0:T(8,128)(2,1)} %param.4, pred[]{:T(512)S(6)} %eq.5, bf16[2,1,32,8192]{3,2,1,0:T(8,128)(2,1)S(1)} %copy-done.1), kind=kLoop, calls=%fused_computation.2 | loop fusion | flops 524288 | bytes 3145729 | tf_op jit(solution)/shard_map/jit(_where)/select_n | solution.py:287
  14.8 0.1 pad_maximum_fusion
  15.0 2.1 %collective-permute-start = (bf16[2,32,8192]{2,1,0:T(8,128)(2,1)S(1)}, bf16[2,32,8192]{2,1,0:T(8,128)(2,1)}, u32[]{:S(2)}, u32[]{:S(2)}) collective-permute-start(bf16[2,32,8192]{2,1,0:T(8,128)(2,1)S(1)} %pad_maximum_fusion), channel_id=1, source_target_pairs={{0,1},{1,0},{2,3},{3,2},{4,5},{5,4},{6,7},{7,6},{8,9},{9,8},{10,11... | collective-permute-start | bytes 3145736 | tf_op jit(solution)/shard_map/ppermute | solution.py:288
  17.1 2.5 %collective-permute-done.taken_ref = bf16[2,32,8192]{2,1,0:T(8,128)(2,1)} collective-permute-done((bf16[2,32,8192]{2,1,0:T(8,128)(2,1)S(1)}, bf16[2,32,8192]{2,1,0:T(8,128)(2,1)}, u32[]{:S(2)}, u32[]{:S(2)}) %collective-permute-start) | collective-permute-done | bytes 1048608 | tf_op jit(solution)/shard_map/ppermute | solution.py:288
  19.6 21.5 %all-to-all-done.w_ref = bf16[16,2,64,512]{3,2,1,0:T(8,128)(2,1)S(1)} async-done(((bf16[16,2,64,512]{3,2,1,0:T(8,128)(2,1)}), bf16[16,2,64,512]{3,2,1,0:T(8,128)(2,1)S(1)}, u32[]{:S(2)}, u32[]{:S(2)}) %all-to-all-start) | async-done | bytes 2097184 | tf_op jit(solution)/shard_map/all_to_all | solution.py:286
  41.1 4.7 %shard_map.59 = (bf16[16,2,64,512]{3,2,1,0:T(8,128)(2,1)}, bf16[32,8192]{1,0:T(8,128)(2,1)}, bf16[32,8192]{1,0:T(8,128)(2,1)}, bf16[32,8192]{1,0:T(8,128)(2,1)},...) custom-call(s32[1]{0:T(128)} %bitcast.core_ref, s32[1]{0:T(128)} %bitcast.1.at_ref, bf16[2,32,8192]{2,1,0:T(8,128)(2,1)} %bitcast.22, ...), custom_call_target="tpu_custom_call" | custom-call | flops 402653184 | bytes 12582912 | tf_op jit(solution)/shard_map/pallas_call | solution.py:140
  45.8 5.2 %all-to-all-start.1 = ((bf16[16,2,64,512]{3,2,1,0:T(8,128)(2,1)}), bf16[16,2,64,512]{3,2,1,0:T(8,128)(2,1)S(1)}, u32[]{:S(2)}, u32[]{:S(2)}) async-start(bf16[16,2,64,512]{3,2,1,0:T(8,128)(2,1)} %get-tuple-element.22), calls=%async_computation.1 | async-start | bytes 4194304 | tf_op jit(solution)/shard_map/all_to_all | solution.py:292
  51.0 1.3 %collective-permute-start.1 = (bf16[32,8192]{1,0:T(8,128)(2,1)}, bf16[32,8192]{1,0:T(8,128)(2,1)S(1)}, u32[]{:S(2)}, u32[]{:S(2)}) collective-permute-start(bf16[32,8192]{1,0:T(8,128)(2,1)} %get-tuple-element.23), channel_id=1, source_target_pairs={{0,16},{1,17},{2,18},{3,19},{4,20},{5,21},{6,22},{7,23},{8,24},{9,... | collective-permute-start | bytes 1572872 | tf_op jit(solution)/shard_map/ppermute | solution.py:273
  52.3 1.3 %collective-permute-start.2 = (bf16[32,8192]{1,0:T(8,128)(2,1)}, bf16[32,8192]{1,0:T(8,128)(2,1)S(1)}, u32[]{:S(2)}, u32[]{:S(2)}) collective-permute-start(bf16[32,8192]{1,0:T(8,128)(2,1)} %get-tuple-element.24), channel_id=1, source_target_pairs={{16,0},{17,1},{18,2},{19,3},{20,4},{21,5},{22,6},{23,7},{24,8},{25... | collective-permute-start | bytes 1572872 | tf_op jit(solution)/shard_map/ppermute | solution.py:273
  53.6 1.3 %collective-permute-start.4 = (bf16[32,8192]{1,0:T(8,128)(2,1)}, bf16[32,8192]{1,0:T(8,128)(2,1)}, u32[]{:S(2)}, u32[]{:S(2)}) collective-permute-start(bf16[32,8192]{1,0:T(8,128)(2,1)} %get-tuple-element.27), channel_id=1, source_target_pairs={{240,1},{241,0},{242,3},{243,2},{244,5},{245,4},{246,7},{247,6},{2... | collective-permute-start | bytes 1572872 | tf_op jit(solution)/shard_map/ppermute | solution.py:273
  54.9 5.3 %collective-permute-start.5 = (bf16[32,8192]{1,0:T(8,128)(2,1)}, bf16[32,8192]{1,0:T(8,128)(2,1)}, u32[]{:S(2)}, u32[]{:S(2)}) collective-permute-start(bf16[32,8192]{1,0:T(8,128)(2,1)} %get-tuple-element.28), channel_id=1, source_target_pairs={{0,17},{1,16},{2,19},{3,18},{4,21},{5,20},{6,23},{7,22},{8,25},{9,... | collective-permute-start | bytes 1572872 | tf_op jit(solution)/shard_map/ppermute | solution.py:273
  60.2 1.3 %collective-permute-start.6 = (bf16[32,8192]{1,0:T(8,128)(2,1)}, bf16[32,8192]{1,0:T(8,128)(2,1)}, u32[]{:S(2)}, u32[]{:S(2)}) collective-permute-start(bf16[32,8192]{1,0:T(8,128)(2,1)} %get-tuple-element.29), channel_id=1, source_target_pairs={{16,1},{17,0},{18,3},{19,2},{20,5},{21,4},{22,7},{23,6},{24,9},{25... | collective-permute-start | bytes 1572872 | tf_op jit(solution)/shard_map/ppermute | solution.py:273
  61.5 17.2 %all-to-all-done.1 = bf16[16,2,64,512]{3,2,1,0:T(8,128)(2,1)S(1)} async-done(((bf16[16,2,64,512]{3,2,1,0:T(8,128)(2,1)}), bf16[16,2,64,512]{3,2,1,0:T(8,128)(2,1)S(1)}, u32[]{:S(2)}, u32[]{:S(2)}) %all-to-all-start.1) | async-done | bytes 2097184 | tf_op jit(solution)/shard_map/all_to_all | solution.py:292
  78.7 0.3 convert_reduce_fusion.sums_ref
  79.0 0.0 collective-permute-done.1.up_ref.up_own
  79.0 0.0 collective-permute-done.2.down_ref.down_own
  79.1 9.8 %collective-permute-start.8 = (bf16[2,2,64,512]{3,2,1,0:T(8,128)(2,1)S(1)}, bf16[2,2,64,512]{3,2,1,0:T(8,128)(2,1)S(1)}, u32[]{:S(2)}, u32[]{:S(2)}) collective-permute-start(bf16[2,2,64,512]{3,2,1,0:T(8,128)(2,1)S(1)} %convert_element_type.11), channel_id=1, source_target_pairs={{0,496},{16,480},{32,464},{48,448},{64,432},{80,416},{96,400},{112... | collective-permute-start | bytes 786440 | tf_op jit(solution)/shard_map/ppermute | solution.py:306
  88.9 0.0 collective-permute-done.4
  88.9 0.0 collective-permute-done.5.up_got
  88.9 0.0 collective-permute-done.6.down_got
  88.9 2.5 %collective-permute-start.7 = (bf16[32,8192]{1,0:T(8,128)(2,1)}, bf16[32,8192]{1,0:T(8,128)(2,1)S(1)}, u32[]{:S(2)}, u32[]{:S(2)}) collective-permute-start(bf16[32,8192]{1,0:T(8,128)(2,1)} %collective-permute-done.4), channel_id=1, source_target_pairs={{0,256},{1,257},{2,258},{3,259},{4,260},{5,261},{6,262},{7,263},{8... | collective-permute-start | bytes 1572872 | tf_op jit(solution)/shard_map/ppermute | solution.py:273
  91.4 0.7 collective-permute-start.3
  92.1 2.4 %shard_map.61 = (bf16[2,32,8192]{2,1,0:T(8,128)(2,1)}, bf16[2,32,8192]{2,1,0:T(8,128)(2,1)}) custom-call(s32[1]{0:T(128)} %bitcast.core_ref, bf16[32,8192]{1,0:T(8,128)(2,1)S(1)} %collective-permute-done.1.up_ref.up_own, bf16[32,8192]{1,0:T(8,128)(2,1)S(1)} %collective-permute-done.2.down_ref.down_own, bf16[32,8192]{1,0:T(8,128)(2,1)} %collective-permute-done.5.up_got, ...), custom_call_target="tpu_custom_call" | custom-call | bytes 4194304 | tf_op jit(solution)/shard_map/pallas_call | solution.py:214
  94.5 17.5 %collective-permute-done.8.partner_ref = bf16[2,2,64,512]{3,2,1,0:T(8,128)(2,1)S(1)} collective-permute-done((bf16[2,2,64,512]{3,2,1,0:T(8,128)(2,1)S(1)}, bf16[2,2,64,512]{3,2,1,0:T(8,128)(2,1)S(1)}, u32[]{:S(2)}, u32[]{:S(2)}) %collective-permute-start.8) | collective-permute-done | bytes 262176 | tf_op jit(solution)/shard_map/ppermute | solution.py:306
  112.1 0.8 shard_map.63
  112.9 0.0 collective-permute-done.7.got_ref
  112.9 0.0 collective-permute-done.3.own_ref
  (3 shorter events, 0.1 us)
Async XLA Ops:
  0.6 1.0 copy-start
  3.0 10.5 %copy-start.1 = (bf16[2,1,32,8192]{3,2,1,0:T(8,128)(2,1)S(1)}, bf16[2,1,32,8192]{3,2,1,0:T(8,128)(2,1)}, u32[]{:S(2)}) copy-start(bf16[2,1,32,8192]{3,2,1,0:T(8,128)(2,1)} %param.3) | copy-start | bytes 3145732
  3.0 38.1 %all-to-all-start = ((bf16[16,2,64,512]{3,2,1,0:T(8,128)(2,1)}), bf16[16,2,64,512]{3,2,1,0:T(8,128)(2,1)S(1)}, u32[]{:S(2)}, u32[]{:S(2)}) async-start(bf16[16,2,64,512]{3,2,1,0:T(8,128)(2,1)} %shard_map.58), calls=%async_computation | async-start | bytes 4194304 | tf_op jit(solution)/shard_map/all_to_all | solution.py:286
  15.0 4.7 %collective-permute-start = (bf16[2,32,8192]{2,1,0:T(8,128)(2,1)S(1)}, bf16[2,32,8192]{2,1,0:T(8,128)(2,1)}, u32[]{:S(2)}, u32[]{:S(2)}) collective-permute-start(bf16[2,32,8192]{2,1,0:T(8,128)(2,1)S(1)} %pad_maximum_fusion), channel_id=1, source_target_pairs={{0,1},{1,0},{2,3},{3,2},{4,5},{5,4},{6,7},{7,6},{8,9},{9,8},{10,11... | collective-permute-start | bytes 3145736 | tf_op jit(solution)/shard_map/ppermute | solution.py:288
  45.8 32.9 %all-to-all-start.1 = ((bf16[16,2,64,512]{3,2,1,0:T(8,128)(2,1)}), bf16[16,2,64,512]{3,2,1,0:T(8,128)(2,1)S(1)}, u32[]{:S(2)}, u32[]{:S(2)}) async-start(bf16[16,2,64,512]{3,2,1,0:T(8,128)(2,1)} %get-tuple-element.22), calls=%async_computation.1 | async-start | bytes 4194304 | tf_op jit(solution)/shard_map/all_to_all | solution.py:292
  51.0 28.0 %collective-permute-start.1 = (bf16[32,8192]{1,0:T(8,128)(2,1)}, bf16[32,8192]{1,0:T(8,128)(2,1)S(1)}, u32[]{:S(2)}, u32[]{:S(2)}) collective-permute-start(bf16[32,8192]{1,0:T(8,128)(2,1)} %get-tuple-element.23), channel_id=1, source_target_pairs={{0,16},{1,17},{2,18},{3,19},{4,20},{5,21},{6,22},{7,23},{8,24},{9,... | collective-permute-start | bytes 1572872 | tf_op jit(solution)/shard_map/ppermute | solution.py:273
  52.3 26.7 %collective-permute-start.2 = (bf16[32,8192]{1,0:T(8,128)(2,1)}, bf16[32,8192]{1,0:T(8,128)(2,1)S(1)}, u32[]{:S(2)}, u32[]{:S(2)}) collective-permute-start(bf16[32,8192]{1,0:T(8,128)(2,1)} %get-tuple-element.24), channel_id=1, source_target_pairs={{16,0},{17,1},{18,2},{19,3},{20,4},{21,5},{22,6},{23,7},{24,8},{25... | collective-permute-start | bytes 1572872 | tf_op jit(solution)/shard_map/ppermute | solution.py:273
  53.6 35.3 %collective-permute-start.4 = (bf16[32,8192]{1,0:T(8,128)(2,1)}, bf16[32,8192]{1,0:T(8,128)(2,1)}, u32[]{:S(2)}, u32[]{:S(2)}) collective-permute-start(bf16[32,8192]{1,0:T(8,128)(2,1)} %get-tuple-element.27), channel_id=1, source_target_pairs={{240,1},{241,0},{242,3},{243,2},{244,5},{245,4},{246,7},{247,6},{2... | collective-permute-start | bytes 1572872 | tf_op jit(solution)/shard_map/ppermute | solution.py:273
  54.9 34.0 %collective-permute-start.5 = (bf16[32,8192]{1,0:T(8,128)(2,1)}, bf16[32,8192]{1,0:T(8,128)(2,1)}, u32[]{:S(2)}, u32[]{:S(2)}) collective-permute-start(bf16[32,8192]{1,0:T(8,128)(2,1)} %get-tuple-element.28), channel_id=1, source_target_pairs={{0,17},{1,16},{2,19},{3,18},{4,21},{5,20},{6,23},{7,22},{8,25},{9,... | collective-permute-start | bytes 1572872 | tf_op jit(solution)/shard_map/ppermute | solution.py:273
  60.2 28.7 %collective-permute-start.6 = (bf16[32,8192]{1,0:T(8,128)(2,1)}, bf16[32,8192]{1,0:T(8,128)(2,1)}, u32[]{:S(2)}, u32[]{:S(2)}) collective-permute-start(bf16[32,8192]{1,0:T(8,128)(2,1)} %get-tuple-element.29), channel_id=1, source_target_pairs={{16,1},{17,0},{18,3},{19,2},{20,5},{21,4},{22,7},{23,6},{24,9},{25... | collective-permute-start | bytes 1572872 | tf_op jit(solution)/shard_map/ppermute | solution.py:273
  79.1 33.0 %collective-permute-start.8 = (bf16[2,2,64,512]{3,2,1,0:T(8,128)(2,1)S(1)}, bf16[2,2,64,512]{3,2,1,0:T(8,128)(2,1)S(1)}, u32[]{:S(2)}, u32[]{:S(2)}) collective-permute-start(bf16[2,2,64,512]{3,2,1,0:T(8,128)(2,1)S(1)} %convert_element_type.11), channel_id=1, source_target_pairs={{0,496},{16,480},{32,464},{48,448},{64,432},{80,416},{96,400},{112... | collective-permute-start | bytes 786440 | tf_op jit(solution)/shard_map/ppermute | solution.py:306
  88.9 24.0 %collective-permute-start.7 = (bf16[32,8192]{1,0:T(8,128)(2,1)}, bf16[32,8192]{1,0:T(8,128)(2,1)S(1)}, u32[]{:S(2)}, u32[]{:S(2)}) collective-permute-start(bf16[32,8192]{1,0:T(8,128)(2,1)} %collective-permute-done.4), channel_id=1, source_target_pairs={{0,256},{1,257},{2,258},{3,259},{4,260},{5,261},{6,262},{7,263},{8... | collective-permute-start | bytes 1572872 | tf_op jit(solution)/shard_map/ppermute | solution.py:273
  91.4 21.5 %collective-permute-start.3 = (bf16[32,8192]{1,0:T(8,128)(2,1)}, bf16[32,8192]{1,0:T(8,128)(2,1)S(1)}, u32[]{:S(2)}, u32[]{:S(2)}) collective-permute-start(bf16[32,8192]{1,0:T(8,128)(2,1)} %shard_map.60), channel_id=1, source_target_pairs={{256,264},{257,265},{258,266},{259,267},{260,268},{261,269},{262,2... | collective-permute-start | bytes 1572872 | tf_op jit(solution)/shard_map/ppermute | solution.py:273
